TPU v7x, 32 devices: a whole 2x2x4 slice. The times are simulated.
32 devices in a mesh: cls: 4 (over z), dom: 8 (over y, x, core).
Axes of the slice: x: 2, y: 2, z: 4, core: 2. Of those that a mesh axis runs over, the one named last changes fastest.
Arguments:
- particles: bfloat16 [4096, 8192], P(('cls', 'dom')), may hold values from -6 to 6
- assign: int32 [4096, 1], P(('cls', 'dom')), may hold values from 0 to 7; in each aligned block of 128 rows (0 to 127, 128 to 255, ...) at most 16 rows name the same one
- inv_sigma: bfloat16 [4096], P(('cls', 'dom')), may hold values from 0.5 to 300, as said below
- projections: bfloat16 [8, 16, 8192], P('cls', 'dom'), may hold values from -0.0625 to 0.0625
Outputs:
- class_sums: float32 [8, 16, 8192], P('cls', 'dom')
- evidence: float32 [4096], P(('cls', 'dom'))
Inputs may be any that keep to these rules, and one draw needn't show every extreme that they name: `assign`: among the 128 particles of one device (aligned blocks of rows) no class is named more than 16 times, a bound that some block reaches. `inv_sigma`: each particle's noise precision, positive.
All inputs are finite; a program needn't handle non-finite values.
Results may differ from a plain program's by a relative error of at most 0.0023.
Values may be sent and summed in bfloat16 or wider, within the bound.
No kernel may reach another device: no remote copies, remote signals or barrier semaphores. Data moves between devices by JAX's collectives and lax.ppermute only.
A program may use at most 64 MiB of HBM per device.

v0:
```python
import jax
import jax.numpy as jnp
from jax import lax
from jax.sharding import PartitionSpec as P


def on_device(particles, assign, inv_sigma, projections):
    local_rows = particles.shape[0]
    width = particles.shape[1]
    per_owner = projections.shape[0]
    own_rows = projections.shape[1]
    owners = lax.axis_size("cls")
    classes = per_owner * owners
    capacity = local_rows // 8
    class_id = assign[:, 0]
    one_hot = (class_id[:, None] == jnp.arange(classes, dtype=jnp.int32)[None, :]).astype(jnp.int32)
    before = jnp.cumsum(one_hot, axis=0) - one_hot
    ranking = jnp.sum(before * one_hot, axis=1)
    slot_index = (
        class_id % per_owner * (owners * capacity) + class_id // per_owner * capacity + ranking
    )
    slots = per_owner * owners * capacity
    source = (
        jnp.full((slots,), local_rows, jnp.int32)
        .at[slot_index]
        .set(jnp.arange(local_rows, dtype=jnp.int32))
    )
    padded = jnp.concatenate([particles, jnp.zeros((1, width), particles.dtype)], axis=0)
    padded_prec = jnp.concatenate([inv_sigma, jnp.zeros((1,), inv_sigma.dtype)], axis=0)
    packed = padded[source].reshape(per_owner, owners, capacity, width)
    packed_prec = padded_prec[source].reshape(per_owner, owners, capacity)
    arrived, arrived_prec = (
        lax.all_to_all(packed, "cls", split_axis=1, concat_axis=1, tiled=True),
        lax.all_to_all(packed_prec, "cls", split_axis=1, concat_axis=1, tiled=True),
    )
    arrived = arrived.reshape(per_owner, owners * capacity, width)
    precision = arrived_prec.reshape(per_owner, owners * capacity).astype(jnp.float32)
    piece = lax.all_gather(projections, "dom", axis=1, tiled=True)
    products = jnp.einsum("kmf,krf->kmr", arrived, piece, preferred_element_type=jnp.float32)
    halves = 0.5 * jnp.sum(jnp.square(piece.astype(jnp.float32)), axis=2)
    scores = precision[:, :, None] * (products - halves[:, None, :])
    is_live = precision > 0.0
    largest = jnp.max(scores, axis=2, keepdims=True)
    exponent = jnp.exp(scores - largest)
    totals = jnp.sum(exponent, axis=2, keepdims=True)
    weights = jnp.where(is_live[:, :, None], exponent / totals, 0.0).astype(jnp.bfloat16)
    log_total = jnp.where(is_live, largest[:, :, 0] + jnp.log(totals[:, :, 0]), 0.0)
    term = jnp.einsum("kmr,kmf->rkf", weights, arrived, preferred_element_type=jnp.float32)
    joined = lax.psum_scatter(
        term.reshape(own_rows * lax.axis_size("dom"), per_owner * width),
        "dom",
        scatter_dimension=0,
        tiled=True,
    )
    class_sums = joined.reshape(own_rows, per_owner, width).transpose(1, 0, 2)
    returned = lax.all_to_all(
        log_total.reshape(per_owner, owners, capacity),
        "cls",
        split_axis=1,
        concat_axis=1,
        tiled=True,
    )
    evidence = returned.reshape(slots)[slot_index]
    return (class_sums, evidence)


def solution(mesh):
    return jax.shard_map(
        on_device,
        mesh=mesh,
        in_specs=(
            P(("cls", "dom"), None),
            P(("cls", "dom"), None),
            P(("cls", "dom")),
            P("cls", "dom", None),
        ),
        out_specs=(P("cls", "dom", None), P(("cls", "dom"))),
        check_vma=False,
    )
```

profile of v0, /device:TPU:0, one launch (start us, length us, event | category | flops | bytes accessed | tf_op | source)
XLA Modules:
  0.0 147.3 jit_solution(16617093541280136181)
XLA Ops:
  7.2 0.7 fusion.2
  7.9 0.2 reduce_window_sum.11
  8.1 0.8 select_reduce_fusion
  8.9 0.7 fusion.11
  9.6 1.0 scatter_custom_fusion
  10.6 0.7 pad_maximum_fusion
  11.3 1.2 gather_fusion.1
  12.5 0.1 reshape.47
  12.6 0.6 copy.31
  13.2 6.3 %all-to-all-start.1 = ((bf16[2,4,16]{2,0,1:T(2,128)(2,1)}), bf16[2,4,16]{2,0,1:T(2,128)(2,1)S(1)}, u32[]{:S(2)}, u32[]{:S(2)}) async-start(bf16[2,4,16]{2,0,1:T(2,128)(2,1)} %copy.31), calls=%async_computation.1 | async-start | bytes 4096 | tf_op jit(solution)/shard_map/all_to_all | solution.py:34
  19.5 1.8 %concatenate.6 = bf16[129,8192]{1,0:T(8,128)(2,1)S(1)} pad(bf16[128,8192]{1,0:T(8,128)(2,1)} %param.4, bf16[]{:T(256)} %constant.38.clone.1), padding=0_1x0_0 | pad | bytes 4210690 | tf_op jit(solution)/shard_map/concatenate | solution.py:28
  21.3 3.2 %gather_fusion = bf16[128,8192]{1,0:T(8,128)(2,1)} fusion(bf16[129,8192]{1,0:T(8,128)(2,1)S(1)} %concatenate.6, s32[1024]{0:T(1024)S(1)} %pad_clamp_fusion.1), kind=kCustom, calls=%fused_computation | custom fusion | bytes 4194816 | tf_op jit(solution)/shard_map/gather | solution.py:30
  24.5 3.1 %copy.29 = bf16[2,4,16,8192]{3,2,0,1:T(8,128)(2,1)} copy(bf16[2,4,16,8192]{3,2,1,0:T(8,128)(2,1)} %bitcast.21) | data formatting | bytes 4194304 | tf_op jit(solution)/shard_map/reshape | solution.py:30
  27.6 5.2 %all-to-all-start = ((bf16[2,4,16,8192]{3,2,0,1:T(8,128)(2,1)}), bf16[2,4,16,8192]{3,2,0,1:T(8,128)(2,1)S(1)}, u32[]{:S(2)}, u32[]{:S(2)}) async-start(bf16[2,4,16,8192]{3,2,0,1:T(8,128)(2,1)} %copy.29), calls=%async_computation | async-start | bytes 4194304 | tf_op jit(solution)/shard_map/all_to_all | solution.py:33
  32.9 9.9 %all_gather.3 = bf16[2,16,8192]{2,0,1:T(2,128)(2,1)S(1)} all-gather(bf16[2,2,8192]{2,0,1:T(2,128)(2,1)S(1)} %copy.33), channel_id=1, replica_groups=mesh['cls'=4,'dom'=8] {'dom'}, dimensions={1}, use_global_device_ids=true | all-gather | bytes 589824 | tf_op jit(solution)/shard_map/all_gather | solution.py:38
  42.8 0.6 multiply_reduce_fusion
  43.4 0.1 copy.35
  43.5 0.1 reshape.51
  43.6 36.9 %all-to-all-done = bf16[2,4,16,8192]{3,2,0,1:T(8,128)(2,1)S(1)} async-done(((bf16[2,4,16,8192]{3,2,0,1:T(8,128)(2,1)}), bf16[2,4,16,8192]{3,2,0,1:T(8,128)(2,1)S(1)}, u32[]{:S(2)}, u32[]{:S(2)}) %all-to-all-start) | async-done | bytes 2097184 | tf_op jit(solution)/shard_map/all_to_all | solution.py:33
  80.5 0.1 copy.30
  80.6 0.7 fusion.15
  81.4 0.4 convolution_bitcast_fusion
  81.8 1.1 copy.40
  82.9 0.1 add.43
  83.0 0.6 copy.38
  83.6 3.2 %all-to-all-start.2 = ((f32[2,4,16]{2,0,1:T(2,128)}), f32[2,4,16]{2,0,1:T(2,128)S(1)}, u32[]{:S(2)}, u32[]{:S(2)}) async-start(f32[2,4,16]{2,0,1:T(2,128)} %copy.38), calls=%async_computation.2 | async-start | bytes 8192 | tf_op jit(solution)/shard_map/all_to_all | solution.py:56
  86.9 0.6 dynamic-slice
  88.1 4.3 %all-to-all-done.2 = f32[2,4,16]{2,0,1:T(2,128)S(1)} async-done(((f32[2,4,16]{2,0,1:T(2,128)}), f32[2,4,16]{2,0,1:T(2,128)S(1)}, u32[]{:S(2)}, u32[]{:S(2)}) %all-to-all-start.2) | async-done | bytes 544 | tf_op jit(solution)/shard_map/all_to_all | solution.py:56
  92.4 0.1 reshape.50
  92.5 1.7 %gather_fusion.2 = f32[128]{0:T(128)} fusion(f32[128]{0:T(128)S(1)} %reshape.50, s32[1024]{0:T(1024)S(1)} %pad_clamp_fusion), kind=kCustom, calls=%fused_computation.2 | custom fusion | bytes 1536 | tf_op jit(solution)/shard_map/gather | solution.py:63
  94.2 44.5 %all-reduce.4.cloned.1.call-done = f32[16,16384]{1,0:T(8,128)} async-done(((f32[16,16384]{1,0:T(8,128)}), f32[16,16384]{1,0:T(8,128)}) %all-reduce.4.cloned.1.call-update) | async-done | bytes 1048592
  138.8 1.7 %constant_dynamic-slice_fusion = f32[2,16384]{1,0:T(2,128)} fusion(f32[16,16384]{1,0:T(8,128)} %all-reduce.4.cloned.1.call-done, u32[]{:T(128)S(6)} %multiply.1), kind=kLoop, calls=%fused_computation.36 | loop fusion | bytes 262148
  (19 shorter events, 0.2 us)
Async XLA Ops:
  13.2 14.4 %all-to-all-start.1 = ((bf16[2,4,16]{2,0,1:T(2,128)(2,1)}), bf16[2,4,16]{2,0,1:T(2,128)(2,1)S(1)}, u32[]{:S(2)}, u32[]{:S(2)}) async-start(bf16[2,4,16]{2,0,1:T(2,128)(2,1)} %copy.31), calls=%async_computation.1 | async-start | bytes 4096 | tf_op jit(solution)/shard_map/all_to_all | solution.py:34
  27.6 5.2 %copy-start = (bf16[2,2,8192]{2,1,0:T(2,128)(2,1)S(1)}, bf16[2,2,8192]{2,1,0:T(2,128)(2,1)}, u32[]{:S(2)}) copy-start(bf16[2,2,8192]{2,1,0:T(2,128)(2,1)} %param.7) | copy-start | bytes 196612
  27.6 52.9 %all-to-all-start = ((bf16[2,4,16,8192]{3,2,0,1:T(8,128)(2,1)}), bf16[2,4,16,8192]{3,2,0,1:T(8,128)(2,1)S(1)}, u32[]{:S(2)}, u32[]{:S(2)}) async-start(bf16[2,4,16,8192]{3,2,0,1:T(8,128)(2,1)} %copy.29), calls=%async_computation | async-start | bytes 4194304 | tf_op jit(solution)/shard_map/all_to_all | solution.py:33
  32.8 105.9 %all-reduce.4.cloned.1.call-start = ((), (), s32[]{:S(2)}) async-start(), calls=%async_computation.3 | async-start | bytes 2097152
  81.8 5.1 %copy-start.1 = (u32[32]{0:T(128)S(1)}, u32[32]{0:T(128)}, u32[]{:S(2)}) copy-start(u32[32]{0:T(128)} %constant.56) | copy-start | bytes 388
  83.6 8.8 %all-to-all-start.2 = ((f32[2,4,16]{2,0,1:T(2,128)}), f32[2,4,16]{2,0,1:T(2,128)S(1)}, u32[]{:S(2)}, u32[]{:S(2)}) async-start(f32[2,4,16]{2,0,1:T(2,128)} %copy.38), calls=%async_computation.2 | async-start | bytes 8192 | tf_op jit(solution)/shard_map/all_to_all | solution.py:56
Sparse Core Ops, SparseCore 0:
  83.0 55.6 all-reduce.3
where the time goes:
time: 148 us; the launch traced here: 147 us
  waiting for transfers between devices  85.7 us (58%)
  local copies, waits for them, and re-layouts  17.3 us (12%)
  starting transfers between devices  14.8 us (10%)
  between operations  14.8 us (10%)
  blocking collectives  9.87 us (7%)
  other arithmetic  3.79 us (3%)
    unnamed x2, waiting for transfers between devices  44.6 us
    all_to_all x1, waiting for transfers between devices, on_device(): lax.all_to_all(packed, 'cls', split_axis=1, concat_axis=1, tiled=True)  36.9 us
    all_gather x1, blocking collectives, on_device(): piece = lax.all_gather(projections, 'dom', axis=1, tiled=True)  9.87 us
    all_to_all x1, starting transfers between devices, on_device(): lax.all_to_all(packed_prec, 'cls', split_axis=1, concat_axis=1, tiled=True)  6.32 us
    all_to_all x1, starting transfers between devices, on_device(): lax.all_to_all(packed, 'cls', split_axis=1, concat_axis=1, tiled=True)  5.22 us
    all_to_all x1, waiting for transfers between devices, on_device(): lax.all_to_all(log_total.reshape(per_owner, owners, capacity), 'cls', spl...  4.28 us
    all_to_all x1, starting transfers between devices, on_device(): lax.all_to_all(log_total.reshape(per_owner, owners, capacity), 'cls', spl...  3.25 us
    gather x1, local copies, waits for them, and re-layouts, on_device(): packed = padded[source].reshape(per_owner, owners, capacity, width)  3.22 us
  transfers between devices with their start and end apart: 4, of which 3 were waited for; matrix products, arithmetic and copies ran while one was open for 8% of the time, Pallas kernels for 0%

commit v1 on v0

v1 whole, which is shorter than its diff:
```python
import jax
import jax.numpy as jnp
from jax import lax
from jax.sharding import PartitionSpec as P

AXES = ("cls", "dom")
CORE = 1


def plan(mesh):
    owners, dom = mesh.shape["cls"], mesh.shape["dom"]
    plane_bits = (dom // 2).bit_length() - 1
    masks = [2 << bit for bit in range(plane_bits)]
    if plane_bits % 2:
        return owners, dom, (masks, masks), False
    low, high = masks[: plane_bits // 2], masks[plane_bits // 2 :]
    return owners, dom, (low + high, high + low), True


def solution(mesh):
    owners, dom, orders, crossed = plan(mesh)
    devices = owners * dom
    steps = len(orders[0])

    def swap(value, masks):
        pairs = [(i, i ^ masks[i % 2]) for i in range(devices)]
        return lax.ppermute(value, AXES, pairs)

    def swap_core(value):
        return swap(value, (CORE, CORE))

    def swap_plane(value, step):
        return swap(value, (orders[0][step], orders[1][step]))

    def swap_cls(value, k):
        return swap(value, (k * dom, k * dom))

    def on_device(particles, assign, inv_sigma, projections):
        local, width = particles.shape
        half = width // 2
        per_owner, own = projections.shape[:2]
        mine_rows = per_owner * own
        first = lax.axis_index("dom") % 2 == 0

        def halves_of(value):
            low, high = value[:, :half], value[:, half:]
            return jnp.where(first, low, high), jnp.where(first, high, low)

        flat = projections.reshape(mine_rows, width)
        kept, sent = halves_of(flat)
        got = swap_core(sent)
        block = jnp.concatenate(
            [jnp.where(first, kept, got), jnp.where(first, got, kept)], axis=0
        )
        pieces = {k: swap_cls(block, k) for k in range(owners - 1, 0, -1)}
        gathered = jnp.concatenate([block] + [pieces[k] for k in range(1, owners)], axis=0)

        side = jnp.stack([inv_sigma.astype(jnp.float32), assign[:, 0].astype(jnp.float32)])
        side = jnp.concatenate([side, swap_core(side)], axis=1)
        precision, class_id = side[0], side[1].astype(jnp.int32)
        kept, sent = halves_of(particles)
        images = jnp.concatenate([kept, swap_core(sent)], axis=0)

        def score(rows):
            products = lax.dot_general(
                rows, images, (((1,), (1,)), ((), ())), preferred_element_type=jnp.float32
            )
            norms = 0.5 * jnp.sum(jnp.square(rows.astype(jnp.float32)), axis=1)
            return products - norms[:, None]

        partial = [score(gathered)]
        for step in range(steps):
            fresh = swap_plane(gathered, step)
            partial.append(score(fresh))
            gathered = jnp.concatenate([gathered, fresh], axis=0)
        partial = jnp.concatenate(partial, axis=0)
        rows = partial.shape[0]
        other = swap_core(partial)
        if crossed:
            side_len = 1 << (steps // 2)
            other = other.reshape(side_len, side_len, -1, 2 * local).transpose(1, 0, 2, 3)
        other = other.reshape(rows, 2, local)[:, ::-1].reshape(rows, 2 * local)
        scores = precision[None, :] * (partial + other)

        z = lax.axis_index("cls") ^ jnp.arange(owners, dtype=jnp.int32)
        kind = z[:, None] * per_owner + jnp.arange(per_owner, dtype=jnp.int32)[None, :]
        kind = jnp.broadcast_to(
            kind[None, :, None, :, None], (rows // (2 * mine_rows * owners), owners, 2, per_owner, own)
        ).reshape(rows)
        named = kind[:, None] == class_id[None, :]
        largest = jnp.max(jnp.where(named, scores, -jnp.inf), axis=0)
        exponent = jnp.where(named, jnp.exp(jnp.where(named, scores - largest[None, :], 0.0)), 0.0)
        totals = jnp.sum(exponent, axis=0)
        weights = (exponent / totals[None, :]).astype(jnp.bfloat16)
        evidence = (largest + jnp.log(totals))[:local]

        def weigh(part, kind):
            return jnp.dot(part, images, preferred_element_type=jnp.float32).astype(kind)

        middle = rows // 2
        fresh = swap_plane(weigh(weights[middle:], jnp.bfloat16), steps - 1)
        sums = weigh(weights[:middle], jnp.float32) + fresh.astype(jnp.float32)
        for step in range(steps - 2, -1, -1):
            middle = sums.shape[0] // 2
            sums = sums[:middle] + swap_plane(sums[middle:], step)
        size = 2 * mine_rows
        total = sums[:size]
        for k in range(owners - 1, 0, -1):
            part = sums[k * size : (k + 1) * size]
            if k > 1:
                part = part.astype(jnp.bfloat16)
            total = total + swap_cls(part, k).astype(jnp.float32)
        low, high = total[:mine_rows], total[mine_rows:]
        kept, sent = jnp.where(first, low, high), jnp.where(first, high, low)
        got = swap_core(sent)
        class_sums = jnp.concatenate(
            [jnp.where(first, kept, got), jnp.where(first, got, kept)], axis=1
        )
        return class_sums.reshape(per_owner, own, width), evidence

    return jax.shard_map(
        on_device,
        mesh=mesh,
        in_specs=(
            P(("cls", "dom"), None),
            P(("cls", "dom"), None),
            P(("cls", "dom")),
            P("cls", "dom", None),
        ),
        out_specs=(P("cls", "dom", None), P(("cls", "dom"))),
        check_vma=False,
    )
```

time: 148 us -> 74.2 us (0.50)
  waiting for transfers between devices: 85.7 us -> 40.6 us
  local copies, waits for them, and re-layouts: 17.3 us -> 3.09 us
  between operations: 14.8 us -> 0.91 us
  blocking collectives: 9.87 us -> 0 us
  matrix products: 1.13 us -> 9.33 us
  starting transfers between devices: 14.8 us -> 16.6 us
    unnamed x2 -> x0, waiting for transfers between devices: 44.6 us -> none
    all_to_all x3 -> x0, waiting for transfers between devices: 41.1 us -> none  [the longest x1 36.9 us: on_device(): lax.all_to_all(packed, 'cls', split_axis=1, concat_axis=1, tiled=True)]
    ppermute x0 -> x15, waiting for transfers between devices: none -> 40.6 us  [swap(): return lax.ppermute(value, AXES, pairs)]
    ppermute x0 -> x15, starting transfers between devices: none -> 16.6 us  [swap(): return lax.ppermute(value, AXES, pairs)]
    all_to_all x3 -> x0, starting transfers between devices: 14.8 us -> none  [the longest x1 6.32 us: on_device(): lax.all_to_all(packed_prec, 'cls', split_axis=1, concat_axis=1, tiled=True)]
    all_gather x1 -> x0, blocking collectives: 9.87 us -> none  [on_device(): piece = lax.all_gather(projections, 'dom', axis=1, tiled=True)]
    dot_general x2 -> x5, matrix products: 1.13 us -> 9.33 us  [the longest x3 5.91 us: score(): lax.dot_general(rows, images, (((1,), (1,)), ((), ())), preferred_element...]
    gather x3 -> x0, local copies, waits for them, and re-layouts: 6.17 us -> none  [the longest x1 3.22 us: on_device(): packed = padded[source].reshape(per_owner, owners, capacity, width)]
  transfers between devices with their start and end apart: 4 -> 15, of which waited for: 3 -> 11; matrix products, arithmetic and copies ran while one was open for 8% -> 5% of each run, Pallas kernels for 0% -> 0%
where the time goes in v1:
time: 74.2 us; the launch traced here: 73.8 us
  waiting for transfers between devices  40.6 us (55%)
  starting transfers between devices  16.6 us (22%)
  matrix products  9.33 us (13%)
  other arithmetic  3.2 us (4%)
  local copies, waits for them, and re-layouts  3.09 us (4%)
  between operations  0.91 us (1%)
    ppermute x15, waiting for transfers between devices, swap(): return lax.ppermute(value, AXES, pairs)  40.6 us
    ppermute x15, starting transfers between devices, swap(): return lax.ppermute(value, AXES, pairs)  16.6 us
    dot_general x3, matrix products, score(): lax.dot_general(rows, images, (((1,), (1,)), ((), ())), preferred_element...  5.91 us
    dot_general x2, matrix products, weigh(): jnp.dot(part, images, preferred_element_type=jnp.float32).astype(kind)  3.42 us
    select_n x2, other arithmetic, halves_of(): return (jnp.where(first, low, high), jnp.where(first, high, low))  1.7 us
  transfers between devices with their start and end apart: 15, of which 11 were waited for; matrix products, arithmetic and copies ran while one was open for 5% of the time, Pallas kernels for 0%

profile of v1, /device:TPU:0, one launch (start us, length us, event | category | flops | bytes accessed | tf_op | source)
XLA Modules:
  0.0 73.8 jit_solution(10776990145057390631)
XLA Ops:
  0.6 0.9 %reshape.114 = bf16[4,8192]{1,0:T(4,128)(2,1)S(1)} reshape(bf16[2,2,8192]{2,1,0:T(2,128)(2,1)} %param.7) | data formatting | bytes 131072 | tf_op jit(solution)/shard_map/reshape | solution.py:49
  1.6 0.5 collective-permute-start.1
  2.1 1.7 %broadcast_select_fusion.1 = (bf16[128,4096]{1,0:T(8,128)(2,1)S(1)}, bf16[128,4096]{1,0:T(8,128)(2,1)S(1)}) fusion(pred[]{:T(512)S(6)} %eq.32, bf16[128,8192]{1,0:T(8,128)(2,1)} %param.4), kind=kLoop, calls=%fused_computation.8 | loop fusion | flops 1048576 | bytes 4194305 | tf_op jit(solution)/shard_map/jit(_where)/select_n | solution.py:47
  3.9 0.5 collective-permute-start
  4.5 2.7 %collective-permute-start.2 = (bf16[8,4096]{1,0:T(8,128)(2,1)S(1)}, bf16[8,4096]{1,0:T(8,128)(2,1)S(1)}, u32[]{:S(2)}, u32[]{:S(2)}) collective-permute-start(bf16[8,4096]{1,0:T(8,128)(2,1)S(1)} %pad_maximum_fusion.3), channel_id=1, source_target_pairs={{0,8},{1,9},{2,10},{3,11},{4,12},{5,13},{6,14},{7,15},{8,0},{9,1},... | collective-permute-start | bytes 196616 | tf_op jit(solution)/shard_map/ppermute | solution.py:27
  7.2 2.6 %collective-permute-start.3 = (bf16[8,4096]{1,0:T(8,128)(2,1)S(1)}, bf16[8,4096]{1,0:T(8,128)(2,1)S(1)}, u32[]{:S(2)}, u32[]{:S(2)}) collective-permute-start(bf16[8,4096]{1,0:T(8,128)(2,1)S(1)} %pad_maximum_fusion.3), channel_id=1, source_target_pairs={{0,16},{1,17},{2,18},{3,19},{4,20},{5,21},{6,22},{7,23},{8,24},{9,... | collective-permute-start | bytes 196616 | tf_op jit(solution)/shard_map/ppermute | solution.py:27
  9.9 5.0 %collective-permute-done.3 = bf16[8,4096]{1,0:T(8,128)(2,1)S(1)} collective-permute-done((bf16[8,4096]{1,0:T(8,128)(2,1)S(1)}, bf16[8,4096]{1,0:T(8,128)(2,1)S(1)}, u32[]{:S(2)}, u32[]{:S(2)}) %collective-permute-start.3) | collective-permute-done | bytes 65568 | tf_op jit(solution)/shard_map/ppermute | solution.py:27
  14.9 1.0 %collective-permute-done.4 = bf16[8,4096]{1,0:T(8,128)(2,1)S(1)} collective-permute-done((bf16[8,4096]{1,0:T(8,128)(2,1)S(1)}, bf16[8,4096]{1,0:T(8,128)(2,1)S(1)}, u32[]{:S(2)}, u32[]{:S(2)}) %collective-permute-start.4) | collective-permute-done | bytes 65568 | tf_op jit(solution)/shard_map/ppermute | solution.py:27
  16.0 1.6 %collective-permute-start.6 = (bf16[32,4096]{1,0:T(8,128)(2,1)S(1)}, bf16[32,4096]{1,0:T(8,128)(2,1)S(1)}, u32[]{:S(2)}, u32[]{:S(2)}) collective-permute-start(bf16[32,4096]{1,0:T(8,128)(2,1)S(1)} %concatenate.35), channel_id=1, source_target_pairs={{0,2},{1,5},{2,0},{3,7},{4,6},{5,1},{6,4},{7,3},{8,10},{9,13},{10,... | collective-permute-start | bytes 786440 | tf_op jit(solution)/shard_map/ppermute | solution.py:27
  18.0 4.4 %collective-permute-done.6 = bf16[32,4096]{1,0:T(8,128)(2,1)S(1)} collective-permute-done((bf16[32,4096]{1,0:T(8,128)(2,1)S(1)}, bf16[32,4096]{1,0:T(8,128)(2,1)S(1)}, u32[]{:S(2)}, u32[]{:S(2)}) %collective-permute-start.6) | collective-permute-done | bytes 262176 | tf_op jit(solution)/shard_map/ppermute | solution.py:27
  22.6 1.6 %collective-permute-start.7 = (bf16[64,4096]{1,0:T(8,128)(2,1)S(1)}, bf16[64,4096]{1,0:T(8,128)(2,1)S(1)}, u32[]{:S(2)}, u32[]{:S(2)}) collective-permute-start(bf16[64,4096]{1,0:T(8,128)(2,1)S(1)} %concatenate.37), channel_id=1, source_target_pairs={{0,4},{1,3},{2,6},{3,1},{4,0},{5,7},{6,2},{7,5},{8,12},{9,11},{10,... | collective-permute-start | bytes 1572872 | tf_op jit(solution)/shard_map/ppermute | solution.py:27
  24.3 7.5 %collective-permute-done.7 = bf16[64,4096]{1,0:T(8,128)(2,1)S(1)} collective-permute-done((bf16[64,4096]{1,0:T(8,128)(2,1)S(1)}, bf16[64,4096]{1,0:T(8,128)(2,1)S(1)}, u32[]{:S(2)}, u32[]{:S(2)}) %collective-permute-start.7) | collective-permute-done | bytes 524320 | tf_op jit(solution)/shard_map/ppermute | solution.py:27
  32.1 2.0 %convolution_subtract_fusion.2 = f32[32,256]{1,0:T(8,128)S(1)} fusion(bf16[32,4096]{1,0:T(8,128)(2,1)S(1)} %concatenate.35, f32[32]{0:T(128)S(1)} %broadcast_multiply_fusion.2, bf16[128,4096]{1,0:T(8,128)(2,1)} %collective-permute-done.5, bf16[128,4096]{1,0:T(8,128)(2,1)S(1)} %get-tuple-element.6), kind=kOutput, calls=%fused_computation.5 | convolution fusion | flops 71311360 | bytes 2392192 | tf_op jit(solution)/shard_map/dot_general | solution.py:65
  34.0 2.0 %convolution_subtract_fusion.1 = f32[32,256]{1,0:T(8,128)S(1)} fusion(bf16[32,4096]{1,0:T(8,128)(2,1)S(1)} %collective-permute-done.6, f32[32]{0:T(128)S(1)} %broadcast_multiply_fusion.1, bf16[128,4096]{1,0:T(8,128)(2,1)} %collective-permute-done.5, bf16[128,4096]{1,0:T(8,128)(2,1)S(1)} %get-tuple-element.6), kind=kOutput, calls=%fused_computation.4 | convolution fusion | flops 71311360 | bytes 2392192 | tf_op jit(solution)/shard_map/dot_general | solution.py:65
  36.0 2.0 %convolution_subtract_fusion = f32[64,256]{1,0:T(8,128)S(1)} fusion(bf16[64,4096]{1,0:T(8,128)(2,1)S(1)} %collective-permute-done.7, f32[64]{0:T(128)S(1)} %broadcast_multiply_fusion, bf16[128,4096]{1,0:T(8,128)(2,1)} %collective-permute-done.5, bf16[128,4096]{1,0:T(8,128)(2,1)S(1)} %get-tuple-element.6), kind=kOutput, calls=%fused_computation.3 | convolution fusion | flops 138428416 | bytes 2687232 | tf_op jit(solution)/shard_map/dot_general | solution.py:65
  38.2 1.2 %collective-permute-done.8 = f32[128,256]{1,0:T(8,128)S(1)} collective-permute-done((f32[128,256]{1,0:T(8,128)S(1)}, f32[128,256]{1,0:T(8,128)S(1)}, u32[]{:S(2)}, u32[]{:S(2)}) %collective-permute-start.8) | collective-permute-done | bytes 131104 | tf_op jit(solution)/shard_map/ppermute | solution.py:27
  39.5 0.3 rev.3
  39.8 0.2 fusion.2
  40.0 0.2 fusion.10
  40.3 1.7 %convolution_convert_fusion = bf16[64,4096]{1,0:T(8,128)(2,1)S(1)} fusion(bf16[128,256]{1,0:T(8,128)(2,1)S(1)} %fusion.9, bf16[128,4096]{1,0:T(8,128)(2,1)} %collective-permute-done.5, bf16[128,4096]{1,0:T(8,128)(2,1)S(1)} %get-tuple-element.6), kind=kOutput, calls=%fused_computation.1 | convolution fusion | flops 138674176 | bytes 2654208 | tf_op jit(solution)/shard_map/dot_general | solution.py:98
  42.1 1.6 %collective-permute-start.9 = (bf16[64,4096]{1,0:T(8,128)(2,1)S(1)}, bf16[64,4096]{1,0:T(8,128)(2,1)S(1)}, u32[]{:S(2)}, u32[]{:S(2)}) collective-permute-start(bf16[64,4096]{1,0:T(8,128)(2,1)S(1)} %convolution_convert_fusion), channel_id=1, source_target_pairs={{0,4},{1,3},{2,6},{3,1},{4,0},{5,7},{6,2},{7,5},{8,12},{9,11},{10,... | collective-permute-start | bytes 1572872 | tf_op jit(solution)/shard_map/ppermute | solution.py:27
  43.6 7.7 %collective-permute-done.9 = bf16[64,4096]{1,0:T(8,128)(2,1)S(1)} collective-permute-done((bf16[64,4096]{1,0:T(8,128)(2,1)S(1)}, bf16[64,4096]{1,0:T(8,128)(2,1)S(1)}, u32[]{:S(2)}, u32[]{:S(2)}) %collective-permute-start.9) | collective-permute-done | bytes 524320 | tf_op jit(solution)/shard_map/ppermute | solution.py:27
  51.3 1.7 %convolution_add_fusion = f32[64,4096]{1,0:T(8,128)S(1)} fusion(bf16[64,4096]{1,0:T(8,128)(2,1)S(1)} %collective-permute-done.9, bf16[128,256]{1,0:T(8,128)(2,1)S(1)} %fusion.9, bf16[128,4096]{1,0:T(8,128)(2,1)} %collective-permute-done.5, bf16[128,4096]{1,0:T(8,128)(2,1)S(1)} %get-tuple-element.6), kind=kOutput, calls=%fused_computation | convolution fusion | flops 138936320 | bytes 3702784 | tf_op jit(solution)/shard_map/dot_general | solution.py:98
  53.1 1.6 %collective-permute-start.10 = (f32[32,4096]{1,0:T(8,128)S(1)}, f32[32,4096]{1,0:T(8,128)S(1)}, u32[]{:S(2)}, u32[]{:S(2)}) collective-permute-start(f32[32,4096]{1,0:T(8,128)S(1)} %slice.77), channel_id=1, source_target_pairs={{0,2},{1,5},{2,0},{3,7},{4,6},{5,1},{6,4},{7,3},{8,10},{9,13},{10,... | collective-permute-start | bytes 1572872 | tf_op jit(solution)/shard_map/ppermute | solution.py:27
  54.6 7.7 %collective-permute-done.10 = f32[32,4096]{1,0:T(8,128)S(1)} collective-permute-done((f32[32,4096]{1,0:T(8,128)S(1)}, f32[32,4096]{1,0:T(8,128)S(1)}, u32[]{:S(2)}, u32[]{:S(2)}) %collective-permute-start.10) | collective-permute-done | bytes 524320 | tf_op jit(solution)/shard_map/ppermute | solution.py:27
  62.4 1.3 %collective-permute-start.13 = (f32[8,4096]{1,0:T(8,128)S(1)}, f32[8,4096]{1,0:T(8,128)S(1)}, u32[]{:S(2)}, u32[]{:S(2)}) collective-permute-start(f32[8,4096]{1,0:T(8,128)S(1)} %slice.81), channel_id=1, source_target_pairs={{0,8},{1,9},{2,10},{3,11},{4,12},{5,13},{6,14},{7,15},{8,0},{9,1},... | collective-permute-start | bytes 393224 | tf_op jit(solution)/shard_map/ppermute | solution.py:27
  63.7 2.5 %collective-permute-start.11 = (bf16[8,4096]{1,0:T(8,128)(2,1)S(1)}, bf16[8,4096]{1,0:T(8,128)(2,1)S(1)}, u32[]{:S(2)}, u32[]{:S(2)}) collective-permute-start(bf16[8,4096]{1,0:T(8,128)(2,1)S(1)} %get-tuple-element.8), channel_id=1, source_target_pairs={{0,24},{1,25},{2,26},{3,27},{4,28},{5,29},{6,30},{7,31},{8,16},{9,... | collective-permute-start | bytes 196616 | tf_op jit(solution)/shard_map/ppermute | solution.py:27
  66.2 3.8 %collective-permute-done.11 = bf16[8,4096]{1,0:T(8,128)(2,1)S(1)} collective-permute-done((bf16[8,4096]{1,0:T(8,128)(2,1)S(1)}, bf16[8,4096]{1,0:T(8,128)(2,1)S(1)}, u32[]{:S(2)}, u32[]{:S(2)}) %collective-permute-start.11) | collective-permute-done | bytes 65568 | tf_op jit(solution)/shard_map/ppermute | solution.py:27
  70.0 1.5 %collective-permute-done.12 = bf16[8,4096]{1,0:T(8,128)(2,1)S(1)} collective-permute-done((bf16[8,4096]{1,0:T(8,128)(2,1)S(1)}, bf16[8,4096]{1,0:T(8,128)(2,1)S(1)}, u32[]{:S(2)}, u32[]{:S(2)}) %collective-permute-start.12) | collective-permute-done | bytes 65568 | tf_op jit(solution)/shard_map/ppermute | solution.py:27
  71.7 0.5 slice.69
  72.2 0.7 collective-permute-done.14
  73.0 0.8 %reshape.118 = f32[2,2,8192]{2,1,0:T(2,128)} reshape(f32[4,8192]{1,0:T(4,128)S(1)} %pad_maximum_fusion.2) | data formatting | bytes 262144 | tf_op jit(solution)/shard_map/reshape | solution.py:119
  (50 shorter events, 2.1 us)
Async XLA Ops:
  1.5 2.4 %copy-start = (bf16[128]{0:T(256)(128)(2,1)S(1)}, bf16[128]{0:T(256)(128)(2,1)}, u32[]{:S(2)}) copy-start(bf16[128]{0:T(256)(128)(2,1)} %param.6) | copy-start | bytes 772
  1.6 2.3 %copy-start.1 = (s32[128,1]{0,1:T(1,128)S(1)}, s32[128,1]{0,1:T(1,128)}, u32[]{:S(2)}) copy-start(s32[128,1]{0,1:T(1,128)} %param.5) | copy-start | bytes 1540
  1.6 2.9 %collective-permute-start.1 = (bf16[4,4096]{1,0:T(4,128)(2,1)S(1)}, bf16[4,4096]{1,0:T(4,128)(2,1)S(1)}, u32[]{:S(2)}, u32[]{:S(2)}) collective-permute-start(bf16[4,4096]{1,0:T(4,128)(2,1)S(1)} %broadcast_select_fusion.6), channel_id=1, source_target_pairs={{0,1},{1,0},{2,3},{3,2},{4,5},{5,4},{6,7},{7,6},{8,9},{9,8},{10,11... | collective-permute-start | bytes 98312 | tf_op jit(solution)/shard_map/ppermute | solution.py:27
  3.8 28.3 %collective-permute-start.5 = (bf16[128,4096]{1,0:T(8,128)(2,1)S(1)}, bf16[128,4096]{1,0:T(8,128)(2,1)}, u32[]{:S(2)}, u32[]{:S(2)}) collective-permute-start(bf16[128,4096]{1,0:T(8,128)(2,1)S(1)} %get-tuple-element.7), channel_id=1, source_target_pairs={{0,1},{1,0},{2,3},{3,2},{4,5},{5,4},{6,7},{7,6},{8,9},{9,8},{10,11... | collective-permute-start | bytes 3145736 | tf_op jit(solution)/shard_map/ppermute | solution.py:27
  3.9 13.9 %collective-permute-start = (f32[2,128]{1,0:T(2,128)S(1)}, f32[2,128]{1,0:T(2,128)S(1)}, u32[]{:S(2)}, u32[]{:S(2)}) collective-permute-start(f32[2,128]{1,0:T(2,128)S(1)} %pad_maximum_fusion.5), channel_id=1, source_target_pairs={{0,1},{1,0},{2,3},{3,2},{4,5},{5,4},{6,7},{7,6},{8,9},{9,8},{10,11... | collective-permute-start | bytes 3080 | tf_op jit(solution)/shard_map/ppermute | solution.py:27
  4.5 5.4 %collective-permute-start.2 = (bf16[8,4096]{1,0:T(8,128)(2,1)S(1)}, bf16[8,4096]{1,0:T(8,128)(2,1)S(1)}, u32[]{:S(2)}, u32[]{:S(2)}) collective-permute-start(bf16[8,4096]{1,0:T(8,128)(2,1)S(1)} %pad_maximum_fusion.3), channel_id=1, source_target_pairs={{0,8},{1,9},{2,10},{3,11},{4,12},{5,13},{6,14},{7,15},{8,0},{9,1},... | collective-permute-start | bytes 196616 | tf_op jit(solution)/shard_map/ppermute | solution.py:27
  7.2 7.7 %collective-permute-start.3 = (bf16[8,4096]{1,0:T(8,128)(2,1)S(1)}, bf16[8,4096]{1,0:T(8,128)(2,1)S(1)}, u32[]{:S(2)}, u32[]{:S(2)}) collective-permute-start(bf16[8,4096]{1,0:T(8,128)(2,1)S(1)} %pad_maximum_fusion.3), channel_id=1, source_target_pairs={{0,16},{1,17},{2,18},{3,19},{4,20},{5,21},{6,22},{7,23},{8,24},{9,... | collective-permute-start | bytes 196616 | tf_op jit(solution)/shard_map/ppermute | solution.py:27
  9.8 6.1 %collective-permute-start.4 = (bf16[8,4096]{1,0:T(8,128)(2,1)S(1)}, bf16[8,4096]{1,0:T(8,128)(2,1)S(1)}, u32[]{:S(2)}, u32[]{:S(2)}) collective-permute-start(bf16[8,4096]{1,0:T(8,128)(2,1)S(1)} %pad_maximum_fusion.3), channel_id=1, source_target_pairs={{0,24},{1,25},{2,26},{3,27},{4,28},{5,29},{6,30},{7,31},{8,16},{9,... | collective-permute-start | bytes 196616 | tf_op jit(solution)/shard_map/ppermute | solution.py:27
  16.0 6.4 %collective-permute-start.6 = (bf16[32,4096]{1,0:T(8,128)(2,1)S(1)}, bf16[32,4096]{1,0:T(8,128)(2,1)S(1)}, u32[]{:S(2)}, u32[]{:S(2)}) collective-permute-start(bf16[32,4096]{1,0:T(8,128)(2,1)S(1)} %concatenate.35), channel_id=1, source_target_pairs={{0,2},{1,5},{2,0},{3,7},{4,6},{5,1},{6,4},{7,3},{8,10},{9,13},{10,... | collective-permute-start | bytes 786440 | tf_op jit(solution)/shard_map/ppermute | solution.py:27
  22.6 9.2 %collective-permute-start.7 = (bf16[64,4096]{1,0:T(8,128)(2,1)S(1)}, bf16[64,4096]{1,0:T(8,128)(2,1)S(1)}, u32[]{:S(2)}, u32[]{:S(2)}) collective-permute-start(bf16[64,4096]{1,0:T(8,128)(2,1)S(1)} %concatenate.37), channel_id=1, source_target_pairs={{0,4},{1,3},{2,6},{3,1},{4,0},{5,7},{6,2},{7,5},{8,12},{9,11},{10,... | collective-permute-start | bytes 1572872 | tf_op jit(solution)/shard_map/ppermute | solution.py:27
  38.0 1.4 %collective-permute-start.8 = (f32[128,256]{1,0:T(8,128)S(1)}, f32[128,256]{1,0:T(8,128)S(1)}, u32[]{:S(2)}, u32[]{:S(2)}) collective-permute-start(f32[128,256]{1,0:T(8,128)S(1)} %pad_maximum_fusion.1), channel_id=1, source_target_pairs={{0,1},{1,0},{2,3},{3,2},{4,5},{5,4},{6,7},{7,6},{8,9},{9,8},{10,11... | collective-permute-start | bytes 393224 | tf_op jit(solution)/shard_map/ppermute | solution.py:27
  42.1 9.2 %collective-permute-start.9 = (bf16[64,4096]{1,0:T(8,128)(2,1)S(1)}, bf16[64,4096]{1,0:T(8,128)(2,1)S(1)}, u32[]{:S(2)}, u32[]{:S(2)}) collective-permute-start(bf16[64,4096]{1,0:T(8,128)(2,1)S(1)} %convolution_convert_fusion), channel_id=1, source_target_pairs={{0,4},{1,3},{2,6},{3,1},{4,0},{5,7},{6,2},{7,5},{8,12},{9,11},{10,... | collective-permute-start | bytes 1572872 | tf_op jit(solution)/shard_map/ppermute | solution.py:27
  53.1 9.2 %collective-permute-start.10 = (f32[32,4096]{1,0:T(8,128)S(1)}, f32[32,4096]{1,0:T(8,128)S(1)}, u32[]{:S(2)}, u32[]{:S(2)}) collective-permute-start(f32[32,4096]{1,0:T(8,128)S(1)} %slice.77), channel_id=1, source_target_pairs={{0,2},{1,5},{2,0},{3,7},{4,6},{5,1},{6,4},{7,3},{8,10},{9,13},{10,... | collective-permute-start | bytes 1572872 | tf_op jit(solution)/shard_map/ppermute | solution.py:27
  62.4 9.1 %collective-permute-start.13 = (f32[8,4096]{1,0:T(8,128)S(1)}, f32[8,4096]{1,0:T(8,128)S(1)}, u32[]{:S(2)}, u32[]{:S(2)}) collective-permute-start(f32[8,4096]{1,0:T(8,128)S(1)} %slice.81), channel_id=1, source_target_pairs={{0,8},{1,9},{2,10},{3,11},{4,12},{5,13},{6,14},{7,15},{8,0},{9,1},... | collective-permute-start | bytes 393224 | tf_op jit(solution)/shard_map/ppermute | solution.py:27
  63.7 6.3 %collective-permute-start.11 = (bf16[8,4096]{1,0:T(8,128)(2,1)S(1)}, bf16[8,4096]{1,0:T(8,128)(2,1)S(1)}, u32[]{:S(2)}, u32[]{:S(2)}) collective-permute-start(bf16[8,4096]{1,0:T(8,128)(2,1)S(1)} %get-tuple-element.8), channel_id=1, source_target_pairs={{0,24},{1,25},{2,26},{3,27},{4,28},{5,29},{6,30},{7,31},{8,16},{9,... | collective-permute-start | bytes 196616 | tf_op jit(solution)/shard_map/ppermute | solution.py:27
  66.2 5.4 %collective-permute-start.12 = (bf16[8,4096]{1,0:T(8,128)(2,1)S(1)}, bf16[8,4096]{1,0:T(8,128)(2,1)S(1)}, u32[]{:S(2)}, u32[]{:S(2)}) collective-permute-start(bf16[8,4096]{1,0:T(8,128)(2,1)S(1)} %get-tuple-element.9), channel_id=1, source_target_pairs={{0,16},{1,17},{2,18},{3,19},{4,20},{5,21},{6,22},{7,23},{8,24},{9,... | collective-permute-start | bytes 196616 | tf_op jit(solution)/shard_map/ppermute | solution.py:27
  71.6 1.3 %collective-permute-start.14 = (f32[4,4096]{1,0:T(4,128)S(1)}, f32[4,4096]{1,0:T(4,128)S(1)}, u32[]{:S(2)}, u32[]{:S(2)}) collective-permute-start(f32[4,4096]{1,0:T(4,128)S(1)} %slice_select_fusion), channel_id=1, source_target_pairs={{0,1},{1,0},{2,3},{3,2},{4,5},{5,4},{6,7},{7,6},{8,9},{9,8},{10,11... | collective-permute-start | bytes 196616 | tf_op jit(solution)/shard_map/ppermute | solution.py:27

commit v2 on v1

--- a/solution.py
+++ b/solution.py
@@ -52,8 +52,20 @@
         block = jnp.concatenate(
             [jnp.where(first, kept, got), jnp.where(first, got, kept)], axis=0
         )
-        pieces = {k: swap_cls(block, k) for k in range(owners - 1, 0, -1)}
-        gathered = jnp.concatenate([block] + [pieces[k] for k in range(1, owners)], axis=0)
+        near = max(owners // 2, 1)
+        pieces = {k: swap_cls(block, k) for k in range(1, owners)}
+        pieces[0] = block
+        groups = [range(0, near)] + ([range(near, owners)] if owners > 1 else [])
+
+        def spread(held):
+            older, newer = [held], []
+            for step in range(steps):
+                sets = [part for part in (older, newer) if part]
+                got = [swap_plane(jnp.concatenate(part, axis=0), step) for part in sets]
+                older, newer = older + newer, got
+            return jnp.concatenate(older + newer, axis=0)
+
+        gathered = [spread(jnp.concatenate([pieces[k] for k in g], axis=0)) for g in groups]
 
         side = jnp.stack([inv_sigma.astype(jnp.float32), assign[:, 0].astype(jnp.float32)])
         side = jnp.concatenate([side, swap_core(side)], axis=1)
@@ -68,24 +80,21 @@
             norms = 0.5 * jnp.sum(jnp.square(rows.astype(jnp.float32)), axis=1)
             return products - norms[:, None]
 
-        partial = [score(gathered)]
-        for step in range(steps):
-            fresh = swap_plane(gathered, step)
-            partial.append(score(fresh))
-            gathered = jnp.concatenate([gathered, fresh], axis=0)
-        partial = jnp.concatenate(partial, axis=0)
+        partial = jnp.concatenate([score(part) for part in gathered], axis=0)
         rows = partial.shape[0]
         other = swap_core(partial)
         if crossed:
             side_len = 1 << (steps // 2)
-            other = other.reshape(side_len, side_len, -1, 2 * local).transpose(1, 0, 2, 3)
+            other = other.reshape(len(groups), side_len, side_len, -1, 2 * local)
+            other = other.transpose(0, 2, 1, 3, 4)
         other = other.reshape(rows, 2, local)[:, ::-1].reshape(rows, 2 * local)
         scores = precision[None, :] * (partial + other)
 
         z = lax.axis_index("cls") ^ jnp.arange(owners, dtype=jnp.int32)
         kind = z[:, None] * per_owner + jnp.arange(per_owner, dtype=jnp.int32)[None, :]
         kind = jnp.broadcast_to(
-            kind[None, :, None, :, None], (rows // (2 * mine_rows * owners), owners, 2, per_owner, own)
+            kind.reshape(len(groups), 1, -1, 1, per_owner, 1),
+            (len(groups), 1 << steps, owners // len(groups), 2, per_owner, own),
         ).reshape(rows)
         named = kind[:, None] == class_id[None, :]
         largest = jnp.max(jnp.where(named, scores, -jnp.inf), axis=0)
@@ -94,22 +103,37 @@
         weights = (exponent / totals[None, :]).astype(jnp.bfloat16)
         evidence = (largest + jnp.log(totals))[:local]
 
-        def weigh(part, kind):
-            return jnp.dot(part, images, preferred_element_type=jnp.float32).astype(kind)
+        def weigh(part):
+            return jnp.dot(part, images, preferred_element_type=jnp.float32)
 
-        middle = rows // 2
-        fresh = swap_plane(weigh(weights[middle:], jnp.bfloat16), steps - 1)
-        sums = weigh(weights[:middle], jnp.float32) + fresh.astype(jnp.float32)
-        for step in range(steps - 2, -1, -1):
-            middle = sums.shape[0] // 2
-            sums = sums[:middle] + swap_plane(sums[middle:], step)
         size = 2 * mine_rows
-        total = sums[:size]
-        for k in range(owners - 1, 0, -1):
-            part = sums[k * size : (k + 1) * size]
-            if k > 1:
-                part = part.astype(jnp.bfloat16)
-            total = total + swap_cls(part, k).astype(jnp.float32)
+
+        def reduce(part):
+            for step in range(steps - 1, -1, -1):
+                kind = jnp.bfloat16 if step == steps - 1 else jnp.float32
+                count = part.shape[0] // 2
+                keep, send = part[:count], part[count:].astype(kind)
+                if step:
+                    far = swap_plane(send[count // 2 :], step).astype(jnp.float32)
+                    close = swap_plane(send[: count // 2], step).astype(jnp.float32)
+                    part = jnp.concatenate(
+                        [keep[: count // 2] + close, keep[count // 2 :] + far], axis=0
+                    )
+                else:
+                    part = keep + swap_plane(send, step).astype(jnp.float32)
+            return part
+
+        total = None
+        count = rows // len(groups)
+        for i in range(len(groups) - 1, -1, -1):
+            sums = reduce(weigh(weights[i * count : (i + 1) * count]))
+            for j, k in enumerate(groups[i]):
+                part = sums[j * size : (j + 1) * size]
+                if k > 1:
+                    part = part.astype(jnp.bfloat16)
+                if k > 0:
+                    part = swap_cls(part, k).astype(jnp.float32)
+                total = part if total is None else total + part
         low, high = total[:mine_rows], total[mine_rows:]
         kept, sent = jnp.where(first, low, high), jnp.where(first, high, low)
         got = swap_core(sent)

time: 74.2 us -> 60.9 us (0.82)
  waiting for transfers between devices: 40.6 us -> 20.7 us
  starting transfers between devices: 16.6 us -> 25.2 us
  matrix products: 9.33 us -> 2.49 us
  local copies, waits for them, and re-layouts: 3.09 us -> 6.98 us
  other arithmetic: 3.2 us -> 4.21 us
    ppermute x15 -> x23, waiting for transfers between devices: 40.6 us -> 20.7 us  [swap(): return lax.ppermute(value, AXES, pairs)]
    ppermute x15 -> x23, starting transfers between devices: 16.6 us -> 25.2 us  [swap(): return lax.ppermute(value, AXES, pairs)]
    dot_general x3 -> x2, matrix products: 5.91 us -> 1.53 us  [score(): lax.dot_general(rows, images, (((1,), (1,)), ((), ())), preferred_element...]
    concatenate x5, local copies, waits for them, and re-layouts: 0.29 us -> 3.51 us  [the longest x2 2.8 us: spread(): return jnp.concatenate(older + newer, axis=0)]
    dot_general x2, matrix products: 3.42 us -> 0.96 us  [weigh(): return jnp.dot(part, images, preferred_element_type=jnp.float32)]
    select_n x2, other arithmetic: 1.7 us -> 2.72 us  [halves_of(): return (jnp.where(first, low, high), jnp.where(first, high, low))]
  transfers between devices with their start and end apart: 15 -> 23, of which waited for: 11 -> 13; matrix products, arithmetic and copies ran while one was open for 5% -> 15% of each run, Pallas kernels for 0% -> 0%
where the time goes in v2:
time: 60.9 us; the launch traced here: 60.6 us
  starting transfers between devices  25.2 us (41%)
  waiting for transfers between devices  20.7 us (34%)
  local copies, waits for them, and re-layouts  6.98 us (11%)
  other arithmetic  4.21 us (7%)
  matrix products  2.49 us (4%)
  between operations  0.94 us (2%)
    ppermute x23, starting transfers between devices, swap(): return lax.ppermute(value, AXES, pairs)  25.2 us
    ppermute x23, waiting for transfers between devices, swap(): return lax.ppermute(value, AXES, pairs)  20.7 us
    concatenate x2, local copies, waits for them, and re-layouts, spread(): return jnp.concatenate(older + newer, axis=0)  2.8 us
    select_n x2, other arithmetic, halves_of(): return (jnp.where(first, low, high), jnp.where(first, high, low))  2.72 us
    dot_general x2, matrix products, score(): lax.dot_general(rows, images, (((1,), (1,)), ((), ())), preferred_element...  1.53 us
  transfers between devices with their start and end apart: 23, of which 13 were waited for; matrix products, arithmetic and copies ran while one was open for 15% of the time, Pallas kernels for 0%

profile of v2, /device:TPU:0, one launch (start us, length us, event | category | flops | bytes accessed | tf_op | source)
XLA Modules:
  0.0 60.6 jit_solution(5863045460895670018)
XLA Ops:
  0.6 0.9 %reshape.103 = bf16[4,8192]{1,0:T(4,128)(2,1)S(1)} reshape(bf16[2,2,8192]{2,1,0:T(2,128)(2,1)} %param.7) | data formatting | bytes 131072 | tf_op jit(solution)/shard_map/reshape | solution.py:49
  2.1 2.7 %broadcast_select_fusion.1 = (bf16[128,4096]{1,0:T(8,128)(2,1)S(1)}, bf16[128,4096]{1,0:T(8,128)(2,1)}) fusion(pred[]{:T(512)S(6)} %eq.32, bf16[128,8192]{1,0:T(8,128)(2,1)} %param.4), kind=kLoop, calls=%fused_computation.6 | loop fusion | flops 1048576 | bytes 4194305 | tf_op jit(solution)/shard_map/jit(_where)/select_n | solution.py:47
  5.5 2.7 %collective-permute-start.2 = (bf16[8,4096]{1,0:T(8,128)(2,1)S(1)}, bf16[8,4096]{1,0:T(8,128)(2,1)S(1)}, u32[]{:S(2)}, u32[]{:S(2)}) collective-permute-start(bf16[8,4096]{1,0:T(8,128)(2,1)S(1)} %pad_maximum_fusion.4), channel_id=1, source_target_pairs={{0,8},{1,9},{2,10},{3,11},{4,12},{5,13},{6,14},{7,15},{8,0},{9,1},... | collective-permute-start | bytes 196616 | tf_op jit(solution)/shard_map/ppermute | solution.py:27
  8.2 2.6 %collective-permute-start.7 = (bf16[8,4096]{1,0:T(8,128)(2,1)S(1)}, bf16[8,4096]{1,0:T(8,128)(2,1)S(1)}, u32[]{:S(2)}, u32[]{:S(2)}) collective-permute-start(bf16[8,4096]{1,0:T(8,128)(2,1)S(1)} %pad_maximum_fusion.4), channel_id=1, source_target_pairs={{0,16},{1,17},{2,18},{3,19},{4,20},{5,21},{6,22},{7,23},{8,24},{9,... | collective-permute-start | bytes 196616 | tf_op jit(solution)/shard_map/ppermute | solution.py:27
  10.9 1.7 %collective-permute-start.3 = (bf16[16,4096]{1,0:T(8,128)(2,1)S(1)}, bf16[16,4096]{1,0:T(8,128)(2,1)S(1)}, u32[]{:S(2)}, u32[]{:S(2)}) collective-permute-start(bf16[16,4096]{1,0:T(8,128)(2,1)S(1)} %pad_maximum_fusion.1), channel_id=1, source_target_pairs={{0,2},{1,5},{2,0},{3,7},{4,6},{5,1},{6,4},{7,3},{8,10},{9,13},{10,... | collective-permute-start | bytes 393224 | tf_op jit(solution)/shard_map/ppermute | solution.py:27
  12.7 2.5 %collective-permute-done.7 = bf16[8,4096]{1,0:T(8,128)(2,1)S(1)} collective-permute-done((bf16[8,4096]{1,0:T(8,128)(2,1)S(1)}, bf16[8,4096]{1,0:T(8,128)(2,1)S(1)}, u32[]{:S(2)}, u32[]{:S(2)}) %collective-permute-start.7) | collective-permute-done | bytes 65568 | tf_op jit(solution)/shard_map/ppermute | solution.py:27
  15.2 0.6 %constant_dynamic-update-slice_fusion.1 = (bf16[16,4096]{1,0:T(8,128)(2,1)}, bf16[64,4096]{1,0:T(8,128)(2,1)S(1)}) fusion(bf16[8,4096]{1,0:T(8,128)(2,1)S(1)} %collective-permute-done.7), kind=kLoop, calls=%fused_computation.49 | loop fusion | bytes 196608
  15.8 1.1 %collective-permute-done.8 = bf16[8,4096]{1,0:T(8,128)(2,1)S(1)} collective-permute-done((bf16[8,4096]{1,0:T(8,128)(2,1)S(1)}, bf16[8,4096]{1,0:T(8,128)(2,1)S(1)}, u32[]{:S(2)}, u32[]{:S(2)}) %collective-permute-start.8) | collective-permute-done | bytes 65568 | tf_op jit(solution)/shard_map/ppermute | solution.py:27
  16.9 0.6 %constant_dynamic-update-slice_fusion = (bf16[16,4096]{1,0:T(8,128)(2,1)}, bf16[64,4096]{1,0:T(8,128)(2,1)S(1)}) fusion(bf16[16,4096]{1,0:T(8,128)(2,1)} %get-tuple-element.18, bf16[8,4096]{1,0:T(8,128)(2,1)S(1)} %collective-permute-done.8, bf16[64,4096]{1,0:T(8,128)(2,1)S(1)} %get-tuple-element.19), kind=kLoop, calls=%fused_computation.48 | loop fusion | bytes 196608 | tf_op jit(solution)/shard_map/concatenate | solution.py:68
  17.5 1.5 %collective-permute-start.9 = (bf16[16,4096]{1,0:T(8,128)(2,1)}, bf16[16,4096]{1,0:T(8,128)(2,1)S(1)}, u32[]{:S(2)}, u32[]{:S(2)}) collective-permute-start(bf16[16,4096]{1,0:T(8,128)(2,1)} %get-tuple-element.16), channel_id=1, source_target_pairs={{0,2},{1,5},{2,0},{3,7},{4,6},{5,1},{6,4},{7,3},{8,10},{9,13},{10,... | collective-permute-start | bytes 393224 | tf_op jit(solution)/shard_map/ppermute | solution.py:27
  19.3 1.6 %collective-permute-start.4 = (bf16[16,4096]{1,0:T(8,128)(2,1)S(1)}, bf16[16,4096]{1,0:T(8,128)(2,1)}, u32[]{:S(2)}, u32[]{:S(2)}) collective-permute-start(bf16[16,4096]{1,0:T(8,128)(2,1)S(1)} %pad_maximum_fusion.1), channel_id=1, source_target_pairs={{0,4},{1,3},{2,6},{3,1},{4,0},{5,7},{6,2},{7,5},{8,12},{9,11},{10,... | collective-permute-start | bytes 393224 | tf_op jit(solution)/shard_map/ppermute | solution.py:27
  21.4 1.5 %collective-permute-start.5 = (bf16[16,4096]{1,0:T(8,128)(2,1)S(1)}, bf16[16,4096]{1,0:T(8,128)(2,1)}, u32[]{:S(2)}, u32[]{:S(2)}) collective-permute-start(bf16[16,4096]{1,0:T(8,128)(2,1)S(1)} %collective-permute-done.3), channel_id=1, source_target_pairs={{0,4},{1,3},{2,6},{3,1},{4,0},{5,7},{6,2},{7,5},{8,12},{9,11},{10,... | collective-permute-start | bytes 393224 | tf_op jit(solution)/shard_map/ppermute | solution.py:27
  22.9 1.1 %collective-permute-done.9 = bf16[16,4096]{1,0:T(8,128)(2,1)S(1)} collective-permute-done((bf16[16,4096]{1,0:T(8,128)(2,1)}, bf16[16,4096]{1,0:T(8,128)(2,1)S(1)}, u32[]{:S(2)}, u32[]{:S(2)}) %collective-permute-start.9) | collective-permute-done | bytes 131104 | tf_op jit(solution)/shard_map/ppermute | solution.py:27
  24.0 1.6 %collective-permute-start.11 = (bf16[16,4096]{1,0:T(8,128)(2,1)S(1)}, bf16[16,4096]{1,0:T(8,128)(2,1)S(1)}, u32[]{:S(2)}, u32[]{:S(2)}) collective-permute-start(bf16[16,4096]{1,0:T(8,128)(2,1)S(1)} %collective-permute-done.9), channel_id=1, source_target_pairs={{0,4},{1,3},{2,6},{3,1},{4,0},{5,7},{6,2},{7,5},{8,12},{9,11},{10,... | collective-permute-start | bytes 393224 | tf_op jit(solution)/shard_map/ppermute | solution.py:27
  26.1 1.5 %collective-permute-done.5 = bf16[16,4096]{1,0:T(8,128)(2,1)} collective-permute-done((bf16[16,4096]{1,0:T(8,128)(2,1)S(1)}, bf16[16,4096]{1,0:T(8,128)(2,1)}, u32[]{:S(2)}, u32[]{:S(2)}) %collective-permute-start.5) | collective-permute-done | bytes 131104 | tf_op jit(solution)/shard_map/ppermute | solution.py:27
  27.6 2.8 %concatenate.41 = bf16[64,4096]{1,0:T(8,128)(2,1)S(1)} concatenate(bf16[4,4096]{1,0:T(4,128)(2,1)S(1)} %get-tuple-element.14, bf16[4,4096]{1,0:T(4,128)(2,1)S(1)} %get-tuple-element.15, bf16[8,4096]{1,0:T(8,128)(2,1)S(1)} %collective-permute-done.2, bf16[16,4096]{1,0:T(8,128)(2,1)} %copy-done, bf16[16,4096]{1,0:T(8,128)(2,1)} %collective-permute-done.4, ...), dimensions={0} | concatenate | bytes 1048576 | tf_op jit(solution)/shard_map/concatenate | solution.py:66
  30.9 0.8 %convolution_subtract_fusion.1 = f32[64,256]{1,0:T(8,128)S(1)} fusion(bf16[64,4096]{1,0:T(8,128)(2,1)S(1)} %concatenate.41, f32[64]{0:T(128)S(1)} %broadcast_multiply_fusion.1, bf16[128,4096]{1,0:T(8,128)(2,1)S(1)} %collective-permute-done.6, bf16[128,4096]{1,0:T(8,128)(2,1)S(1)} %get-tuple-element.4), kind=kOutput, calls=%fused_computation.2 | convolution fusion | flops 138428416 | bytes 2687232 | tf_op jit(solution)/shard_map/dot_general | solution.py:77
  31.6 0.8 %convolution_subtract_fusion = f32[64,256]{1,0:T(8,128)S(1)} fusion(bf16[64,4096]{1,0:T(8,128)(2,1)S(1)} %constant_dynamic-update-slice_fusion.2, f32[64]{0:T(128)S(1)} %broadcast_multiply_fusion, bf16[128,4096]{1,0:T(8,128)(2,1)S(1)} %collective-permute-done.6, bf16[128,4096]{1,0:T(8,128)(2,1)S(1)} %get-tuple-element.4), kind=kOutput, calls=%fused_computation.1 | convolution fusion | flops 138428416 | bytes 2687232 | tf_op jit(solution)/shard_map/dot_general | solution.py:77
  32.6 1.2 %collective-permute-done.12 = f32[128,256]{1,0:T(8,128)S(1)} collective-permute-done((f32[128,256]{1,0:T(8,128)S(1)}, f32[128,256]{1,0:T(8,128)S(1)}, u32[]{:S(2)}, u32[]{:S(2)}) %collective-permute-start.12) | collective-permute-done | bytes 131104 | tf_op jit(solution)/shard_map/ppermute | solution.py:27
  35.3 1.3 %collective-permute-start.19 = (bf16[16,4096]{1,0:T(8,128)(2,1)S(1)}, bf16[16,4096]{1,0:T(8,128)(2,1)S(1)}, u32[]{:S(2)}, u32[]{:S(2)}) collective-permute-start(bf16[16,4096]{1,0:T(8,128)(2,1)S(1)} %get-tuple-element.9), channel_id=1, source_target_pairs={{0,4},{1,3},{2,6},{3,1},{4,0},{5,7},{6,2},{7,5},{8,12},{9,11},{10,... | collective-permute-start | bytes 393224 | tf_op jit(solution)/shard_map/ppermute | solution.py:27
  37.0 0.9 %collective-permute-start.14 = (bf16[16,4096]{1,0:T(8,128)(2,1)S(1)}, bf16[16,4096]{1,0:T(8,128)(2,1)S(1)}, u32[]{:S(2)}, u32[]{:S(2)}) collective-permute-start(bf16[16,4096]{1,0:T(8,128)(2,1)S(1)} %get-tuple-element.7), channel_id=1, source_target_pairs={{0,4},{1,3},{2,6},{3,1},{4,0},{5,7},{6,2},{7,5},{8,12},{9,11},{10,... | collective-permute-start | bytes 393224 | tf_op jit(solution)/shard_map/ppermute | solution.py:27
  37.9 1.2 %collective-permute-start.13 = (bf16[16,4096]{1,0:T(8,128)(2,1)S(1)}, bf16[16,4096]{1,0:T(8,128)(2,1)S(1)}, u32[]{:S(2)}, u32[]{:S(2)}) collective-permute-start(bf16[16,4096]{1,0:T(8,128)(2,1)S(1)} %get-tuple-element.6), channel_id=1, source_target_pairs={{0,4},{1,3},{2,6},{3,1},{4,0},{5,7},{6,2},{7,5},{8,12},{9,11},{10,... | collective-permute-start | bytes 393224 | tf_op jit(solution)/shard_map/ppermute | solution.py:27
  39.1 0.8 %collective-permute-start.18 = (bf16[16,4096]{1,0:T(8,128)(2,1)S(1)}, bf16[16,4096]{1,0:T(8,128)(2,1)S(1)}, u32[]{:S(2)}, u32[]{:S(2)}) collective-permute-start(bf16[16,4096]{1,0:T(8,128)(2,1)S(1)} %get-tuple-element.8), channel_id=1, source_target_pairs={{0,4},{1,3},{2,6},{3,1},{4,0},{5,7},{6,2},{7,5},{8,12},{9,11},{10,... | collective-permute-start | bytes 393224 | tf_op jit(solution)/shard_map/ppermute | solution.py:27
  40.9 1.1 %collective-permute-done.14 = bf16[16,4096]{1,0:T(8,128)(2,1)S(1)} collective-permute-done((bf16[16,4096]{1,0:T(8,128)(2,1)S(1)}, bf16[16,4096]{1,0:T(8,128)(2,1)S(1)}, u32[]{:S(2)}, u32[]{:S(2)}) %collective-permute-start.14) | collective-permute-done | bytes 131104 | tf_op jit(solution)/shard_map/ppermute | solution.py:27
  42.7 4.7 %collective-permute-done.18 = bf16[16,4096]{1,0:T(8,128)(2,1)S(1)} collective-permute-done((bf16[16,4096]{1,0:T(8,128)(2,1)S(1)}, bf16[16,4096]{1,0:T(8,128)(2,1)S(1)}, u32[]{:S(2)}, u32[]{:S(2)}) %collective-permute-start.18) | collective-permute-done | bytes 131104 | tf_op jit(solution)/shard_map/ppermute | solution.py:27
  47.5 1.3 %collective-permute-start.21 = (f32[8,4096]{1,0:T(8,128)S(1)}, f32[8,4096]{1,0:T(8,128)S(1)}, u32[]{:S(2)}, u32[]{:S(2)}) collective-permute-start(f32[8,4096]{1,0:T(8,128)S(1)} %slice.125), channel_id=1, source_target_pairs={{0,8},{1,9},{2,10},{3,11},{4,12},{5,13},{6,14},{7,15},{8,0},{9,1},... | collective-permute-start | bytes 393224 | tf_op jit(solution)/shard_map/ppermute | solution.py:27
  48.8 0.8 %collective-permute-done.15 = f32[16,4096]{1,0:T(8,128)S(1)} collective-permute-done((f32[16,4096]{1,0:T(8,128)S(1)}, f32[16,4096]{1,0:T(8,128)S(1)}, u32[]{:S(2)}, u32[]{:S(2)}) %collective-permute-start.15) | collective-permute-done | bytes 262176 | tf_op jit(solution)/shard_map/ppermute | solution.py:27
  49.7 2.2 %collective-permute-start.16 = (bf16[8,4096]{1,0:T(8,128)(2,1)S(1)}, bf16[8,4096]{1,0:T(8,128)(2,1)S(1)}, u32[]{:S(2)}, u32[]{:S(2)}) collective-permute-start(bf16[8,4096]{1,0:T(8,128)(2,1)S(1)} %get-tuple-element.12), channel_id=1, source_target_pairs={{0,16},{1,17},{2,18},{3,19},{4,20},{5,21},{6,22},{7,23},{8,24},{9,... | collective-permute-start | bytes 196616 | tf_op jit(solution)/shard_map/ppermute | solution.py:27
  51.9 1.4 %collective-permute-start.17 = (bf16[8,4096]{1,0:T(8,128)(2,1)S(1)}, bf16[8,4096]{1,0:T(8,128)(2,1)S(1)}, u32[]{:S(2)}, u32[]{:S(2)}) collective-permute-start(bf16[8,4096]{1,0:T(8,128)(2,1)S(1)} %get-tuple-element.13), channel_id=1, source_target_pairs={{0,24},{1,25},{2,26},{3,27},{4,28},{5,29},{6,30},{7,31},{8,16},{9,... | collective-permute-start | bytes 196616 | tf_op jit(solution)/shard_map/ppermute | solution.py:27
  53.3 5.1 %collective-permute-done.16 = bf16[8,4096]{1,0:T(8,128)(2,1)S(1)} collective-permute-done((bf16[8,4096]{1,0:T(8,128)(2,1)S(1)}, bf16[8,4096]{1,0:T(8,128)(2,1)S(1)}, u32[]{:S(2)}, u32[]{:S(2)}) %collective-permute-start.16) | collective-permute-done | bytes 65568 | tf_op jit(solution)/shard_map/ppermute | solution.py:27
  59.1 0.7 %collective-permute-done.22 = f32[4,4096]{1,0:T(4,128)S(1)} collective-permute-done((f32[4,4096]{1,0:T(4,128)S(1)}, f32[4,4096]{1,0:T(4,128)S(1)}, u32[]{:S(2)}, u32[]{:S(2)}) %collective-permute-start.22) | collective-permute-done | bytes 65568 | tf_op jit(solution)/shard_map/ppermute | solution.py:27
  59.8 0.8 %reshape.107 = f32[2,2,8192]{2,1,0:T(2,128)} reshape(f32[4,8192]{1,0:T(4,128)S(1)} %pad_maximum_fusion.3) | data formatting | bytes 262144 | tf_op jit(solution)/shard_map/reshape | solution.py:143
  (73 shorter events, 7.7 us)
Async XLA Ops:
  1.5 3.3 %copy-start.1 = (bf16[128]{0:T(256)(128)(2,1)S(1)}, bf16[128]{0:T(256)(128)(2,1)}, u32[]{:S(2)}) copy-start(bf16[128]{0:T(256)(128)(2,1)} %param.6) | copy-start | bytes 772
  1.6 3.3 %copy-start.2 = (s32[128,1]{0,1:T(1,128)S(1)}, s32[128,1]{0,1:T(1,128)}, u32[]{:S(2)}) copy-start(s32[128,1]{0,1:T(1,128)} %param.5) | copy-start | bytes 1540
  1.6 3.8 %collective-permute-start.1 = (bf16[4,4096]{1,0:T(4,128)(2,1)S(1)}, bf16[4,4096]{1,0:T(4,128)(2,1)S(1)}, u32[]{:S(2)}, u32[]{:S(2)}) collective-permute-start(bf16[4,4096]{1,0:T(4,128)(2,1)S(1)} %broadcast_select_fusion.6), channel_id=1, source_target_pairs={{0,1},{1,0},{2,3},{3,2},{4,5},{5,4},{6,7},{7,6},{8,9},{9,8},{10,11... | collective-permute-start | bytes 98312 | tf_op jit(solution)/shard_map/ppermute | solution.py:27
  4.8 26.1 %collective-permute-start.6 = (bf16[128,4096]{1,0:T(8,128)(2,1)}, bf16[128,4096]{1,0:T(8,128)(2,1)S(1)}, u32[]{:S(2)}, u32[]{:S(2)}) collective-permute-start(bf16[128,4096]{1,0:T(8,128)(2,1)} %get-tuple-element.5), channel_id=1, source_target_pairs={{0,1},{1,0},{2,3},{3,2},{4,5},{5,4},{6,7},{7,6},{8,9},{9,8},{10,11... | collective-permute-start | bytes 3145736 | tf_op jit(solution)/shard_map/ppermute | solution.py:27
  4.9 14.4 %collective-permute-start = (f32[2,128]{1,0:T(2,128)S(1)}, f32[2,128]{1,0:T(2,128)S(1)}, u32[]{:S(2)}, u32[]{:S(2)}) collective-permute-start(f32[2,128]{1,0:T(2,128)S(1)} %pad_maximum_fusion.6), channel_id=1, source_target_pairs={{0,1},{1,0},{2,3},{3,2},{4,5},{5,4},{6,7},{7,6},{8,9},{9,8},{10,11... | collective-permute-start | bytes 3080 | tf_op jit(solution)/shard_map/ppermute | solution.py:27
  5.5 5.4 %collective-permute-start.2 = (bf16[8,4096]{1,0:T(8,128)(2,1)S(1)}, bf16[8,4096]{1,0:T(8,128)(2,1)S(1)}, u32[]{:S(2)}, u32[]{:S(2)}) collective-permute-start(bf16[8,4096]{1,0:T(8,128)(2,1)S(1)} %pad_maximum_fusion.4), channel_id=1, source_target_pairs={{0,8},{1,9},{2,10},{3,11},{4,12},{5,13},{6,14},{7,15},{8,0},{9,1},... | collective-permute-start | bytes 196616 | tf_op jit(solution)/shard_map/ppermute | solution.py:27
  8.2 7.0 %collective-permute-start.7 = (bf16[8,4096]{1,0:T(8,128)(2,1)S(1)}, bf16[8,4096]{1,0:T(8,128)(2,1)S(1)}, u32[]{:S(2)}, u32[]{:S(2)}) collective-permute-start(bf16[8,4096]{1,0:T(8,128)(2,1)S(1)} %pad_maximum_fusion.4), channel_id=1, source_target_pairs={{0,16},{1,17},{2,18},{3,19},{4,20},{5,21},{6,22},{7,23},{8,24},{9,... | collective-permute-start | bytes 196616 | tf_op jit(solution)/shard_map/ppermute | solution.py:27
  10.7 6.1 %collective-permute-start.8 = (bf16[8,4096]{1,0:T(8,128)(2,1)S(1)}, bf16[8,4096]{1,0:T(8,128)(2,1)S(1)}, u32[]{:S(2)}, u32[]{:S(2)}) collective-permute-start(bf16[8,4096]{1,0:T(8,128)(2,1)S(1)} %pad_maximum_fusion.4), channel_id=1, source_target_pairs={{0,24},{1,25},{2,26},{3,27},{4,28},{5,29},{6,30},{7,31},{8,16},{9,... | collective-permute-start | bytes 196616 | tf_op jit(solution)/shard_map/ppermute | solution.py:27
  10.9 10.5 %collective-permute-start.3 = (bf16[16,4096]{1,0:T(8,128)(2,1)S(1)}, bf16[16,4096]{1,0:T(8,128)(2,1)S(1)}, u32[]{:S(2)}, u32[]{:S(2)}) collective-permute-start(bf16[16,4096]{1,0:T(8,128)(2,1)S(1)} %pad_maximum_fusion.1), channel_id=1, source_target_pairs={{0,2},{1,5},{2,0},{3,7},{4,6},{5,1},{6,4},{7,3},{8,10},{9,13},{10,... | collective-permute-start | bytes 393224 | tf_op jit(solution)/shard_map/ppermute | solution.py:27
  17.5 6.5 %collective-permute-start.9 = (bf16[16,4096]{1,0:T(8,128)(2,1)}, bf16[16,4096]{1,0:T(8,128)(2,1)S(1)}, u32[]{:S(2)}, u32[]{:S(2)}) collective-permute-start(bf16[16,4096]{1,0:T(8,128)(2,1)} %get-tuple-element.16), channel_id=1, source_target_pairs={{0,2},{1,5},{2,0},{3,7},{4,6},{5,1},{6,4},{7,3},{8,10},{9,13},{10,... | collective-permute-start | bytes 393224 | tf_op jit(solution)/shard_map/ppermute | solution.py:27
  19.3 6.8 %collective-permute-start.4 = (bf16[16,4096]{1,0:T(8,128)(2,1)S(1)}, bf16[16,4096]{1,0:T(8,128)(2,1)}, u32[]{:S(2)}, u32[]{:S(2)}) collective-permute-start(bf16[16,4096]{1,0:T(8,128)(2,1)S(1)} %pad_maximum_fusion.1), channel_id=1, source_target_pairs={{0,4},{1,3},{2,6},{3,1},{4,0},{5,7},{6,2},{7,5},{8,12},{9,11},{10,... | collective-permute-start | bytes 393224 | tf_op jit(solution)/shard_map/ppermute | solution.py:27
  20.9 5.2 %collective-permute-start.10 = (bf16[16,4096]{1,0:T(8,128)(2,1)}, bf16[16,4096]{1,0:T(8,128)(2,1)S(1)}, u32[]{:S(2)}, u32[]{:S(2)}) collective-permute-start(bf16[16,4096]{1,0:T(8,128)(2,1)} %get-tuple-element.16), channel_id=1, source_target_pairs={{0,4},{1,3},{2,6},{3,1},{4,0},{5,7},{6,2},{7,5},{8,12},{9,11},{10,... | collective-permute-start | bytes 393224 | tf_op jit(solution)/shard_map/ppermute | solution.py:27
  21.4 4.7 %copy-start = (bf16[16,4096]{1,0:T(8,128)(2,1)}, bf16[16,4096]{1,0:T(8,128)(2,1)S(1)}, u32[]{:S(2)}) copy-start(bf16[16,4096]{1,0:T(8,128)(2,1)S(1)} %collective-permute-done.3) | copy-start | bytes 393220
  21.4 6.2 %collective-permute-start.5 = (bf16[16,4096]{1,0:T(8,128)(2,1)S(1)}, bf16[16,4096]{1,0:T(8,128)(2,1)}, u32[]{:S(2)}, u32[]{:S(2)}) collective-permute-start(bf16[16,4096]{1,0:T(8,128)(2,1)S(1)} %collective-permute-done.3), channel_id=1, source_target_pairs={{0,4},{1,3},{2,6},{3,1},{4,0},{5,7},{6,2},{7,5},{8,12},{9,11},{10,... | collective-permute-start | bytes 393224 | tf_op jit(solution)/shard_map/ppermute | solution.py:27
  24.0 6.6 %collective-permute-start.11 = (bf16[16,4096]{1,0:T(8,128)(2,1)S(1)}, bf16[16,4096]{1,0:T(8,128)(2,1)S(1)}, u32[]{:S(2)}, u32[]{:S(2)}) collective-permute-start(bf16[16,4096]{1,0:T(8,128)(2,1)S(1)} %collective-permute-done.9), channel_id=1, source_target_pairs={{0,4},{1,3},{2,6},{3,1},{4,0},{5,7},{6,2},{7,5},{8,12},{9,11},{10,... | collective-permute-start | bytes 393224 | tf_op jit(solution)/shard_map/ppermute | solution.py:27
  32.4 1.4 %collective-permute-start.12 = (f32[128,256]{1,0:T(8,128)S(1)}, f32[128,256]{1,0:T(8,128)S(1)}, u32[]{:S(2)}, u32[]{:S(2)}) collective-permute-start(f32[128,256]{1,0:T(8,128)S(1)} %pad_maximum_fusion.2), channel_id=1, source_target_pairs={{0,1},{1,0},{2,3},{3,2},{4,5},{5,4},{6,7},{7,6},{8,9},{9,8},{10,11... | collective-permute-start | bytes 393224 | tf_op jit(solution)/shard_map/ppermute | solution.py:27
  35.3 5.0 %collective-permute-start.19 = (bf16[16,4096]{1,0:T(8,128)(2,1)S(1)}, bf16[16,4096]{1,0:T(8,128)(2,1)S(1)}, u32[]{:S(2)}, u32[]{:S(2)}) collective-permute-start(bf16[16,4096]{1,0:T(8,128)(2,1)S(1)} %get-tuple-element.9), channel_id=1, source_target_pairs={{0,4},{1,3},{2,6},{3,1},{4,0},{5,7},{6,2},{7,5},{8,12},{9,11},{10,... | collective-permute-start | bytes 393224 | tf_op jit(solution)/shard_map/ppermute | solution.py:27
  37.0 5.0 %collective-permute-start.14 = (bf16[16,4096]{1,0:T(8,128)(2,1)S(1)}, bf16[16,4096]{1,0:T(8,128)(2,1)S(1)}, u32[]{:S(2)}, u32[]{:S(2)}) collective-permute-start(bf16[16,4096]{1,0:T(8,128)(2,1)S(1)} %get-tuple-element.7), channel_id=1, source_target_pairs={{0,4},{1,3},{2,6},{3,1},{4,0},{5,7},{6,2},{7,5},{8,12},{9,11},{10,... | collective-permute-start | bytes 393224 | tf_op jit(solution)/shard_map/ppermute | solution.py:27
  37.9 10.9 %collective-permute-start.13 = (bf16[16,4096]{1,0:T(8,128)(2,1)S(1)}, bf16[16,4096]{1,0:T(8,128)(2,1)S(1)}, u32[]{:S(2)}, u32[]{:S(2)}) collective-permute-start(bf16[16,4096]{1,0:T(8,128)(2,1)S(1)} %get-tuple-element.6), channel_id=1, source_target_pairs={{0,4},{1,3},{2,6},{3,1},{4,0},{5,7},{6,2},{7,5},{8,12},{9,11},{10,... | collective-permute-start | bytes 393224 | tf_op jit(solution)/shard_map/ppermute | solution.py:27
  39.1 8.3 %collective-permute-start.18 = (bf16[16,4096]{1,0:T(8,128)(2,1)S(1)}, bf16[16,4096]{1,0:T(8,128)(2,1)S(1)}, u32[]{:S(2)}, u32[]{:S(2)}) collective-permute-start(bf16[16,4096]{1,0:T(8,128)(2,1)S(1)} %get-tuple-element.8), channel_id=1, source_target_pairs={{0,4},{1,3},{2,6},{3,1},{4,0},{5,7},{6,2},{7,5},{8,12},{9,11},{10,... | collective-permute-start | bytes 393224 | tf_op jit(solution)/shard_map/ppermute | solution.py:27
  40.3 7.1 %collective-permute-start.20 = (f32[16,4096]{1,0:T(8,128)S(1)}, f32[16,4096]{1,0:T(8,128)S(1)}, u32[]{:S(2)}, u32[]{:S(2)}) collective-permute-start(f32[16,4096]{1,0:T(8,128)S(1)} %slice_add_fusion), channel_id=1, source_target_pairs={{0,2},{1,5},{2,0},{3,7},{4,6},{5,1},{6,4},{7,3},{8,10},{9,13},{10,... | collective-permute-start | bytes 786440 | tf_op jit(solution)/shard_map/ppermute | solution.py:27
  42.1 7.5 %collective-permute-start.15 = (f32[16,4096]{1,0:T(8,128)S(1)}, f32[16,4096]{1,0:T(8,128)S(1)}, u32[]{:S(2)}, u32[]{:S(2)}) collective-permute-start(f32[16,4096]{1,0:T(8,128)S(1)} %slice_add_fusion.2), channel_id=1, source_target_pairs={{0,2},{1,5},{2,0},{3,7},{4,6},{5,1},{6,4},{7,3},{8,10},{9,13},{10,... | collective-permute-start | bytes 786440 | tf_op jit(solution)/shard_map/ppermute | solution.py:27
  47.5 10.9 %collective-permute-start.21 = (f32[8,4096]{1,0:T(8,128)S(1)}, f32[8,4096]{1,0:T(8,128)S(1)}, u32[]{:S(2)}, u32[]{:S(2)}) collective-permute-start(f32[8,4096]{1,0:T(8,128)S(1)} %slice.125), channel_id=1, source_target_pairs={{0,8},{1,9},{2,10},{3,11},{4,12},{5,13},{6,14},{7,15},{8,0},{9,1},... | collective-permute-start | bytes 393224 | tf_op jit(solution)/shard_map/ppermute | solution.py:27
  49.7 8.7 %collective-permute-start.16 = (bf16[8,4096]{1,0:T(8,128)(2,1)S(1)}, bf16[8,4096]{1,0:T(8,128)(2,1)S(1)}, u32[]{:S(2)}, u32[]{:S(2)}) collective-permute-start(bf16[8,4096]{1,0:T(8,128)(2,1)S(1)} %get-tuple-element.12), channel_id=1, source_target_pairs={{0,16},{1,17},{2,18},{3,19},{4,20},{5,21},{6,22},{7,23},{8,24},{9,... | collective-permute-start | bytes 196616 | tf_op jit(solution)/shard_map/ppermute | solution.py:27
  51.9 6.5 %collective-permute-start.17 = (bf16[8,4096]{1,0:T(8,128)(2,1)S(1)}, bf16[8,4096]{1,0:T(8,128)(2,1)S(1)}, u32[]{:S(2)}, u32[]{:S(2)}) collective-permute-start(bf16[8,4096]{1,0:T(8,128)(2,1)S(1)} %get-tuple-element.13), channel_id=1, source_target_pairs={{0,24},{1,25},{2,26},{3,27},{4,28},{5,29},{6,30},{7,31},{8,16},{9,... | collective-permute-start | bytes 196616 | tf_op jit(solution)/shard_map/ppermute | solution.py:27
  58.5 1.3 %collective-permute-start.22 = (f32[4,4096]{1,0:T(4,128)S(1)}, f32[4,4096]{1,0:T(4,128)S(1)}, u32[]{:S(2)}, u32[]{:S(2)}) collective-permute-start(f32[4,4096]{1,0:T(4,128)S(1)} %slice_select_fusion), channel_id=1, source_target_pairs={{0,1},{1,0},{2,3},{3,2},{4,5},{5,4},{6,7},{7,6},{8,9},{9,8},{10,11... | collective-permute-start | bytes 196616 | tf_op jit(solution)/shard_map/ppermute | solution.py:27

commit v3 on v1

v3 whole, which is shorter than its diff:
```python
import functools
import math

import jax
import jax.numpy as jnp
from jax import lax
from jax.experimental import pallas as pl
from jax.experimental.pallas import tpu as pltpu
from jax.sharding import PartitionSpec as P

AXES = ("cls", "dom")
CORE = 1
FLOAT, SHORT = jnp.float32, jnp.bfloat16
NT = (((1,), (1,)), ((), ()))
COSTS = {"score": [(1 << 28, 1 << 21)] * 2, "softmax": (1 << 28, 1 << 22), "weigh": (1 << 28, 1 << 22), "near": (1 << 20, 1 << 16), "sum": (1 << 31, 1 << 16)}


def plan(mesh):
    owners, dom = mesh.shape["cls"], mesh.shape["dom"]
    plane_bits = (dom // 2).bit_length() - 1
    masks = [2 << bit for bit in range(plane_bits)]
    if plane_bits % 2:
        return owners, dom, (masks, masks), False
    low, high = masks[: plane_bits // 2], masks[plane_bits // 2 :]
    return owners, dom, (low + high, high + low), True


def call(body, outs, cost, *args, smem=()):
    spaces = [
        pl.BlockSpec(memory_space=pltpu.SMEM if i in smem else pltpu.VMEM) for i in range(len(args))
    ]
    out_shape = [jax.ShapeDtypeStruct(shape, kind) for shape, kind in outs]
    held = sum(math.prod(array.shape) * array.dtype.itemsize for array in [*args, *out_shape])
    return pl.pallas_call(
        body,
        out_shape=out_shape,
        in_specs=spaces,
        out_specs=[pl.BlockSpec(memory_space=pltpu.VMEM)] * len(outs),
        compiler_params=pltpu.CompilerParams(vmem_limit_bytes=min(held + (8 << 20), 56 << 20)),
        cost_estimate=pl.CostEstimate(flops=cost[0], bytes_accessed=cost[1], transcendentals=0),
    )(*args)


def by_core(core, body):
    @pl.when(core[0] == 0)
    def _():
        body(0)

    @pl.when(core[0] != 0)
    def _():
        body(1)


def copy_body(source, out):
    out[...] = source[...]


def block_body(core, mine, theirs, out):
    quarter = out.shape[2]

    def fill(c):
        pair = (theirs, mine) if c else (mine, theirs)
        for ch in range(2):
            lo = (2 * c + ch) * quarter
            rows = [
                ref[k, :, lo : lo + quarter].astype(FLOAT) for ref in pair for k in range(ref.shape[0])
            ]
            rows = jnp.concatenate(rows, axis=0)
            out[0, ch * rows.shape[0] : (ch + 1) * rows.shape[0]] = rows.astype(SHORT)

    by_core(core, fill)


def sum_body(*refs):
    *parts, out = refs
    total = parts[0][...].astype(FLOAT)
    for part in parts[1:]:
        total += part[...].astype(FLOAT)
    out[...] = total


def near_body(*refs):
    count = sum(1 for ref in refs if ref.shape != refs[0].shape)
    parts, outs = refs[:-count], refs[-count:]
    at = 0
    for out in outs:
        total = 0.0
        for part in parts:
            total += part[at : at + out.shape[0]].astype(FLOAT)
        out[...] = total
        at += out.shape[0]


def total_body(core, *refs):
    *parts, kept, sent = refs
    rows = kept.shape[1]
    total = parts[0][0].astype(FLOAT)
    for part in parts[1:]:
        total += part[0].astype(FLOAT)

    def fill(c):
        for ch in range(2):
            at = 2 * ch * rows
            kept[ch] = total[at + c * rows : at + (c + 1) * rows]
            sent[ch] = total[at + (1 - c) * rows : at + (2 - c) * rows]

    by_core(core, fill)


def final_body(core, kept, got, out):
    quarter, (classes, own) = kept.shape[2], out.shape[:2]

    def fill(c):
        for j, part in ((c, kept), (1 - c, got)):
            for ch in range(2):
                lo = (2 * j + ch) * quarter
                for k in range(classes):
                    out[k, :, lo : lo + quarter] = part[ch, k * own : (k + 1) * own]

    by_core(core, fill)


def score_body(count, *refs):
    core, images, other, out = refs[count:]
    quarter = refs[0].shape[2]
    rows = jnp.concatenate([ref[...].reshape(-1, quarter) for ref in refs[:count]], axis=0)
    blocks = rows.shape[0] // 16
    wide = rows.astype(FLOAT)
    norms = jnp.sum(wide * wide, axis=1, keepdims=True).reshape(blocks, 16, 1)
    norms = 0.5 * (norms[:, :8] + norms[:, 8:]).reshape(blocks * 8, 1)
    local = images.shape[0]

    def fill(c):
        for j, (part, at) in enumerate(((images, 2 * c * quarter), (other, 0))):
            sums = 0.0
            for ch in range(2):
                chunk = part[:, at + ch * quarter : at + (ch + 1) * quarter]
                scores = lax.dot_general(rows, chunk, NT, preferred_element_type=FLOAT)
                sums += scores.reshape(blocks, 16, local)[:, ch * 8 : ch * 8 + 8]
            out[:, j * local : (j + 1) * local] = sums.reshape(blocks * 8, local) - norms

    by_core(core, fill)


def score(pieces, core, images, other, cost):
    blocks = sum(piece.shape[0] for piece in pieces)
    return call(
        functools.partial(score_body, len(pieces)),
        [((blocks * 8, 2 * images.shape[0]), FLOAT)],
        cost,
        *pieces,
        core,
        images,
        other,
        smem=(len(pieces),),
    )[0]


def weigh_rows(weights, core, images, other, outs):
    quarter = outs[0].shape[2]
    blocks = weights.shape[0] // 8
    step = 512
    offset = pl.multiple_of(core[0] * (2 * quarter), 128)
    for begin in range(0, quarter, step):
        halves = []
        for lo in (begin, quarter + begin):
            chunk = jnp.concatenate(
                [images[:, pl.ds(offset + lo, step)], other[:, lo : lo + step]], axis=0
            )
            sums = jnp.dot(weights, chunk, preferred_element_type=FLOAT)
            halves.append(sums.reshape(blocks, 8, step))
        at = 0
        for out in outs:
            count = out.shape[0]
            both = [sums[at : at + count] for sums in halves]
            out[:, :, begin : begin + step] = jnp.concatenate(both, axis=1).astype(out.dtype)
            at += count


def weigh_body(weights, core, images, other, *outs):
    weigh_rows(weights[...], core, images, other, outs)


def softmax_body(order, leave, cut, count, *refs):
    mine, theirs = (
        jnp.concatenate([ref[...] for ref in part], axis=0)
        for part in (refs[:count], refs[count : 2 * count])
    )
    precision, named_class, kind, core, images, other = refs[2 * count : 2 * count + 6]
    weights_near, evidence, *outs = refs[2 * count + 6 :]
    local = images.shape[0]
    theirs = jnp.concatenate([theirs[lo:hi] for lo, hi in order], axis=0)
    theirs = jnp.concatenate([theirs[:, local:], theirs[:, :local]], axis=1)
    scores = precision[...] * (mine + theirs)
    named = kind[...] == named_class[...]
    largest = jnp.max(jnp.where(named, scores, -jnp.inf), axis=0, keepdims=True)
    exponent = jnp.where(named, jnp.exp(jnp.where(named, scores - largest, 0.0)), 0.0)
    totals = jnp.sum(exponent, axis=0, keepdims=True)
    weights = exponent / totals
    weights = jnp.concatenate([weights[lo:hi] for lo, hi in leave], axis=0).astype(SHORT)
    evidence[...] = largest + jnp.log(totals)
    weights_near[...] = weights[:cut]
    weigh_rows(weights[cut:], core, images, other, outs)


def part_body(core, images, sent):
    half = sent.shape[1]

    def fill(c):
        sent[...] = images[:, (1 - c) * half : (2 - c) * half]

    by_core(core, fill)


def solution(mesh):
    owners, dom, orders, crossed = plan(mesh)
    devices = owners * dom
    steps = len(orders[0])
    near_count = max(owners // 2, 1)
    groups = [range(0, near_count)] + ([range(near_count, owners)] if owners > 1 else [])

    def swap(value, masks, name):
        pairs = [(i, i ^ masks[i % 2]) for i in range(devices)]
        with jax.named_scope(name):
            return lax.ppermute(value, AXES, pairs)

    def swap_core(value, name):
        return swap(value, (CORE, CORE), "core_" + name)

    def swap_plane(value, step, name):
        return swap(value, (orders[0][step], orders[1][step]), f"plane{step}_{name}")

    def swap_cls(value, k, name):
        return swap(value, (k * dom, k * dom), f"cls{k}_{name}")

    def on_device(particles, assign, inv_sigma, projections):
        local, width = particles.shape
        half, quarter = width // 2, width // 4
        per_owner, own = projections.shape[:2]
        mine_rows = per_owner * own
        size = 2 * mine_rows
        core = lax.axis_index("dom") % 2
        where = core.astype(jnp.int32)[None]

        got = swap_core(projections, "rows")
        rows = call(
            copy_body, [(projections.shape, SHORT)], (0, 4 * mine_rows * width), projections
        )[0]
        block = call(
            block_body,
            [((1, 2 * size, quarter), SHORT)],
            (0, 3 * size * half),
            where,
            rows,
            got,
            smem=(0,),
        )[0]
        pieces = {k: swap_cls(block, k, "rows") for k in range(1, owners)}
        pieces[0] = block

        def spread(held, name):
            older, newer = [held], []
            for step in range(steps):
                sets = [part for part in (older, newer) if part]
                got = [
                    swap_plane(jnp.concatenate(part, axis=0), step, f"{name}{i}")
                    for i, part in enumerate(sets)
                ]
                older, newer = older + newer, got
            return older + newer

        gathered = [
            spread(jnp.concatenate([pieces[k] for k in g], axis=0), f"rows{i}")
            for i, g in enumerate(groups)
        ]

        late, late_assign, late_sigma, _ = lax.optimization_barrier(
            (particles, assign, inv_sigma, got)
        )
        side = jnp.stack([late_sigma.astype(FLOAT), late_assign[:, 0].astype(FLOAT)])
        side = jnp.concatenate([side, swap_core(side, "side")], axis=1)
        precision, class_id = side[:1], side[1:].astype(jnp.int32)
        sent = call(
            part_body, [((local, half), SHORT)], (0, 4 * local * half), where, late, smem=(0,)
        )[0]
        other = swap_core(sent, "images")

        partial = [score(gathered[0], where, particles, other, COSTS["score"][0])]
        others = [swap_core(partial[0], "scores0")]
        if len(gathered) > 1:
            gathered[1][-1], others[0] = lax.optimization_barrier((gathered[1][-1], others[0]))
            partial.append(score(gathered[1], where, particles, other, COSTS["score"][1]))
            others.append(swap_core(partial[1], "scores1"))
        rows_far = partial[0].shape[0]
        rows = rows_far * len(groups)

        positions = 1 << steps
        each = rows_far // positions
        side_len = 1 << (steps // 2)
        order = []
        for g in range(len(groups)):
            for p in range(positions):
                q = p % side_len * side_len + p // side_len if crossed else p
                begin = g * rows_far + q * each
                order.append((begin, begin + each))

        z = lax.axis_index("cls") ^ jnp.arange(owners, dtype=jnp.int32)
        kind = z[:, None] * per_owner + jnp.arange(per_owner, dtype=jnp.int32)[None, :]
        kind = jnp.broadcast_to(
            kind.reshape(len(groups), 1, -1, 1, per_owner, 1),
            (len(groups), positions, owners // len(groups), 2, per_owner, own),
        ).reshape(rows, 1)

        stays, goes = [], []
        unit = each // near_count
        for p in range(positions):
            stays.append((p * each, p * each + unit))
        for j in range(1, near_count):
            goes += [(p * each + j * unit, p * each + (j + 1) * unit) for p in range(positions)]
        specs_stay = [((positions, 2 * size, quarter), FLOAT)]
        specs_go = [((positions, 2 * size, quarter), SHORT)] * (near_count - 1)
        keeps = 2 if steps > 1 else 1
        if owners > 1:
            stays.append((rows_far, rows_far + rows_far // 2))
            goes.append((rows_far + rows_far // 2, rows))
            count = rows_far // size // (2 * keeps)
            specs_stay += [((count, 2 * size, quarter), FLOAT)] * keeps
            specs_go += [((count, 2 * size, quarter), SHORT)] * keeps
        cut = sum(hi - lo for lo, hi in stays)
        weights, evidence, *sends = call(
            functools.partial(softmax_body, order, stays + goes, cut, len(partial)),
            [((cut, 2 * local), SHORT), ((1, 2 * local), FLOAT)] + specs_go,
            COSTS["softmax"],
            *partial,
            *others,
            precision,
            class_id,
            kind,
            where,
            particles,
            other,
            smem=(2 * len(partial) + 3,),
        )
        held, *kept = call(
            weigh_body, specs_stay, COSTS["weigh"], weights, where, particles, other, smem=(1,)
        )

        ends = []
        if owners > 1:
            far = sends[near_count - 1 :]
            fresh = [swap_plane(far[i], steps - 1, f"far{i}") for i in range(keeps)[::-1]][::-1]
            kept = [part + new.astype(FLOAT) for part, new in zip(kept, fresh, strict=True)]
            for step in range(steps - 2, -1, -1):
                stay, send = kept
                if step == steps - 2:
                    send = send.astype(SHORT)
                if step == 0:
                    kept = [stay + swap_plane(send, step, "far").astype(FLOAT)]
                    continue
                n = stay.shape[0] // 2
                away = stay[n:] + swap_plane(send[n:], step, "far1").astype(FLOAT)
                kept = [stay[:n] + swap_plane(send[:n], step, "far0").astype(FLOAT), away]
            for j, k in enumerate(groups[1]):
                ends.append(swap_cls(kept[0][j : j + 1].astype(SHORT), k, "far"))
            ends = call(sum_body, [((1, 2 * size, quarter), FLOAT)], COSTS["sum"], *ends)
        near = [swap_cls(part, k, "near") for k, part in enumerate(sends[: near_count - 1], 1)]
        pieces = [((1, 2 * size, quarter), FLOAT)] * positions
        held = call(near_body, pieces, COSTS["near"], held, *near)
        ends = [held[0], *ends]
        for q in range(positions - 1, 0, -1):
            masks = [
                functools.reduce(int.__xor__, [m for s, m in enumerate(way) if q >> s & 1])
                for way in orders
            ]
            ends.append(swap(held[q], masks, f"plane_own{q}"))
        kept, sent = call(
            total_body,
            [((2, mine_rows, quarter), FLOAT)] * 2,
            (0, 8 * size * half),
            where,
            *ends,
            smem=(0,),
        )
        got = swap_core(sent, "sums")
        class_sums = call(
            final_body,
            [((per_owner, own, width), FLOAT)],
            (0, 8 * mine_rows * width),
            where,
            kept,
            got,
            smem=(0,),
        )[0]
        return class_sums, evidence[0, :local]

    return jax.shard_map(
        on_device,
        mesh=mesh,
        in_specs=(
            P(("cls", "dom"), None),
            P(("cls", "dom"), None),
            P(("cls", "dom")),
            P("cls", "dom", None),
        ),
        out_specs=(P("cls", "dom", None), P(("cls", "dom"))),
        check_vma=False,
    )
```

time: 74.2 us -> 53.1 us (0.72)
  waiting for transfers between devices: 40.6 us -> 17.8 us
  starting transfers between devices: 16.6 us -> 27.2 us
  matrix products: 9.33 us -> 0 us
  Pallas kernels: 0 us -> 3.71 us
  other arithmetic: 3.2 us -> 0.21 us
    ppermute x15 -> x24, waiting for transfers between devices: 40.6 us -> 17.8 us  [swap(): return lax.ppermute(value, AXES, pairs)]
    ppermute x15 -> x24, starting transfers between devices: 16.6 us -> 27.2 us  [swap(): return lax.ppermute(value, AXES, pairs)]
    dot_general x5 -> x0, matrix products: 9.33 us -> none  [the longest x3 5.91 us: score(): lax.dot_general(rows, images, (((1,), (1,)), ((), ())), preferred_element...]
    pallas_call x0 -> x11, Pallas kernels: none -> 3.71 us  [call(): pl.pallas_call(body, out_shape=out_shape, in_specs=spaces, out_specs=[pl....]
    unnamed x4 -> x11, local copies, waits for them, and re-layouts: 0.01 us -> 2.45 us
    select_n x5 -> x0, other arithmetic: 1.79 us -> none  [the longest x2 1.7 us: halves_of(): return (jnp.where(first, low, high), jnp.where(first, high, low))]
    reshape x3 -> x1, local copies, waits for them, and re-layouts: 1.7 us -> 0.1 us  [on_device(): kind = jnp.broadcast_to(kind.reshape(len(groups), 1, -1, 1, per_owner, 1)...]
    reduce_sum x4 -> x0, other arithmetic: 0.77 us -> none  [the longest x3 0.55 us: score(): norms = 0.5 * jnp.sum(jnp.square(rows.astype(jnp.float32)), axis=1)]
  transfers between devices with their start and end apart: 15 -> 24, of which waited for: 11 -> 11; matrix products, arithmetic and copies ran while one was open for 5% -> 2% of each run, Pallas kernels for 0% -> 3%
where the time goes in v3:
time: 53.1 us; the launch traced here: 52.9 us
  starting transfers between devices  27.2 us (51%)
  waiting for transfers between devices  17.8 us (34%)
  Pallas kernels  3.71 us (7%)
  local copies, waits for them, and re-layouts  3.16 us (6%)
  between operations  0.85 us (2%)
    ppermute x24, starting transfers between devices, swap(): return lax.ppermute(value, AXES, pairs)  27.2 us
    ppermute x24, waiting for transfers between devices, swap(): return lax.ppermute(value, AXES, pairs)  17.8 us
    pallas_call x11, Pallas kernels, call(): pl.pallas_call(body, out_shape=out_shape, in_specs=spaces, out_specs=[pl....  3.71 us
    unnamed x11, local copies, waits for them, and re-layouts  2.45 us
  transfers between devices with their start and end apart: 24, of which 11 were waited for; matrix products, arithmetic and copies ran while one was open for 2% of the time, Pallas kernels for 3%

profile of v3, /device:TPU:0, one launch (start us, length us, event | category | flops | bytes accessed | tf_op | source)
XLA Modules:
  0.0 52.9 jit_solution(15242379741237220207)
XLA Ops:
  1.3 0.8 %copy-done.2 = bf16[2,2,8192]{2,1,0:T(2,128)(2,1)S(1)} copy-done((bf16[2,2,8192]{2,1,0:T(2,128)(2,1)S(1)}, bf16[2,2,8192]{2,1,0:T(2,128)(2,1)}, u32[]{:S(2)}) %copy-start.2) | copy-done | bytes 65560
  2.3 3.0 %collective-permute-start.1 = (bf16[1,16,2048]{2,1,0:T(8,128)(2,1)S(1)}, bf16[1,16,2048]{2,1,0:T(8,128)(2,1)S(1)}, u32[]{:S(2)}, u32[]{:S(2)}) collective-permute-start(bf16[1,16,2048]{2,1,0:T(8,128)(2,1)S(1)} %shard_map.60), channel_id=1, source_target_pairs={{0,8},{1,9},{2,10},{3,11},{4,12},{5,13},{6,14},{7,15},{8,0},{9,1},... | collective-permute-start | bytes 196616 | tf_op jit(solution)/shard_map/cls1_rows/ppermute | solution.py:225
  5.3 2.6 %collective-permute-start.6 = (bf16[1,16,2048]{2,1,0:T(8,128)(2,1)S(1)}, bf16[1,16,2048]{2,1,0:T(8,128)(2,1)S(1)}, u32[]{:S(2)}, u32[]{:S(2)}) collective-permute-start(bf16[1,16,2048]{2,1,0:T(8,128)(2,1)S(1)} %shard_map.60), channel_id=1, source_target_pairs={{0,16},{1,17},{2,18},{3,19},{4,20},{5,21},{6,22},{7,23},{8,24},{9,... | collective-permute-start | bytes 196616 | tf_op jit(solution)/shard_map/cls2_rows/ppermute | solution.py:225
  7.9 1.6 %copy-done = bf16[128,8192]{1,0:T(8,128)(2,1)S(1)} copy-done((bf16[128,8192]{1,0:T(8,128)(2,1)S(1)}, bf16[128,8192]{1,0:T(8,128)(2,1)}, u32[]{:S(2)}) %copy-start) | copy-done | bytes 2097176
  9.7 1.8 %collective-permute-start.2 = (bf16[2,16,2048]{2,1,0:T(8,128)(2,1)S(1)}, bf16[2,16,2048]{2,1,0:T(8,128)(2,1)S(1)}, u32[]{:S(2)}, u32[]{:S(2)}) collective-permute-start(bf16[2,16,2048]{2,1,0:T(8,128)(2,1)S(1)} %pad_maximum_fusion.refs_0_), channel_id=1, source_target_pairs={{0,2},{1,5},{2,0},{3,7},{4,6},{5,1},{6,4},{7,3},{8,10},{9,13},{10,... | collective-permute-start | bytes 393224 | tf_op jit(solution)/shard_map/plane0_rows00/ppermute | solution.py:225
  11.5 1.5 %collective-permute-start.3 = (bf16[2,16,2048]{2,1,0:T(8,128)(2,1)S(1)}, bf16[2,16,2048]{2,1,0:T(8,128)(2,1)S(1)}, u32[]{:S(2)}, u32[]{:S(2)}) collective-permute-start(bf16[2,16,2048]{2,1,0:T(8,128)(2,1)S(1)} %pad_maximum_fusion.refs_0_), channel_id=1, source_target_pairs={{0,4},{1,3},{2,6},{3,1},{4,0},{5,7},{6,2},{7,5},{8,12},{9,11},{10,... | collective-permute-start | bytes 393224 | tf_op jit(solution)/shard_map/plane1_rows00/ppermute | solution.py:225
  13.0 1.1 %collective-permute-done.7 = bf16[1,16,2048]{2,1,0:T(8,128)(2,1)S(1)} collective-permute-done((bf16[1,16,2048]{2,1,0:T(8,128)(2,1)S(1)}, bf16[1,16,2048]{2,1,0:T(8,128)(2,1)S(1)}, u32[]{:S(2)}, u32[]{:S(2)}) %collective-permute-start.7) | collective-permute-done | bytes 65568 | tf_op jit(solution)/shard_map/cls3_rows/ppermute | solution.py:225
  14.1 1.5 %collective-permute-start.8 = (bf16[2,16,2048]{2,1,0:T(8,128)(2,1)S(1)}, bf16[2,16,2048]{2,1,0:T(8,128)(2,1)S(1)}, u32[]{:S(2)}, u32[]{:S(2)}) collective-permute-start(bf16[2,16,2048]{2,1,0:T(8,128)(2,1)S(1)} %constant_dynamic-update-slice_fusion.refs_0_), channel_id=1, source_target_pairs={{0,2},{1,5},{2,0},{3,7},{4,6},{5,1},{6,4},{7,3},{8,10},{9,13},{10,... | collective-permute-start | bytes 393224 | tf_op jit(solution)/shard_map/plane0_rows10/ppermute | solution.py:225
  15.6 1.9 %collective-permute-start.4 = (bf16[2,16,2048]{2,1,0:T(8,128)(2,1)S(1)}, bf16[2,16,2048]{2,1,0:T(8,128)(2,1)S(1)}, u32[]{:S(2)}, u32[]{:S(2)}) collective-permute-start(bf16[2,16,2048]{2,1,0:T(8,128)(2,1)S(1)} %collective-permute-done.2.refs_1_), channel_id=1, source_target_pairs={{0,4},{1,3},{2,6},{3,1},{4,0},{5,7},{6,2},{7,5},{8,12},{9,11},{10,... | collective-permute-start | bytes 393224 | tf_op jit(solution)/shard_map/plane1_rows01/ppermute | solution.py:225
  17.6 1.7 %collective-permute-start.9 = (bf16[2,16,2048]{2,1,0:T(8,128)(2,1)S(1)}, bf16[2,16,2048]{2,1,0:T(8,128)(2,1)S(1)}, u32[]{:S(2)}, u32[]{:S(2)}) collective-permute-start(bf16[2,16,2048]{2,1,0:T(8,128)(2,1)S(1)} %constant_dynamic-update-slice_fusion.refs_0_), channel_id=1, source_target_pairs={{0,4},{1,3},{2,6},{3,1},{4,0},{5,7},{6,2},{7,5},{8,12},{9,11},{10,... | collective-permute-start | bytes 393224 | tf_op jit(solution)/shard_map/plane1_rows10/ppermute | solution.py:225
  19.3 1.0 %collective-permute-done.8.refs_1_ = bf16[2,16,2048]{2,1,0:T(8,128)(2,1)S(1)} collective-permute-done((bf16[2,16,2048]{2,1,0:T(8,128)(2,1)S(1)}, bf16[2,16,2048]{2,1,0:T(8,128)(2,1)S(1)}, u32[]{:S(2)}, u32[]{:S(2)}) %collective-permute-start.8) | collective-permute-done | bytes 131104 | tf_op jit(solution)/shard_map/plane0_rows10/ppermute | solution.py:225
  20.4 1.6 %collective-permute-start.10 = (bf16[2,16,2048]{2,1,0:T(8,128)(2,1)S(1)}, bf16[2,16,2048]{2,1,0:T(8,128)(2,1)S(1)}, u32[]{:S(2)}, u32[]{:S(2)}) collective-permute-start(bf16[2,16,2048]{2,1,0:T(8,128)(2,1)S(1)} %collective-permute-done.8.refs_1_), channel_id=1, source_target_pairs={{0,4},{1,3},{2,6},{3,1},{4,0},{5,7},{6,2},{7,5},{8,12},{9,11},{10,... | collective-permute-start | bytes 393224 | tf_op jit(solution)/shard_map/plane1_rows11/ppermute | solution.py:225
  22.0 0.8 %shard_map.62.refs_0_ = f32[64,256]{1,0:T(8,128)S(1)} custom-call(bf16[2,16,2048]{2,1,0:T(8,128)(2,1)S(1)} %pad_maximum_fusion.refs_0_, bf16[2,16,2048]{2,1,0:T(8,128)(2,1)S(1)} %collective-permute-done.2.refs_1_, bf16[2,16,2048]{2,1,0:T(8,128)(2,1)S(1)} %collective-permute-done.3.refs_2_, bf16[2,16,2048]{2,1,0:T(8,128)(2,1)S(1)} %collective-permute-done.4.refs_3_, ...), custom_call_target="tpu_custom_call" | custom-call | flops 268435456 | bytes 2097152 | tf_op jit(solution)/shard_map/pallas_call | solution.py:34
  22.9 2.4 %collective-permute-done.10.refs_3_ = bf16[2,16,2048]{2,1,0:T(8,128)(2,1)S(1)} collective-permute-done((bf16[2,16,2048]{2,1,0:T(8,128)(2,1)S(1)}, bf16[2,16,2048]{2,1,0:T(8,128)(2,1)S(1)}, u32[]{:S(2)}, u32[]{:S(2)}) %collective-permute-start.10) | collective-permute-done | bytes 131104 | tf_op jit(solution)/shard_map/plane1_rows11/ppermute | solution.py:225
  25.3 0.8 %shard_map.63.refs_1_ = f32[64,256]{1,0:T(8,128)S(1)} custom-call(bf16[2,16,2048]{2,1,0:T(8,128)(2,1)S(1)} %constant_dynamic-update-slice_fusion.refs_0_, bf16[2,16,2048]{2,1,0:T(8,128)(2,1)S(1)} %collective-permute-done.8.refs_1_, bf16[2,16,2048]{2,1,0:T(8,128)(2,1)S(1)} %collective-permute-done.9.refs_2_, ...), custom_call_target="tpu_custom_call" | custom-call | flops 268435456 | bytes 2097152 | tf_op jit(solution)/shard_map/pallas_call | solution.py:34
  26.3 1.2 %collective-permute-done.12.refs_3_ = f32[64,256]{1,0:T(8,128)S(1)} collective-permute-done((f32[64,256]{1,0:T(8,128)S(1)}, f32[64,256]{1,0:T(8,128)S(1)}, u32[]{:S(2)}, u32[]{:S(2)}) %collective-permute-start.12) | collective-permute-done | bytes 65568 | tf_op jit(solution)/shard_map/core_scores1/ppermute | solution.py:225
  27.5 0.6 %shard_map.64 = (bf16[64,256]{1,0:T(8,128)(2,1)S(1)}, f32[1,256]{1,0:T(1,128)S(1)}, bf16[4,16,2048]{2,1,0:T(8,128)(2,1)S(1)}, bf16[2,16,2048]{2,1,0:T(8,128)(2,1)S(1)}, bf16[2,16,2048]{2,1,0:T(8,128)(2,1)S(1)}) custom-call(f32[64,256]{1,0:T(8,128)S(1)} %shard_map.62.refs_0_, f32[64,256]{1,0:T(8,128)S(1)} %shard_map.63.refs_1_, ...), custom_call_target="tpu_custom_call" | custom-call | flops 268435456 | bytes 4194304 | tf_op jit(solution)/shard_map/pallas_call | solution.py:34
  28.1 1.7 %collective-permute-start.16 = (bf16[2,16,2048]{2,1,0:T(8,128)(2,1)S(1)}, bf16[2,16,2048]{2,1,0:T(8,128)(2,1)S(1)}, u32[]{:S(2)}, u32[]{:S(2)}) collective-permute-start(bf16[2,16,2048]{2,1,0:T(8,128)(2,1)S(1)} %get-tuple-element.33), channel_id=1, source_target_pairs={{0,4},{1,3},{2,6},{3,1},{4,0},{5,7},{6,2},{7,5},{8,12},{9,11},{10,... | collective-permute-start | bytes 393224 | tf_op jit(solution)/shard_map/plane1_far1/ppermute | solution.py:225
  30.7 2.5 %collective-permute-done.16 = bf16[2,16,2048]{2,1,0:T(8,128)(2,1)S(1)} collective-permute-done((bf16[2,16,2048]{2,1,0:T(8,128)(2,1)S(1)}, bf16[2,16,2048]{2,1,0:T(8,128)(2,1)S(1)}, u32[]{:S(2)}, u32[]{:S(2)}) %collective-permute-start.16) | collective-permute-done | bytes 131104 | tf_op jit(solution)/shard_map/plane1_far1/ppermute | solution.py:225
  33.2 1.5 %collective-permute-start.17 = (bf16[2,16,2048]{2,1,0:T(8,128)(2,1)S(1)}, bf16[2,16,2048]{2,1,0:T(8,128)(2,1)S(1)}, u32[]{:S(2)}, u32[]{:S(2)}) collective-permute-start(bf16[2,16,2048]{2,1,0:T(8,128)(2,1)S(1)} %add_convert_fusion.1), channel_id=1, source_target_pairs={{0,2},{1,5},{2,0},{3,7},{4,6},{5,1},{6,4},{7,3},{8,10},{9,13},{10,... | collective-permute-start | bytes 393224 | tf_op jit(solution)/shard_map/plane0_far/ppermute | solution.py:225
  34.7 0.8 %collective-permute-start.14 = (bf16[4,16,2048]{2,1,0:T(8,128)(2,1)S(1)}, bf16[4,16,2048]{2,1,0:T(8,128)(2,1)S(1)}, u32[]{:S(2)}, u32[]{:S(2)}) collective-permute-start(bf16[4,16,2048]{2,1,0:T(8,128)(2,1)S(1)} %get-tuple-element.28), channel_id=1, source_target_pairs={{0,8},{1,9},{2,10},{3,11},{4,12},{5,13},{6,14},{7,15},{8,0},{9,1},... | collective-permute-start | bytes 786440 | tf_op jit(solution)/shard_map/cls1_near/ppermute | solution.py:225
  35.4 2.8 %collective-permute-done.17 = bf16[2,16,2048]{2,1,0:T(8,128)(2,1)S(1)} collective-permute-done((bf16[2,16,2048]{2,1,0:T(8,128)(2,1)S(1)}, bf16[2,16,2048]{2,1,0:T(8,128)(2,1)S(1)}, u32[]{:S(2)}, u32[]{:S(2)}) %collective-permute-start.17) | collective-permute-done | bytes 131104 | tf_op jit(solution)/shard_map/plane0_far/ppermute | solution.py:225
  38.3 1.5 %collective-permute-start.18 = (bf16[1,16,2048]{2,1,0:T(8,128)(2,1)S(1)}, bf16[1,16,2048]{2,1,0:T(8,128)(2,1)S(1)}, u32[]{:S(2)}, u32[]{:S(2)}) collective-permute-start(bf16[1,16,2048]{2,1,0:T(8,128)(2,1)S(1)} %get-tuple-element.41), channel_id=1, source_target_pairs={{0,16},{1,17},{2,18},{3,19},{4,20},{5,21},{6,22},{7,23},{8,24},{9,... | collective-permute-start | bytes 196616 | tf_op jit(solution)/shard_map/cls2_far/ppermute | solution.py:225
  39.8 1.3 %collective-permute-start.19 = (bf16[1,16,2048]{2,1,0:T(8,128)(2,1)S(1)}, bf16[1,16,2048]{2,1,0:T(8,128)(2,1)S(1)}, u32[]{:S(2)}, u32[]{:S(2)}) collective-permute-start(bf16[1,16,2048]{2,1,0:T(8,128)(2,1)S(1)} %get-tuple-element.40), channel_id=1, source_target_pairs={{0,24},{1,25},{2,26},{3,27},{4,28},{5,29},{6,30},{7,31},{8,16},{9,... | collective-permute-start | bytes 196616 | tf_op jit(solution)/shard_map/cls3_far/ppermute | solution.py:225
  41.2 1.6 %collective-permute-done.14.refs_1_ = bf16[4,16,2048]{2,1,0:T(8,128)(2,1)S(1)} collective-permute-done((bf16[4,16,2048]{2,1,0:T(8,128)(2,1)S(1)}, bf16[4,16,2048]{2,1,0:T(8,128)(2,1)S(1)}, u32[]{:S(2)}, u32[]{:S(2)}) %collective-permute-start.14) | collective-permute-done | bytes 262176 | tf_op jit(solution)/shard_map/cls1_near/ppermute | solution.py:225
  42.9 1.4 %collective-permute-start.20 = (f32[1,16,2048]{2,1,0:T(8,128)S(1)}, f32[1,16,2048]{2,1,0:T(8,128)S(1)}, u32[]{:S(2)}, u32[]{:S(2)}) collective-permute-start(f32[1,16,2048]{2,1,0:T(8,128)S(1)} %get-tuple-element.34), channel_id=1, source_target_pairs={{0,6},{1,7},{2,4},{3,5},{4,2},{5,3},{6,0},{7,1},{8,14},{9,15},{10,... | collective-permute-start | bytes 393224 | tf_op jit(solution)/shard_map/plane_own3/ppermute | solution.py:225
  44.3 1.6 %collective-permute-start.21 = (f32[1,16,2048]{2,1,0:T(8,128)S(1)}, f32[1,16,2048]{2,1,0:T(8,128)S(1)}, u32[]{:S(2)}, u32[]{:S(2)}) collective-permute-start(f32[1,16,2048]{2,1,0:T(8,128)S(1)} %get-tuple-element.35), channel_id=1, source_target_pairs={{0,4},{1,3},{2,6},{3,1},{4,0},{5,7},{6,2},{7,5},{8,12},{9,11},{10,... | collective-permute-start | bytes 393224 | tf_op jit(solution)/shard_map/plane_own2/ppermute | solution.py:225
  45.9 0.5 collective-permute-start.22
  46.4 3.3 %collective-permute-done.20.refs_2_ = f32[1,16,2048]{2,1,0:T(8,128)S(1)} collective-permute-done((f32[1,16,2048]{2,1,0:T(8,128)S(1)}, f32[1,16,2048]{2,1,0:T(8,128)S(1)}, u32[]{:S(2)}, u32[]{:S(2)}) %collective-permute-start.20) | collective-permute-done | bytes 131104 | tf_op jit(solution)/shard_map/plane_own3/ppermute | solution.py:225
  49.7 0.6 %collective-permute-done.21.refs_3_ = f32[1,16,2048]{2,1,0:T(8,128)S(1)} collective-permute-done((f32[1,16,2048]{2,1,0:T(8,128)S(1)}, f32[1,16,2048]{2,1,0:T(8,128)S(1)}, u32[]{:S(2)}, u32[]{:S(2)}) %collective-permute-start.21) | collective-permute-done | bytes 131104 | tf_op jit(solution)/shard_map/plane_own2/ppermute | solution.py:225
  51.5 0.7 %collective-permute-done.23.got = f32[2,4,2048]{2,1,0:T(4,128)S(1)} collective-permute-done((f32[2,4,2048]{2,1,0:T(4,128)S(1)}, f32[2,4,2048]{2,1,0:T(4,128)S(1)}, u32[]{:S(2)}, u32[]{:S(2)}) %collective-permute-start.23) | collective-permute-done | bytes 65568 | tf_op jit(solution)/shard_map/core_sums/ppermute | solution.py:225
  52.2 0.7 %shard_map.69 = f32[2,2,8192]{2,1,0:T(2,128)} custom-call(s32[1]{0:T(128)} %bitcast.core.refs_4_.refs_7_, f32[2,4,2048]{2,1,0:T(4,128)S(1)} %get-tuple-element.37.kept, f32[2,4,2048]{2,1,0:T(4,128)S(1)} %collective-permute-done.23.got), custom_call_target="tpu_custom_call" | custom-call | bytes 262144 | tf_op jit(solution)/shard_map/pallas_call | solution.py:34
  (53 shorter events, 3.5 us)
Async XLA Ops:
  0.6 16.9 %copy-start.4 = (s32[128,1]{0,1:T(1,128)S(1)}, s32[128,1]{0,1:T(1,128)}, u32[]{:S(2)}) copy-start(s32[128,1]{0,1:T(1,128)} %param.5) | copy-start | bytes 1540
  0.6 9.0 %copy-start.3 = (bf16[128]{0:T(256)(128)(2,1)S(1)}, bf16[128]{0:T(256)(128)(2,1)}, u32[]{:S(2)}) copy-start(bf16[128]{0:T(256)(128)(2,1)} %param.6) | copy-start | bytes 772
  0.6 1.6 %collective-permute-start = (bf16[2,2,8192]{2,1,0:T(2,128)(2,1)}, bf16[2,2,8192]{2,1,0:T(2,128)(2,1)S(1)}, u32[]{:S(2)}, u32[]{:S(2)}) collective-permute-start(bf16[2,2,8192]{2,1,0:T(2,128)(2,1)} %source.1), channel_id=1, source_target_pairs={{0,1},{1,0},{2,3},{3,2},{4,5},{5,4},{6,7},{7,6},{8,9},{9,8},{10,11... | collective-permute-start | bytes 196616 | tf_op jit(solution)/shard_map/core_rows/ppermute | solution.py:225
  1.3 0.8 %copy-start.2 = (bf16[2,2,8192]{2,1,0:T(2,128)(2,1)S(1)}, bf16[2,2,8192]{2,1,0:T(2,128)(2,1)}, u32[]{:S(2)}) copy-start(bf16[2,2,8192]{2,1,0:T(2,128)(2,1)} %source.1) | copy-start | bytes 196612
  2.3 7.4 %collective-permute-start.1 = (bf16[1,16,2048]{2,1,0:T(8,128)(2,1)S(1)}, bf16[1,16,2048]{2,1,0:T(8,128)(2,1)S(1)}, u32[]{:S(2)}, u32[]{:S(2)}) collective-permute-start(bf16[1,16,2048]{2,1,0:T(8,128)(2,1)S(1)} %shard_map.60), channel_id=1, source_target_pairs={{0,8},{1,9},{2,10},{3,11},{4,12},{5,13},{6,14},{7,15},{8,0},{9,1},... | collective-permute-start | bytes 196616 | tf_op jit(solution)/shard_map/cls1_rows/ppermute | solution.py:225
  5.3 7.7 %collective-permute-start.6 = (bf16[1,16,2048]{2,1,0:T(8,128)(2,1)S(1)}, bf16[1,16,2048]{2,1,0:T(8,128)(2,1)S(1)}, u32[]{:S(2)}, u32[]{:S(2)}) collective-permute-start(bf16[1,16,2048]{2,1,0:T(8,128)(2,1)S(1)} %shard_map.60), channel_id=1, source_target_pairs={{0,16},{1,17},{2,18},{3,19},{4,20},{5,21},{6,22},{7,23},{8,24},{9,... | collective-permute-start | bytes 196616 | tf_op jit(solution)/shard_map/cls2_rows/ppermute | solution.py:225
  7.9 6.2 %collective-permute-start.7 = (bf16[1,16,2048]{2,1,0:T(8,128)(2,1)S(1)}, bf16[1,16,2048]{2,1,0:T(8,128)(2,1)S(1)}, u32[]{:S(2)}, u32[]{:S(2)}) collective-permute-start(bf16[1,16,2048]{2,1,0:T(8,128)(2,1)S(1)} %shard_map.60), channel_id=1, source_target_pairs={{0,24},{1,25},{2,26},{3,27},{4,28},{5,29},{6,30},{7,31},{8,16},{9,... | collective-permute-start | bytes 196616 | tf_op jit(solution)/shard_map/cls3_rows/ppermute | solution.py:225
  7.9 1.6 %copy-start = (bf16[128,8192]{1,0:T(8,128)(2,1)S(1)}, bf16[128,8192]{1,0:T(8,128)(2,1)}, u32[]{:S(2)}) copy-start(bf16[128,8192]{1,0:T(8,128)(2,1)} %images.2) | copy-start | bytes 6291460
  9.5 12.5 %copy-start.1 = (bf16[128,8192]{1,0:T(8,128)(2,1)S(1)}, bf16[128,8192]{1,0:T(8,128)(2,1)}, u32[]{:S(2)}) copy-start(bf16[128,8192]{1,0:T(8,128)(2,1)} %images.2) | copy-start | bytes 6291460
  9.6 12.4 %collective-permute-start.5 = (bf16[128,4096]{1,0:T(8,128)(2,1)S(1)}, bf16[128,4096]{1,0:T(8,128)(2,1)S(1)}, u32[]{:S(2)}, u32[]{:S(2)}) collective-permute-start(bf16[128,4096]{1,0:T(8,128)(2,1)S(1)} %shard_map.61), channel_id=1, source_target_pairs={{0,1},{1,0},{2,3},{3,2},{4,5},{5,4},{6,7},{7,6},{8,9},{9,8},{10,11... | collective-permute-start | bytes 3145736 | tf_op jit(solution)/shard_map/core_images/ppermute | solution.py:225
  9.7 5.9 %collective-permute-start.2 = (bf16[2,16,2048]{2,1,0:T(8,128)(2,1)S(1)}, bf16[2,16,2048]{2,1,0:T(8,128)(2,1)S(1)}, u32[]{:S(2)}, u32[]{:S(2)}) collective-permute-start(bf16[2,16,2048]{2,1,0:T(8,128)(2,1)S(1)} %pad_maximum_fusion.refs_0_), channel_id=1, source_target_pairs={{0,2},{1,5},{2,0},{3,7},{4,6},{5,1},{6,4},{7,3},{8,10},{9,13},{10,... | collective-permute-start | bytes 393224 | tf_op jit(solution)/shard_map/plane0_rows00/ppermute | solution.py:225
  11.5 6.1 %collective-permute-start.3 = (bf16[2,16,2048]{2,1,0:T(8,128)(2,1)S(1)}, bf16[2,16,2048]{2,1,0:T(8,128)(2,1)S(1)}, u32[]{:S(2)}, u32[]{:S(2)}) collective-permute-start(bf16[2,16,2048]{2,1,0:T(8,128)(2,1)S(1)} %pad_maximum_fusion.refs_0_), channel_id=1, source_target_pairs={{0,4},{1,3},{2,6},{3,1},{4,0},{5,7},{6,2},{7,5},{8,12},{9,11},{10,... | collective-permute-start | bytes 393224 | tf_op jit(solution)/shard_map/plane1_rows00/ppermute | solution.py:225
  14.1 6.3 %collective-permute-start.8 = (bf16[2,16,2048]{2,1,0:T(8,128)(2,1)S(1)}, bf16[2,16,2048]{2,1,0:T(8,128)(2,1)S(1)}, u32[]{:S(2)}, u32[]{:S(2)}) collective-permute-start(bf16[2,16,2048]{2,1,0:T(8,128)(2,1)S(1)} %constant_dynamic-update-slice_fusion.refs_0_), channel_id=1, source_target_pairs={{0,2},{1,5},{2,0},{3,7},{4,6},{5,1},{6,4},{7,3},{8,10},{9,13},{10,... | collective-permute-start | bytes 393224 | tf_op jit(solution)/shard_map/plane0_rows10/ppermute | solution.py:225
  15.6 6.4 %collective-permute-start.4 = (bf16[2,16,2048]{2,1,0:T(8,128)(2,1)S(1)}, bf16[2,16,2048]{2,1,0:T(8,128)(2,1)S(1)}, u32[]{:S(2)}, u32[]{:S(2)}) collective-permute-start(bf16[2,16,2048]{2,1,0:T(8,128)(2,1)S(1)} %collective-permute-done.2.refs_1_), channel_id=1, source_target_pairs={{0,4},{1,3},{2,6},{3,1},{4,0},{5,7},{6,2},{7,5},{8,12},{9,11},{10,... | collective-permute-start | bytes 393224 | tf_op jit(solution)/shard_map/plane1_rows01/ppermute | solution.py:225
  17.5 5.4 %collective-permute-start.13 = (f32[2,128]{1,0:T(2,128)S(1)}, f32[2,128]{1,0:T(2,128)S(1)}, u32[]{:S(2)}, u32[]{:S(2)}) collective-permute-start(f32[2,128]{1,0:T(2,128)S(1)} %pad_maximum_fusion.2), channel_id=1, source_target_pairs={{0,1},{1,0},{2,3},{3,2},{4,5},{5,4},{6,7},{7,6},{8,9},{9,8},{10,11... | collective-permute-start | bytes 3080 | tf_op jit(solution)/shard_map/core_side/ppermute | solution.py:225
  17.6 7.8 %collective-permute-start.9 = (bf16[2,16,2048]{2,1,0:T(8,128)(2,1)S(1)}, bf16[2,16,2048]{2,1,0:T(8,128)(2,1)S(1)}, u32[]{:S(2)}, u32[]{:S(2)}) collective-permute-start(bf16[2,16,2048]{2,1,0:T(8,128)(2,1)S(1)} %constant_dynamic-update-slice_fusion.refs_0_), channel_id=1, source_target_pairs={{0,4},{1,3},{2,6},{3,1},{4,0},{5,7},{6,2},{7,5},{8,12},{9,11},{10,... | collective-permute-start | bytes 393224 | tf_op jit(solution)/shard_map/plane1_rows10/ppermute | solution.py:225
  20.4 5.0 %collective-permute-start.10 = (bf16[2,16,2048]{2,1,0:T(8,128)(2,1)S(1)}, bf16[2,16,2048]{2,1,0:T(8,128)(2,1)S(1)}, u32[]{:S(2)}, u32[]{:S(2)}) collective-permute-start(bf16[2,16,2048]{2,1,0:T(8,128)(2,1)S(1)} %collective-permute-done.8.refs_1_), channel_id=1, source_target_pairs={{0,4},{1,3},{2,6},{3,1},{4,0},{5,7},{6,2},{7,5},{8,12},{9,11},{10,... | collective-permute-start | bytes 393224 | tf_op jit(solution)/shard_map/plane1_rows11/ppermute | solution.py:225
  22.8 2.5 %collective-permute-start.11 = (f32[64,256]{1,0:T(8,128)S(1)}, f32[64,256]{1,0:T(8,128)S(1)}, u32[]{:S(2)}, u32[]{:S(2)}) collective-permute-start(f32[64,256]{1,0:T(8,128)S(1)} %shard_map.62.refs_0_), channel_id=1, source_target_pairs={{0,1},{1,0},{2,3},{3,2},{4,5},{5,4},{6,7},{7,6},{8,9},{9,8},{10,11... | collective-permute-start | bytes 196616 | tf_op jit(solution)/shard_map/core_scores0/ppermute | solution.py:225
  26.2 1.3 %collective-permute-start.12 = (f32[64,256]{1,0:T(8,128)S(1)}, f32[64,256]{1,0:T(8,128)S(1)}, u32[]{:S(2)}, u32[]{:S(2)}) collective-permute-start(f32[64,256]{1,0:T(8,128)S(1)} %shard_map.63.refs_1_), channel_id=1, source_target_pairs={{0,1},{1,0},{2,3},{3,2},{4,5},{5,4},{6,7},{7,6},{8,9},{9,8},{10,11... | collective-permute-start | bytes 196616 | tf_op jit(solution)/shard_map/core_scores1/ppermute | solution.py:225
  28.1 5.0 %collective-permute-start.16 = (bf16[2,16,2048]{2,1,0:T(8,128)(2,1)S(1)}, bf16[2,16,2048]{2,1,0:T(8,128)(2,1)S(1)}, u32[]{:S(2)}, u32[]{:S(2)}) collective-permute-start(bf16[2,16,2048]{2,1,0:T(8,128)(2,1)S(1)} %get-tuple-element.33), channel_id=1, source_target_pairs={{0,4},{1,3},{2,6},{3,1},{4,0},{5,7},{6,2},{7,5},{8,12},{9,11},{10,... | collective-permute-start | bytes 393224 | tf_op jit(solution)/shard_map/plane1_far1/ppermute | solution.py:225
  29.8 5.6 %collective-permute-start.15 = (bf16[2,16,2048]{2,1,0:T(8,128)(2,1)S(1)}, bf16[2,16,2048]{2,1,0:T(8,128)(2,1)S(1)}, u32[]{:S(2)}, u32[]{:S(2)}) collective-permute-start(bf16[2,16,2048]{2,1,0:T(8,128)(2,1)S(1)} %get-tuple-element.31), channel_id=1, source_target_pairs={{0,4},{1,3},{2,6},{3,1},{4,0},{5,7},{6,2},{7,5},{8,12},{9,11},{10,... | collective-permute-start | bytes 393224 | tf_op jit(solution)/shard_map/plane1_far0/ppermute | solution.py:225
  33.2 5.0 %collective-permute-start.17 = (bf16[2,16,2048]{2,1,0:T(8,128)(2,1)S(1)}, bf16[2,16,2048]{2,1,0:T(8,128)(2,1)S(1)}, u32[]{:S(2)}, u32[]{:S(2)}) collective-permute-start(bf16[2,16,2048]{2,1,0:T(8,128)(2,1)S(1)} %add_convert_fusion.1), channel_id=1, source_target_pairs={{0,2},{1,5},{2,0},{3,7},{4,6},{5,1},{6,4},{7,3},{8,10},{9,13},{10,... | collective-permute-start | bytes 393224 | tf_op jit(solution)/shard_map/plane0_far/ppermute | solution.py:225
  34.7 8.1 %collective-permute-start.14 = (bf16[4,16,2048]{2,1,0:T(8,128)(2,1)S(1)}, bf16[4,16,2048]{2,1,0:T(8,128)(2,1)S(1)}, u32[]{:S(2)}, u32[]{:S(2)}) collective-permute-start(bf16[4,16,2048]{2,1,0:T(8,128)(2,1)S(1)} %get-tuple-element.28), channel_id=1, source_target_pairs={{0,8},{1,9},{2,10},{3,11},{4,12},{5,13},{6,14},{7,15},{8,0},{9,1},... | collective-permute-start | bytes 786440 | tf_op jit(solution)/shard_map/cls1_near/ppermute | solution.py:225
  38.3 8.1 %collective-permute-start.18 = (bf16[1,16,2048]{2,1,0:T(8,128)(2,1)S(1)}, bf16[1,16,2048]{2,1,0:T(8,128)(2,1)S(1)}, u32[]{:S(2)}, u32[]{:S(2)}) collective-permute-start(bf16[1,16,2048]{2,1,0:T(8,128)(2,1)S(1)} %get-tuple-element.41), channel_id=1, source_target_pairs={{0,16},{1,17},{2,18},{3,19},{4,20},{5,21},{6,22},{7,23},{8,24},{9,... | collective-permute-start | bytes 196616 | tf_op jit(solution)/shard_map/cls2_far/ppermute | solution.py:225
  39.8 6.6 %collective-permute-start.19 = (bf16[1,16,2048]{2,1,0:T(8,128)(2,1)S(1)}, bf16[1,16,2048]{2,1,0:T(8,128)(2,1)S(1)}, u32[]{:S(2)}, u32[]{:S(2)}) collective-permute-start(bf16[1,16,2048]{2,1,0:T(8,128)(2,1)S(1)} %get-tuple-element.40), channel_id=1, source_target_pairs={{0,24},{1,25},{2,26},{3,27},{4,28},{5,29},{6,30},{7,31},{8,16},{9,... | collective-permute-start | bytes 196616 | tf_op jit(solution)/shard_map/cls3_far/ppermute | solution.py:225
  42.9 6.9 %collective-permute-start.20 = (f32[1,16,2048]{2,1,0:T(8,128)S(1)}, f32[1,16,2048]{2,1,0:T(8,128)S(1)}, u32[]{:S(2)}, u32[]{:S(2)}) collective-permute-start(f32[1,16,2048]{2,1,0:T(8,128)S(1)} %get-tuple-element.34), channel_id=1, source_target_pairs={{0,6},{1,7},{2,4},{3,5},{4,2},{5,3},{6,0},{7,1},{8,14},{9,15},{10,... | collective-permute-start | bytes 393224 | tf_op jit(solution)/shard_map/plane_own3/ppermute | solution.py:225
  44.3 6.1 %collective-permute-start.21 = (f32[1,16,2048]{2,1,0:T(8,128)S(1)}, f32[1,16,2048]{2,1,0:T(8,128)S(1)}, u32[]{:S(2)}, u32[]{:S(2)}) collective-permute-start(f32[1,16,2048]{2,1,0:T(8,128)S(1)} %get-tuple-element.35), channel_id=1, source_target_pairs={{0,4},{1,3},{2,6},{3,1},{4,0},{5,7},{6,2},{7,5},{8,12},{9,11},{10,... | collective-permute-start | bytes 393224 | tf_op jit(solution)/shard_map/plane_own2/ppermute | solution.py:225
  45.9 5.0 %collective-permute-start.22 = (f32[1,16,2048]{2,1,0:T(8,128)S(1)}, f32[1,16,2048]{2,1,0:T(8,128)S(1)}, u32[]{:S(2)}, u32[]{:S(2)}) collective-permute-start(f32[1,16,2048]{2,1,0:T(8,128)S(1)} %get-tuple-element.36), channel_id=1, source_target_pairs={{0,2},{1,5},{2,0},{3,7},{4,6},{5,1},{6,4},{7,3},{8,10},{9,13},{10,... | collective-permute-start | bytes 393224 | tf_op jit(solution)/shard_map/plane_own1/ppermute | solution.py:225
  50.9 1.3 %collective-permute-start.23 = (f32[2,4,2048]{2,1,0:T(4,128)S(1)}, f32[2,4,2048]{2,1,0:T(4,128)S(1)}, u32[]{:S(2)}, u32[]{:S(2)}) collective-permute-start(f32[2,4,2048]{2,1,0:T(4,128)S(1)} %get-tuple-element.38), channel_id=1, source_target_pairs={{0,1},{1,0},{2,3},{3,2},{4,5},{5,4},{6,7},{7,6},{8,9},{9,8},{10,11... | collective-permute-start | bytes 196616 | tf_op jit(solution)/shard_map/core_sums/ppermute | solution.py:225

commit v4 on v3

v4 whole, which is shorter than its diff:
```python
import functools
import math

import jax
import jax.numpy as jnp
from jax import lax
from jax.experimental import pallas as pl
from jax.experimental.pallas import tpu as pltpu
from jax.sharding import PartitionSpec as P

AXES = ("cls", "dom")
CORE = 1
FLOAT, SHORT = jnp.float32, jnp.bfloat16
NT = (((1,), (1,)), ((), ()))
COSTS = {
    "part": (1 << 30, 1 << 20),
    "near_score": (1 << 28, 1 << 21),
    "far_score": (1 << 20, 1 << 20),
    "softmax": (1 << 28, 1 << 22),
    "weigh": (1 << 28, 1 << 22),
    "near": (1 << 20, 1 << 16),
    "sum": (1 << 31, 1 << 16),
}


def plan(mesh):
    owners, dom = mesh.shape["cls"], mesh.shape["dom"]
    plane_bits = (dom // 2).bit_length() - 1
    masks = [2 << bit for bit in range(plane_bits)]
    if plane_bits % 2:
        return owners, dom, (masks, masks), False
    low, high = masks[: plane_bits // 2], masks[plane_bits // 2 :]
    return owners, dom, (low + high, high + low), True


def call(body, outs, cost, *args, smem=()):
    spaces = [
        pl.BlockSpec(memory_space=pltpu.SMEM if i in smem else pltpu.VMEM) for i in range(len(args))
    ]
    out_shape = [jax.ShapeDtypeStruct(shape, kind) for shape, kind in outs]
    held = sum(math.prod(array.shape) * array.dtype.itemsize for array in [*args, *out_shape])
    return pl.pallas_call(
        body,
        out_shape=out_shape,
        in_specs=spaces,
        out_specs=[pl.BlockSpec(memory_space=pltpu.VMEM)] * len(outs),
        compiler_params=pltpu.CompilerParams(vmem_limit_bytes=min(held + (8 << 20), 56 << 20)),
        cost_estimate=pl.CostEstimate(flops=cost[0], bytes_accessed=cost[1], transcendentals=0),
    )(*args)


def by_core(core, body):
    @pl.when(core[0] == 0)
    def _():
        body(0)

    @pl.when(core[0] != 0)
    def _():
        body(1)


def copy_body(source, out):
    out[...] = source[...]


def block_body(core, mine, theirs, out):
    quarter = out.shape[2]

    def fill(c):
        pair = (theirs, mine) if c else (mine, theirs)
        for ch in range(2):
            lo = (2 * c + ch) * quarter
            rows = [
                ref[k, :, lo : lo + quarter].astype(FLOAT) for ref in pair for k in range(ref.shape[0])
            ]
            rows = jnp.concatenate(rows, axis=0)
            out[0, ch * rows.shape[0] : (ch + 1) * rows.shape[0]] = rows.astype(SHORT)

    by_core(core, fill)


def total_body(core, *refs):
    *parts, kept, sent = refs
    rows = kept.shape[1]
    total = parts[0][0].astype(FLOAT)
    for part in parts[1:]:
        total += part[0].astype(FLOAT)

    def fill(c):
        for ch in range(2):
            at = 2 * ch * rows
            kept[ch] = total[at + c * rows : at + (c + 1) * rows]
            sent[ch] = total[at + (1 - c) * rows : at + (2 - c) * rows]

    by_core(core, fill)


def final_body(core, kept, got, out):
    quarter, (classes, own) = kept.shape[2], out.shape[:2]

    def fill(c):
        for j, part in ((c, kept), (1 - c, got)):
            for ch in range(2):
                lo = (2 * j + ch) * quarter
                for k in range(classes):
                    out[k, :, lo : lo + quarter] = part[ch, k * own : (k + 1) * own]

    by_core(core, fill)


def sum_body(*refs):
    *parts, out = refs
    total = parts[0][...].astype(FLOAT)
    for part in parts[1:]:
        total += part[...].astype(FLOAT)
    out[...] = total


def near_body(*refs):
    count = sum(1 for ref in refs if ref.shape[0] != refs[0].shape[0])
    parts, outs = refs[:-count], refs[-count:]
    at = 0
    for out in outs:
        total = 0.0
        for part in parts:
            total += part[at : at + out.shape[0]].astype(FLOAT)
        out[...] = total.astype(out.dtype)
        at += out.shape[0]


def part_body(core, images, sent):
    half = sent.shape[1]

    def fill(c):
        sent[...] = images[:, (1 - c) * half : (2 - c) * half]

    by_core(core, fill)


def columns(images, other, j, c, lo, count):
    if j:
        return other[:, lo : lo + count]
    lo += c * other.shape[1]
    return images[:, lo : lo + count]


def score_body(count, *refs):
    core, images, other, out = refs[count:]
    quarter = refs[0].shape[2]
    rows = jnp.concatenate([ref[...].reshape(-1, quarter) for ref in refs[:count]], axis=0)
    blocks = rows.shape[0] // 16
    wide = rows.astype(FLOAT)
    norms = jnp.sum(wide * wide, axis=1, keepdims=True).reshape(blocks, 16, 1)
    norms = 0.5 * (norms[:, :8] + norms[:, 8:]).reshape(blocks * 8, 1)
    local = images.shape[0]

    def fill(c):
        for j in range(2):
            sums = 0.0
            for ch in range(2):
                chunk = columns(images, other, j, c, ch * quarter, quarter)
                scores = lax.dot_general(rows, chunk, NT, preferred_element_type=FLOAT)
                sums += scores.reshape(blocks, 16, local)[:, ch * 8 : ch * 8 + 8]
            out[:, j * local : (j + 1) * local] = sums.reshape(blocks * 8, local) - norms

    by_core(core, fill)


def score(pieces, core, images, other, cost):
    blocks = sum(piece.shape[0] for piece in pieces)
    return call(
        functools.partial(score_body, len(pieces)),
        [((blocks * 8, 2 * images.shape[0]), FLOAT)],
        cost,
        *pieces,
        core,
        images,
        other,
        smem=(len(pieces),),
    )[0]


def weigh_rows(weights, core, images, other, outs):
    quarter = outs[0].shape[2]
    blocks = weights.shape[0] // 8
    step = 512

    def fill(c):
        for begin in range(0, quarter, step):
            halves = []
            for lo in (begin, quarter + begin):
                chunk = [columns(images, other, j, c, lo, step) for j in range(2)]
                chunk = jnp.concatenate(chunk, axis=0)
                sums = jnp.dot(weights, chunk, preferred_element_type=FLOAT)
                halves.append(sums.reshape(blocks, 8, step))
            at = 0
            for out in outs:
                count = out.shape[0]
                both = [sums[at : at + count] for sums in halves]
                out[:, :, begin : begin + step] = jnp.concatenate(both, axis=1).astype(out.dtype)
                at += count

    by_core(core, fill)


def weigh_body(weights, core, images, other, *outs):
    weigh_rows(weights[...], core, images, other, outs)


def softmax_body(order, places, per_owner, own, leave, cut, count, *refs):
    mine, theirs = (
        jnp.concatenate([ref[...] for ref in part], axis=0)
        for part in (refs[:count], refs[count : 2 * count])
    )
    precision, named_class, place, core, images, other = refs[2 * count : 2 * count + 6]
    weights_near, evidence, *outs = refs[2 * count + 6 :]
    local = images.shape[0]
    theirs = jnp.concatenate([theirs[lo:hi] for lo, hi in order], axis=0)
    theirs = jnp.concatenate([theirs[:, local:], theirs[:, :local]], axis=1)
    scores = precision[...] * (mine + theirs)
    rows = lax.broadcasted_iota(jnp.int32, (2 * per_owner * own, 2 * local), 0)
    rows = lax.rem(lax.div(rows, own), per_owner)
    kind = [rows + (place[0] ^ k) * per_owner for k in places]
    named = jnp.concatenate(kind, axis=0) == named_class[...]
    largest = jnp.max(jnp.where(named, scores, -jnp.inf), axis=0, keepdims=True)
    exponent = jnp.where(named, jnp.exp(jnp.where(named, scores - largest, 0.0)), 0.0)
    totals = jnp.sum(exponent, axis=0, keepdims=True)
    weights = exponent / totals
    weights = jnp.concatenate([weights[lo:hi] for lo, hi in leave], axis=0).astype(SHORT)
    evidence[...] = largest + jnp.log(totals)
    weights_near[...] = weights[:cut]
    weigh_rows(weights[cut:], core, images, other, outs)


def solution(mesh):
    owners, dom, orders, crossed = plan(mesh)
    devices = owners * dom
    steps = len(orders[0])
    positions = 1 << steps
    near_count = max(owners // 2, 1)
    far_count = owners - near_count

    def swap(value, masks, name):
        pairs = [(i, i ^ masks[i % 2]) for i in range(devices)]
        with jax.named_scope(name):
            return lax.ppermute(value, AXES, pairs)

    def masks_of(q):
        return [
            functools.reduce(int.__xor__, [m for s, m in enumerate(way) if q >> s & 1])
            for way in orders
        ]

    def swap_core(value, name):
        return swap(value, (CORE, CORE), "core_" + name)

    def swap_plane(value, step, name):
        return swap(value, (orders[0][step], orders[1][step]), f"plane{step}_{name}")

    def swap_cls(value, k, name):
        return swap(value, (k * dom, k * dom), f"cls{k}_{name}")

    def on_device(particles, assign, inv_sigma, projections):
        local, width = particles.shape
        half, quarter = width // 2, width // 4
        per_owner, own = projections.shape[:2]
        mine_rows = per_owner * own
        size = 2 * mine_rows
        core = lax.axis_index("dom") % 2
        where = core.astype(jnp.int32)[None]
        place = lax.axis_index("cls").astype(jnp.int32)[None]
        got = swap_core(projections, "rows")
        rows = call(
            copy_body, [(projections.shape, SHORT)], (0, 4 * mine_rows * width), projections
        )[0]
        block = call(
            block_body, [((1, 2 * size, quarter), SHORT)], (0, 3 * size * half), where, rows, got,
            smem=(0,),
        )[0]

        def spread(held, name):
            older, newer = [held], []
            for step in range(steps):
                sets = [part for part in (older, newer) if part]
                fresh = [
                    swap_plane(jnp.concatenate(part, axis=0), step, f"{name}{i}")
                    for i, part in enumerate(sets)
                ]
                older, newer = older + newer, fresh
            return older + newer

        pieces = {0: block}
        for k in range(owners - 1, 0, -1):
            pieces[k] = swap_cls(block, k, "rows")
        groups = [range(near_count)] + ([range(near_count, owners)] if far_count else [])
        gathered = [
            spread(jnp.concatenate([pieces[k] for k in group], axis=0), f"rows{i}")
            for i, group in enumerate(groups)
        ]
        layout = [(k, q) for group in groups for q in range(positions) for k in group]

        late, late_assign, late_sigma, _ = lax.optimization_barrier(
            (particles, assign, inv_sigma, got)
        )
        side = jnp.stack([late_sigma.astype(FLOAT), late_assign[:, 0].astype(FLOAT)])
        side = jnp.concatenate([side, swap_core(side, "side")], axis=1)
        precision, class_id = side[:1], side[1:].astype(jnp.int32)
        sent = call(part_body, [((local, half), SHORT)], COSTS["part"], where, late, smem=(0,))[0]
        other = swap_core(sent, "images")

        partial = [score(gathered[0], where, particles, other, COSTS["near_score"])]
        others = [swap_core(partial[0], "scores0")]
        if far_count:
            gathered[1][-1], others[0] = lax.optimization_barrier((gathered[1][-1], others[0]))
            partial.append(score(gathered[1], where, particles, other, COSTS["far_score"]))
            others.append(swap_core(partial[1], "scores1"))

        index = {key: i for i, key in enumerate(layout)}
        side_len = 1 << (steps // 2)

        def span(key):
            return (index[key] * size, (index[key] + 1) * size)

        order = []
        for k, p in layout:
            q = p % side_len * side_len + p // side_len if crossed else p
            order.append(span((k, q)))
        places = [k for k, _ in layout]

        far_keys = [(k, q) for q in range(positions) for k in range(near_count, owners)]
        cut_far = len(far_keys) // 2
        stay_keys = [(0, q) for q in range(positions)] + far_keys[:cut_far]
        go_keys = [(k, q) for k in range(1, near_count) for q in range(positions)]
        go_keys += far_keys[cut_far:]
        leave = [span(key) for key in stay_keys + go_keys]
        cut = len(stay_keys) * size
        keeps = 2 if steps > 1 else 1
        specs_stay = [((positions, 2 * size, quarter), FLOAT)]
        specs_go = [((positions, 2 * size, quarter), SHORT)] * (near_count - 1)
        if far_count:
            count = len(far_keys) // (2 * keeps)
            specs_stay += [((count, 2 * size, quarter), FLOAT)] * keeps
            specs_go += [((count, 2 * size, quarter), SHORT)] * keeps
        weights, evidence, *sends = call(
            functools.partial(
                softmax_body, order, places, per_owner, own, leave, cut, len(partial)
            ),
            [((cut, 2 * local), SHORT), ((1, 2 * local), FLOAT)] + specs_go,
            COSTS["softmax"],
            *partial,
            *others,
            precision,
            class_id,
            place,
            where,
            particles,
            other,
            smem=(2 * len(partial) + 2, 2 * len(partial) + 3),
        )
        held, *kept = call(
            weigh_body, specs_stay, COSTS["weigh"], weights, where, particles, other, smem=(1,)
        )

        near = [swap_cls(part, k, "near") for k, part in enumerate(sends[: near_count - 1], 1)]
        ends = []
        if far_count:
            far = sends[near_count - 1 :]
            fresh = [swap_plane(far[i], steps - 1, f"far{i}") for i in range(keeps)[::-1]][::-1]
            kept = [part + new.astype(FLOAT) for part, new in zip(kept, fresh, strict=True)]
            for step in range(steps - 2, -1, -1):
                stay, send = kept
                if step == steps - 2:
                    send = send.astype(SHORT)
                if step == 0:
                    fresh = swap_plane(send, step, "far")
                    kept = [stay + fresh.astype(FLOAT)]
                    continue
                n = stay.shape[0] // 2
                away = stay[n:] + swap_plane(send[n:], step, "far1").astype(FLOAT)
                kept = [stay[:n] + swap_plane(send[:n], step, "far0").astype(FLOAT), away]
            for k in range(near_count, owners):
                j = k - near_count
                ends.append(swap_cls(kept[0][j : j + 1].astype(SHORT), k, "far"))
            ends = call(sum_body, [((1, 2 * size, quarter), FLOAT)], COSTS["sum"], *ends)
        kinds = [FLOAT] * (positions - 1) + [SHORT]
        own_parts = call(
            near_body,
            [((1, 2 * size, quarter), kind) for kind in kinds],
            COSTS["near"],
            held,
            *near,
        )
        ends = [own_parts[0], *ends]
        for q in range(positions - 1, 0, -1):
            ends.append(swap(own_parts[q], masks_of(q), f"plane_own{q}"))
        kept, sent = call(
            total_body,
            [((2, mine_rows, quarter), FLOAT)] * 2,
            (0, 8 * size * half),
            where,
            *ends,
            smem=(0,),
        )
        got = swap_core(sent, "sums")
        class_sums = call(
            final_body,
            [((per_owner, own, width), FLOAT)],
            (0, 8 * mine_rows * width),
            where,
            kept,
            got,
            smem=(0,),
        )[0]
        return class_sums, evidence[0, :local]

    return jax.shard_map(
        on_device,
        mesh=mesh,
        in_specs=(
            P(("cls", "dom"), None),
            P(("cls", "dom"), None),
            P(("cls", "dom")),
            P("cls", "dom", None),
        ),
        out_specs=(P("cls", "dom", None), P(("cls", "dom"))),
        check_vma=False,
    )
```

time: 53.1 us -> 52.4 us (0.987)
  transfers between devices with their start and end apart: 24 -> 24, of which waited for: 11 -> 10; matrix products, arithmetic and copies ran while one was open for 2% -> 1% of each run, Pallas kernels for 3% -> 3%
where the time goes in v4:
time: 52.4 us; the launch traced here: 52.2 us
  starting transfers between devices  27.2 us (52%)
  waiting for transfers between devices  17.4 us (33%)
  Pallas kernels  3.69 us (7%)
  local copies, waits for them, and re-layouts  2.98 us (6%)
  between operations  0.84 us (2%)
    ppermute x24, starting transfers between devices, swap(): return lax.ppermute(value, AXES, pairs)  27.2 us
    ppermute x24, waiting for transfers between devices, swap(): return lax.ppermute(value, AXES, pairs)  17.4 us
    pallas_call x11, Pallas kernels, call(): pl.pallas_call(body, out_shape=out_shape, in_specs=spaces, out_specs=[pl....  3.69 us
    unnamed x11, local copies, waits for them, and re-layouts  2.45 us
  transfers between devices with their start and end apart: 24, of which 10 were waited for; matrix products, arithmetic and copies ran while one was open for 1% of the time, Pallas kernels for 3%

profile of v4, /device:TPU:0, one launch (start us, length us, event | category | flops | bytes accessed | tf_op | source)
XLA Modules:
  0.0 52.2 jit_solution(4543071231487518997)
XLA Ops:
  0.6 0.5 collective-permute-start
  1.1 0.8 %copy-done.2 = bf16[2,2,8192]{2,1,0:T(2,128)(2,1)S(1)} copy-done((bf16[2,2,8192]{2,1,0:T(2,128)(2,1)S(1)}, bf16[2,2,8192]{2,1,0:T(2,128)(2,1)}, u32[]{:S(2)}) %copy-start.2) | copy-done | bytes 65560
  2.3 3.0 %collective-permute-start.1 = (bf16[1,16,2048]{2,1,0:T(8,128)(2,1)S(1)}, bf16[1,16,2048]{2,1,0:T(8,128)(2,1)S(1)}, u32[]{:S(2)}, u32[]{:S(2)}) collective-permute-start(bf16[1,16,2048]{2,1,0:T(8,128)(2,1)S(1)} %shard_map.60), channel_id=1, source_target_pairs={{0,8},{1,9},{2,10},{3,11},{4,12},{5,13},{6,14},{7,15},{8,0},{9,1},... | collective-permute-start | bytes 196616 | tf_op jit(solution)/shard_map/cls1_rows/ppermute | solution.py:246
  5.3 2.6 %collective-permute-start.6 = (bf16[1,16,2048]{2,1,0:T(8,128)(2,1)S(1)}, bf16[1,16,2048]{2,1,0:T(8,128)(2,1)S(1)}, u32[]{:S(2)}, u32[]{:S(2)}) collective-permute-start(bf16[1,16,2048]{2,1,0:T(8,128)(2,1)S(1)} %shard_map.60), channel_id=1, source_target_pairs={{0,16},{1,17},{2,18},{3,19},{4,20},{5,21},{6,22},{7,23},{8,24},{9,... | collective-permute-start | bytes 196616 | tf_op jit(solution)/shard_map/cls2_rows/ppermute | solution.py:246
  7.9 1.6 %copy-done = bf16[128,8192]{1,0:T(8,128)(2,1)S(1)} copy-done((bf16[128,8192]{1,0:T(8,128)(2,1)S(1)}, bf16[128,8192]{1,0:T(8,128)(2,1)}, u32[]{:S(2)}) %copy-start) | copy-done | bytes 2097176
  9.7 1.8 %collective-permute-start.2 = (bf16[2,16,2048]{2,1,0:T(8,128)(2,1)S(1)}, bf16[2,16,2048]{2,1,0:T(8,128)(2,1)S(1)}, u32[]{:S(2)}, u32[]{:S(2)}) collective-permute-start(bf16[2,16,2048]{2,1,0:T(8,128)(2,1)S(1)} %pad_maximum_fusion.refs_0_), channel_id=1, source_target_pairs={{0,2},{1,5},{2,0},{3,7},{4,6},{5,1},{6,4},{7,3},{8,10},{9,13},{10,... | collective-permute-start | bytes 393224 | tf_op jit(solution)/shard_map/plane0_rows00/ppermute | solution.py:246
  11.5 1.5 %collective-permute-start.3 = (bf16[2,16,2048]{2,1,0:T(8,128)(2,1)S(1)}, bf16[2,16,2048]{2,1,0:T(8,128)(2,1)S(1)}, u32[]{:S(2)}, u32[]{:S(2)}) collective-permute-start(bf16[2,16,2048]{2,1,0:T(8,128)(2,1)S(1)} %pad_maximum_fusion.refs_0_), channel_id=1, source_target_pairs={{0,4},{1,3},{2,6},{3,1},{4,0},{5,7},{6,2},{7,5},{8,12},{9,11},{10,... | collective-permute-start | bytes 393224 | tf_op jit(solution)/shard_map/plane1_rows00/ppermute | solution.py:246
  13.0 1.1 %collective-permute-done.7 = bf16[1,16,2048]{2,1,0:T(8,128)(2,1)S(1)} collective-permute-done((bf16[1,16,2048]{2,1,0:T(8,128)(2,1)S(1)}, bf16[1,16,2048]{2,1,0:T(8,128)(2,1)S(1)}, u32[]{:S(2)}, u32[]{:S(2)}) %collective-permute-start.7) | collective-permute-done | bytes 65568 | tf_op jit(solution)/shard_map/cls3_rows/ppermute | solution.py:246
  14.1 1.5 %collective-permute-start.8 = (bf16[2,16,2048]{2,1,0:T(8,128)(2,1)S(1)}, bf16[2,16,2048]{2,1,0:T(8,128)(2,1)S(1)}, u32[]{:S(2)}, u32[]{:S(2)}) collective-permute-start(bf16[2,16,2048]{2,1,0:T(8,128)(2,1)S(1)} %constant_dynamic-update-slice_fusion.refs_0_), channel_id=1, source_target_pairs={{0,2},{1,5},{2,0},{3,7},{4,6},{5,1},{6,4},{7,3},{8,10},{9,13},{10,... | collective-permute-start | bytes 393224 | tf_op jit(solution)/shard_map/plane0_rows10/ppermute | solution.py:246
  15.6 1.9 %collective-permute-start.4 = (bf16[2,16,2048]{2,1,0:T(8,128)(2,1)S(1)}, bf16[2,16,2048]{2,1,0:T(8,128)(2,1)S(1)}, u32[]{:S(2)}, u32[]{:S(2)}) collective-permute-start(bf16[2,16,2048]{2,1,0:T(8,128)(2,1)S(1)} %collective-permute-done.2.refs_1_), channel_id=1, source_target_pairs={{0,4},{1,3},{2,6},{3,1},{4,0},{5,7},{6,2},{7,5},{8,12},{9,11},{10,... | collective-permute-start | bytes 393224 | tf_op jit(solution)/shard_map/plane1_rows01/ppermute | solution.py:246
  17.6 1.7 %collective-permute-start.9 = (bf16[2,16,2048]{2,1,0:T(8,128)(2,1)S(1)}, bf16[2,16,2048]{2,1,0:T(8,128)(2,1)S(1)}, u32[]{:S(2)}, u32[]{:S(2)}) collective-permute-start(bf16[2,16,2048]{2,1,0:T(8,128)(2,1)S(1)} %constant_dynamic-update-slice_fusion.refs_0_), channel_id=1, source_target_pairs={{0,4},{1,3},{2,6},{3,1},{4,0},{5,7},{6,2},{7,5},{8,12},{9,11},{10,... | collective-permute-start | bytes 393224 | tf_op jit(solution)/shard_map/plane1_rows10/ppermute | solution.py:246
  19.3 1.0 %collective-permute-done.8.refs_1_ = bf16[2,16,2048]{2,1,0:T(8,128)(2,1)S(1)} collective-permute-done((bf16[2,16,2048]{2,1,0:T(8,128)(2,1)S(1)}, bf16[2,16,2048]{2,1,0:T(8,128)(2,1)S(1)}, u32[]{:S(2)}, u32[]{:S(2)}) %collective-permute-start.8) | collective-permute-done | bytes 131104 | tf_op jit(solution)/shard_map/plane0_rows10/ppermute | solution.py:246
  20.4 1.6 %collective-permute-start.10 = (bf16[2,16,2048]{2,1,0:T(8,128)(2,1)S(1)}, bf16[2,16,2048]{2,1,0:T(8,128)(2,1)S(1)}, u32[]{:S(2)}, u32[]{:S(2)}) collective-permute-start(bf16[2,16,2048]{2,1,0:T(8,128)(2,1)S(1)} %collective-permute-done.8.refs_1_), channel_id=1, source_target_pairs={{0,4},{1,3},{2,6},{3,1},{4,0},{5,7},{6,2},{7,5},{8,12},{9,11},{10,... | collective-permute-start | bytes 393224 | tf_op jit(solution)/shard_map/plane1_rows11/ppermute | solution.py:246
  22.0 0.8 %shard_map.62.refs_0_ = f32[64,256]{1,0:T(8,128)S(1)} custom-call(bf16[2,16,2048]{2,1,0:T(8,128)(2,1)S(1)} %pad_maximum_fusion.refs_0_, bf16[2,16,2048]{2,1,0:T(8,128)(2,1)S(1)} %collective-permute-done.2.refs_1_, bf16[2,16,2048]{2,1,0:T(8,128)(2,1)S(1)} %collective-permute-done.3.refs_2_, bf16[2,16,2048]{2,1,0:T(8,128)(2,1)S(1)} %collective-permute-done.4.refs_3_, ...), custom_call_target="tpu_custom_call" | custom-call | flops 268435456 | bytes 2097152 | tf_op jit(solution)/shard_map/pallas_call | solution.py:42
  22.9 2.4 %collective-permute-done.10.refs_3_ = bf16[2,16,2048]{2,1,0:T(8,128)(2,1)S(1)} collective-permute-done((bf16[2,16,2048]{2,1,0:T(8,128)(2,1)S(1)}, bf16[2,16,2048]{2,1,0:T(8,128)(2,1)S(1)}, u32[]{:S(2)}, u32[]{:S(2)}) %collective-permute-start.10) | collective-permute-done | bytes 131104 | tf_op jit(solution)/shard_map/plane1_rows11/ppermute | solution.py:246
  25.3 0.8 %shard_map.63.refs_1_ = f32[64,256]{1,0:T(8,128)S(1)} custom-call(bf16[2,16,2048]{2,1,0:T(8,128)(2,1)S(1)} %constant_dynamic-update-slice_fusion.refs_0_, bf16[2,16,2048]{2,1,0:T(8,128)(2,1)S(1)} %collective-permute-done.8.refs_1_, bf16[2,16,2048]{2,1,0:T(8,128)(2,1)S(1)} %collective-permute-done.9.refs_2_, ...), custom_call_target="tpu_custom_call" | custom-call | flops 1048576 | bytes 1048576 | tf_op jit(solution)/shard_map/pallas_call | solution.py:42
  26.3 1.2 %collective-permute-done.12.refs_3_ = f32[64,256]{1,0:T(8,128)S(1)} collective-permute-done((f32[64,256]{1,0:T(8,128)S(1)}, f32[64,256]{1,0:T(8,128)S(1)}, u32[]{:S(2)}, u32[]{:S(2)}) %collective-permute-start.12) | collective-permute-done | bytes 65568 | tf_op jit(solution)/shard_map/core_scores1/ppermute | solution.py:246
  27.5 0.6 %shard_map.64 = (bf16[64,256]{1,0:T(8,128)(2,1)S(1)}, f32[1,256]{1,0:T(1,128)S(1)}, bf16[4,16,2048]{2,1,0:T(8,128)(2,1)S(1)}, bf16[2,16,2048]{2,1,0:T(8,128)(2,1)S(1)}, bf16[2,16,2048]{2,1,0:T(8,128)(2,1)S(1)}) custom-call(f32[64,256]{1,0:T(8,128)S(1)} %shard_map.62.refs_0_, f32[64,256]{1,0:T(8,128)S(1)} %shard_map.63.refs_1_, ...), custom_call_target="tpu_custom_call" | custom-call | flops 268435456 | bytes 4194304 | tf_op jit(solution)/shard_map/pallas_call | solution.py:42
  28.1 1.7 %collective-permute-start.16 = (bf16[2,16,2048]{2,1,0:T(8,128)(2,1)S(1)}, bf16[2,16,2048]{2,1,0:T(8,128)(2,1)S(1)}, u32[]{:S(2)}, u32[]{:S(2)}) collective-permute-start(bf16[2,16,2048]{2,1,0:T(8,128)(2,1)S(1)} %get-tuple-element.33), channel_id=1, source_target_pairs={{0,4},{1,3},{2,6},{3,1},{4,0},{5,7},{6,2},{7,5},{8,12},{9,11},{10,... | collective-permute-start | bytes 393224 | tf_op jit(solution)/shard_map/plane1_far1/ppermute | solution.py:246
  30.7 2.5 %collective-permute-done.16 = bf16[2,16,2048]{2,1,0:T(8,128)(2,1)S(1)} collective-permute-done((bf16[2,16,2048]{2,1,0:T(8,128)(2,1)S(1)}, bf16[2,16,2048]{2,1,0:T(8,128)(2,1)S(1)}, u32[]{:S(2)}, u32[]{:S(2)}) %collective-permute-start.16) | collective-permute-done | bytes 131104 | tf_op jit(solution)/shard_map/plane1_far1/ppermute | solution.py:246
  33.1 1.5 %collective-permute-start.17 = (bf16[2,16,2048]{2,1,0:T(8,128)(2,1)S(1)}, bf16[2,16,2048]{2,1,0:T(8,128)(2,1)S(1)}, u32[]{:S(2)}, u32[]{:S(2)}) collective-permute-start(bf16[2,16,2048]{2,1,0:T(8,128)(2,1)S(1)} %add_convert_fusion.1), channel_id=1, source_target_pairs={{0,2},{1,5},{2,0},{3,7},{4,6},{5,1},{6,4},{7,3},{8,10},{9,13},{10,... | collective-permute-start | bytes 393224 | tf_op jit(solution)/shard_map/plane0_far/ppermute | solution.py:246
  34.6 0.8 %collective-permute-start.14 = (bf16[4,16,2048]{2,1,0:T(8,128)(2,1)S(1)}, bf16[4,16,2048]{2,1,0:T(8,128)(2,1)S(1)}, u32[]{:S(2)}, u32[]{:S(2)}) collective-permute-start(bf16[4,16,2048]{2,1,0:T(8,128)(2,1)S(1)} %get-tuple-element.28), channel_id=1, source_target_pairs={{0,8},{1,9},{2,10},{3,11},{4,12},{5,13},{6,14},{7,15},{8,0},{9,1},... | collective-permute-start | bytes 786440 | tf_op jit(solution)/shard_map/cls1_near/ppermute | solution.py:246
  35.4 2.8 %collective-permute-done.17 = bf16[2,16,2048]{2,1,0:T(8,128)(2,1)S(1)} collective-permute-done((bf16[2,16,2048]{2,1,0:T(8,128)(2,1)S(1)}, bf16[2,16,2048]{2,1,0:T(8,128)(2,1)S(1)}, u32[]{:S(2)}, u32[]{:S(2)}) %collective-permute-start.17) | collective-permute-done | bytes 131104 | tf_op jit(solution)/shard_map/plane0_far/ppermute | solution.py:246
  38.2 1.5 %collective-permute-start.18 = (bf16[1,16,2048]{2,1,0:T(8,128)(2,1)S(1)}, bf16[1,16,2048]{2,1,0:T(8,128)(2,1)S(1)}, u32[]{:S(2)}, u32[]{:S(2)}) collective-permute-start(bf16[1,16,2048]{2,1,0:T(8,128)(2,1)S(1)} %get-tuple-element.41), channel_id=1, source_target_pairs={{0,16},{1,17},{2,18},{3,19},{4,20},{5,21},{6,22},{7,23},{8,24},{9,... | collective-permute-start | bytes 196616 | tf_op jit(solution)/shard_map/cls2_far/ppermute | solution.py:246
  39.7 1.3 %collective-permute-start.19 = (bf16[1,16,2048]{2,1,0:T(8,128)(2,1)S(1)}, bf16[1,16,2048]{2,1,0:T(8,128)(2,1)S(1)}, u32[]{:S(2)}, u32[]{:S(2)}) collective-permute-start(bf16[1,16,2048]{2,1,0:T(8,128)(2,1)S(1)} %get-tuple-element.40), channel_id=1, source_target_pairs={{0,24},{1,25},{2,26},{3,27},{4,28},{5,29},{6,30},{7,31},{8,16},{9,... | collective-permute-start | bytes 196616 | tf_op jit(solution)/shard_map/cls3_far/ppermute | solution.py:246
  41.1 1.7 %collective-permute-done.14.refs_1_ = bf16[4,16,2048]{2,1,0:T(8,128)(2,1)S(1)} collective-permute-done((bf16[4,16,2048]{2,1,0:T(8,128)(2,1)S(1)}, bf16[4,16,2048]{2,1,0:T(8,128)(2,1)S(1)}, u32[]{:S(2)}, u32[]{:S(2)}) %collective-permute-start.14) | collective-permute-done | bytes 262176 | tf_op jit(solution)/shard_map/cls1_near/ppermute | solution.py:246
  42.8 0.7 %collective-permute-start.21 = (f32[1,16,2048]{2,1,0:T(8,128)S(1)}, f32[1,16,2048]{2,1,0:T(8,128)S(1)}, u32[]{:S(2)}, u32[]{:S(2)}) collective-permute-start(f32[1,16,2048]{2,1,0:T(8,128)S(1)} %get-tuple-element.35), channel_id=1, source_target_pairs={{0,4},{1,3},{2,6},{3,1},{4,0},{5,7},{6,2},{7,5},{8,12},{9,11},{10,... | collective-permute-start | bytes 393224 | tf_op jit(solution)/shard_map/plane_own2/ppermute | solution.py:246
  43.5 1.2 %collective-permute-start.22 = (f32[1,16,2048]{2,1,0:T(8,128)S(1)}, f32[1,16,2048]{2,1,0:T(8,128)S(1)}, u32[]{:S(2)}, u32[]{:S(2)}) collective-permute-start(f32[1,16,2048]{2,1,0:T(8,128)S(1)} %get-tuple-element.36), channel_id=1, source_target_pairs={{0,2},{1,5},{2,0},{3,7},{4,6},{5,1},{6,4},{7,3},{8,10},{9,13},{10,... | collective-permute-start | bytes 393224 | tf_op jit(solution)/shard_map/plane_own1/ppermute | solution.py:246
  44.8 1.6 %collective-permute-start.20 = (bf16[1,16,2048]{2,1,0:T(8,128)(2,1)S(1)}, bf16[1,16,2048]{2,1,0:T(8,128)(2,1)S(1)}, u32[]{:S(2)}, u32[]{:S(2)}) collective-permute-start(bf16[1,16,2048]{2,1,0:T(8,128)(2,1)S(1)} %get-tuple-element.34), channel_id=1, source_target_pairs={{0,6},{1,7},{2,4},{3,5},{4,2},{5,3},{6,0},{7,1},{8,14},{9,15},{10,... | collective-permute-start | bytes 196616 | tf_op jit(solution)/shard_map/plane_own3/ppermute | solution.py:246
  46.4 3.7 %collective-permute-done.20.refs_2_ = bf16[1,16,2048]{2,1,0:T(8,128)(2,1)S(1)} collective-permute-done((bf16[1,16,2048]{2,1,0:T(8,128)(2,1)S(1)}, bf16[1,16,2048]{2,1,0:T(8,128)(2,1)S(1)}, u32[]{:S(2)}, u32[]{:S(2)}) %collective-permute-start.20) | collective-permute-done | bytes 65568 | tf_op jit(solution)/shard_map/plane_own3/ppermute | solution.py:246
  50.8 0.7 %collective-permute-done.23.got = f32[2,4,2048]{2,1,0:T(4,128)S(1)} collective-permute-done((f32[2,4,2048]{2,1,0:T(4,128)S(1)}, f32[2,4,2048]{2,1,0:T(4,128)S(1)}, u32[]{:S(2)}, u32[]{:S(2)}) %collective-permute-start.23) | collective-permute-done | bytes 65568 | tf_op jit(solution)/shard_map/core_sums/ppermute | solution.py:246
  51.5 0.7 %shard_map.69 = f32[2,2,8192]{2,1,0:T(2,128)} custom-call(s32[1]{0:T(128)} %bitcast.core.refs_4_.refs_7_, f32[2,4,2048]{2,1,0:T(4,128)S(1)} %get-tuple-element.37.kept, f32[2,4,2048]{2,1,0:T(4,128)S(1)} %collective-permute-done.23.got), custom_call_target="tpu_custom_call" | custom-call | bytes 262144 | tf_op jit(solution)/shard_map/pallas_call | solution.py:42
  (49 shorter events, 2.5 us)
Async XLA Ops:
  0.6 1.6 %collective-permute-start = (bf16[2,2,8192]{2,1,0:T(2,128)(2,1)}, bf16[2,2,8192]{2,1,0:T(2,128)(2,1)S(1)}, u32[]{:S(2)}, u32[]{:S(2)}) collective-permute-start(bf16[2,2,8192]{2,1,0:T(2,128)(2,1)} %source.1), channel_id=1, source_target_pairs={{0,1},{1,0},{2,3},{3,2},{4,5},{5,4},{6,7},{7,6},{8,9},{9,8},{10,11... | collective-permute-start | bytes 196616 | tf_op jit(solution)/shard_map/core_rows/ppermute | solution.py:246
  1.1 0.8 %copy-start.2 = (bf16[2,2,8192]{2,1,0:T(2,128)(2,1)S(1)}, bf16[2,2,8192]{2,1,0:T(2,128)(2,1)}, u32[]{:S(2)}) copy-start(bf16[2,2,8192]{2,1,0:T(2,128)(2,1)} %source.1) | copy-start | bytes 196612
  2.0 7.7 %copy-start.3 = (bf16[128]{0:T(256)(128)(2,1)S(1)}, bf16[128]{0:T(256)(128)(2,1)}, u32[]{:S(2)}) copy-start(bf16[128]{0:T(256)(128)(2,1)} %param.6) | copy-start | bytes 772
  2.3 15.2 %copy-start.4 = (s32[128,1]{0,1:T(1,128)S(1)}, s32[128,1]{0,1:T(1,128)}, u32[]{:S(2)}) copy-start(s32[128,1]{0,1:T(1,128)} %param.5) | copy-start | bytes 1540
  2.3 7.4 %collective-permute-start.1 = (bf16[1,16,2048]{2,1,0:T(8,128)(2,1)S(1)}, bf16[1,16,2048]{2,1,0:T(8,128)(2,1)S(1)}, u32[]{:S(2)}, u32[]{:S(2)}) collective-permute-start(bf16[1,16,2048]{2,1,0:T(8,128)(2,1)S(1)} %shard_map.60), channel_id=1, source_target_pairs={{0,8},{1,9},{2,10},{3,11},{4,12},{5,13},{6,14},{7,15},{8,0},{9,1},... | collective-permute-start | bytes 196616 | tf_op jit(solution)/shard_map/cls1_rows/ppermute | solution.py:246
  5.3 7.7 %collective-permute-start.6 = (bf16[1,16,2048]{2,1,0:T(8,128)(2,1)S(1)}, bf16[1,16,2048]{2,1,0:T(8,128)(2,1)S(1)}, u32[]{:S(2)}, u32[]{:S(2)}) collective-permute-start(bf16[1,16,2048]{2,1,0:T(8,128)(2,1)S(1)} %shard_map.60), channel_id=1, source_target_pairs={{0,16},{1,17},{2,18},{3,19},{4,20},{5,21},{6,22},{7,23},{8,24},{9,... | collective-permute-start | bytes 196616 | tf_op jit(solution)/shard_map/cls2_rows/ppermute | solution.py:246
  7.9 6.2 %collective-permute-start.7 = (bf16[1,16,2048]{2,1,0:T(8,128)(2,1)S(1)}, bf16[1,16,2048]{2,1,0:T(8,128)(2,1)S(1)}, u32[]{:S(2)}, u32[]{:S(2)}) collective-permute-start(bf16[1,16,2048]{2,1,0:T(8,128)(2,1)S(1)} %shard_map.60), channel_id=1, source_target_pairs={{0,24},{1,25},{2,26},{3,27},{4,28},{5,29},{6,30},{7,31},{8,16},{9,... | collective-permute-start | bytes 196616 | tf_op jit(solution)/shard_map/cls3_rows/ppermute | solution.py:246
  7.9 1.6 %copy-start = (bf16[128,8192]{1,0:T(8,128)(2,1)S(1)}, bf16[128,8192]{1,0:T(8,128)(2,1)}, u32[]{:S(2)}) copy-start(bf16[128,8192]{1,0:T(8,128)(2,1)} %images.2) | copy-start | bytes 6291460
  9.5 12.5 %copy-start.1 = (bf16[128,8192]{1,0:T(8,128)(2,1)S(1)}, bf16[128,8192]{1,0:T(8,128)(2,1)}, u32[]{:S(2)}) copy-start(bf16[128,8192]{1,0:T(8,128)(2,1)} %images.2) | copy-start | bytes 6291460
  9.6 12.4 %collective-permute-start.5 = (bf16[128,4096]{1,0:T(8,128)(2,1)S(1)}, bf16[128,4096]{1,0:T(8,128)(2,1)S(1)}, u32[]{:S(2)}, u32[]{:S(2)}) collective-permute-start(bf16[128,4096]{1,0:T(8,128)(2,1)S(1)} %shard_map.61), channel_id=1, source_target_pairs={{0,1},{1,0},{2,3},{3,2},{4,5},{5,4},{6,7},{7,6},{8,9},{9,8},{10,11... | collective-permute-start | bytes 3145736 | tf_op jit(solution)/shard_map/core_images/ppermute | solution.py:246
  9.7 5.9 %collective-permute-start.2 = (bf16[2,16,2048]{2,1,0:T(8,128)(2,1)S(1)}, bf16[2,16,2048]{2,1,0:T(8,128)(2,1)S(1)}, u32[]{:S(2)}, u32[]{:S(2)}) collective-permute-start(bf16[2,16,2048]{2,1,0:T(8,128)(2,1)S(1)} %pad_maximum_fusion.refs_0_), channel_id=1, source_target_pairs={{0,2},{1,5},{2,0},{3,7},{4,6},{5,1},{6,4},{7,3},{8,10},{9,13},{10,... | collective-permute-start | bytes 393224 | tf_op jit(solution)/shard_map/plane0_rows00/ppermute | solution.py:246
  11.5 6.1 %collective-permute-start.3 = (bf16[2,16,2048]{2,1,0:T(8,128)(2,1)S(1)}, bf16[2,16,2048]{2,1,0:T(8,128)(2,1)S(1)}, u32[]{:S(2)}, u32[]{:S(2)}) collective-permute-start(bf16[2,16,2048]{2,1,0:T(8,128)(2,1)S(1)} %pad_maximum_fusion.refs_0_), channel_id=1, source_target_pairs={{0,4},{1,3},{2,6},{3,1},{4,0},{5,7},{6,2},{7,5},{8,12},{9,11},{10,... | collective-permute-start | bytes 393224 | tf_op jit(solution)/shard_map/plane1_rows00/ppermute | solution.py:246
  14.1 6.3 %collective-permute-start.8 = (bf16[2,16,2048]{2,1,0:T(8,128)(2,1)S(1)}, bf16[2,16,2048]{2,1,0:T(8,128)(2,1)S(1)}, u32[]{:S(2)}, u32[]{:S(2)}) collective-permute-start(bf16[2,16,2048]{2,1,0:T(8,128)(2,1)S(1)} %constant_dynamic-update-slice_fusion.refs_0_), channel_id=1, source_target_pairs={{0,2},{1,5},{2,0},{3,7},{4,6},{5,1},{6,4},{7,3},{8,10},{9,13},{10,... | collective-permute-start | bytes 393224 | tf_op jit(solution)/shard_map/plane0_rows10/ppermute | solution.py:246
  15.6 6.4 %collective-permute-start.4 = (bf16[2,16,2048]{2,1,0:T(8,128)(2,1)S(1)}, bf16[2,16,2048]{2,1,0:T(8,128)(2,1)S(1)}, u32[]{:S(2)}, u32[]{:S(2)}) collective-permute-start(bf16[2,16,2048]{2,1,0:T(8,128)(2,1)S(1)} %collective-permute-done.2.refs_1_), channel_id=1, source_target_pairs={{0,4},{1,3},{2,6},{3,1},{4,0},{5,7},{6,2},{7,5},{8,12},{9,11},{10,... | collective-permute-start | bytes 393224 | tf_op jit(solution)/shard_map/plane1_rows01/ppermute | solution.py:246
  17.5 5.4 %collective-permute-start.13 = (f32[2,128]{1,0:T(2,128)S(1)}, f32[2,128]{1,0:T(2,128)S(1)}, u32[]{:S(2)}, u32[]{:S(2)}) collective-permute-start(f32[2,128]{1,0:T(2,128)S(1)} %pad_maximum_fusion.2), channel_id=1, source_target_pairs={{0,1},{1,0},{2,3},{3,2},{4,5},{5,4},{6,7},{7,6},{8,9},{9,8},{10,11... | collective-permute-start | bytes 3080 | tf_op jit(solution)/shard_map/core_side/ppermute | solution.py:246
  17.6 7.8 %collective-permute-start.9 = (bf16[2,16,2048]{2,1,0:T(8,128)(2,1)S(1)}, bf16[2,16,2048]{2,1,0:T(8,128)(2,1)S(1)}, u32[]{:S(2)}, u32[]{:S(2)}) collective-permute-start(bf16[2,16,2048]{2,1,0:T(8,128)(2,1)S(1)} %constant_dynamic-update-slice_fusion.refs_0_), channel_id=1, source_target_pairs={{0,4},{1,3},{2,6},{3,1},{4,0},{5,7},{6,2},{7,5},{8,12},{9,11},{10,... | collective-permute-start | bytes 393224 | tf_op jit(solution)/shard_map/plane1_rows10/ppermute | solution.py:246
  20.4 5.0 %collective-permute-start.10 = (bf16[2,16,2048]{2,1,0:T(8,128)(2,1)S(1)}, bf16[2,16,2048]{2,1,0:T(8,128)(2,1)S(1)}, u32[]{:S(2)}, u32[]{:S(2)}) collective-permute-start(bf16[2,16,2048]{2,1,0:T(8,128)(2,1)S(1)} %collective-permute-done.8.refs_1_), channel_id=1, source_target_pairs={{0,4},{1,3},{2,6},{3,1},{4,0},{5,7},{6,2},{7,5},{8,12},{9,11},{10,... | collective-permute-start | bytes 393224 | tf_op jit(solution)/shard_map/plane1_rows11/ppermute | solution.py:246
  22.8 2.5 %collective-permute-start.11 = (f32[64,256]{1,0:T(8,128)S(1)}, f32[64,256]{1,0:T(8,128)S(1)}, u32[]{:S(2)}, u32[]{:S(2)}) collective-permute-start(f32[64,256]{1,0:T(8,128)S(1)} %shard_map.62.refs_0_), channel_id=1, source_target_pairs={{0,1},{1,0},{2,3},{3,2},{4,5},{5,4},{6,7},{7,6},{8,9},{9,8},{10,11... | collective-permute-start | bytes 196616 | tf_op jit(solution)/shard_map/core_scores0/ppermute | solution.py:246
  26.2 1.3 %collective-permute-start.12 = (f32[64,256]{1,0:T(8,128)S(1)}, f32[64,256]{1,0:T(8,128)S(1)}, u32[]{:S(2)}, u32[]{:S(2)}) collective-permute-start(f32[64,256]{1,0:T(8,128)S(1)} %shard_map.63.refs_1_), channel_id=1, source_target_pairs={{0,1},{1,0},{2,3},{3,2},{4,5},{5,4},{6,7},{7,6},{8,9},{9,8},{10,11... | collective-permute-start | bytes 196616 | tf_op jit(solution)/shard_map/core_scores1/ppermute | solution.py:246
  28.1 5.0 %collective-permute-start.16 = (bf16[2,16,2048]{2,1,0:T(8,128)(2,1)S(1)}, bf16[2,16,2048]{2,1,0:T(8,128)(2,1)S(1)}, u32[]{:S(2)}, u32[]{:S(2)}) collective-permute-start(bf16[2,16,2048]{2,1,0:T(8,128)(2,1)S(1)} %get-tuple-element.33), channel_id=1, source_target_pairs={{0,4},{1,3},{2,6},{3,1},{4,0},{5,7},{6,2},{7,5},{8,12},{9,11},{10,... | collective-permute-start | bytes 393224 | tf_op jit(solution)/shard_map/plane1_far1/ppermute | solution.py:246
  29.7 5.6 %collective-permute-start.15 = (bf16[2,16,2048]{2,1,0:T(8,128)(2,1)S(1)}, bf16[2,16,2048]{2,1,0:T(8,128)(2,1)S(1)}, u32[]{:S(2)}, u32[]{:S(2)}) collective-permute-start(bf16[2,16,2048]{2,1,0:T(8,128)(2,1)S(1)} %get-tuple-element.31), channel_id=1, source_target_pairs={{0,4},{1,3},{2,6},{3,1},{4,0},{5,7},{6,2},{7,5},{8,12},{9,11},{10,... | collective-permute-start | bytes 393224 | tf_op jit(solution)/shard_map/plane1_far0/ppermute | solution.py:246
  33.1 5.0 %collective-permute-start.17 = (bf16[2,16,2048]{2,1,0:T(8,128)(2,1)S(1)}, bf16[2,16,2048]{2,1,0:T(8,128)(2,1)S(1)}, u32[]{:S(2)}, u32[]{:S(2)}) collective-permute-start(bf16[2,16,2048]{2,1,0:T(8,128)(2,1)S(1)} %add_convert_fusion.1), channel_id=1, source_target_pairs={{0,2},{1,5},{2,0},{3,7},{4,6},{5,1},{6,4},{7,3},{8,10},{9,13},{10,... | collective-permute-start | bytes 393224 | tf_op jit(solution)/shard_map/plane0_far/ppermute | solution.py:246
  34.6 8.1 %collective-permute-start.14 = (bf16[4,16,2048]{2,1,0:T(8,128)(2,1)S(1)}, bf16[4,16,2048]{2,1,0:T(8,128)(2,1)S(1)}, u32[]{:S(2)}, u32[]{:S(2)}) collective-permute-start(bf16[4,16,2048]{2,1,0:T(8,128)(2,1)S(1)} %get-tuple-element.28), channel_id=1, source_target_pairs={{0,8},{1,9},{2,10},{3,11},{4,12},{5,13},{6,14},{7,15},{8,0},{9,1},... | collective-permute-start | bytes 786440 | tf_op jit(solution)/shard_map/cls1_near/ppermute | solution.py:246
  38.2 8.1 %collective-permute-start.18 = (bf16[1,16,2048]{2,1,0:T(8,128)(2,1)S(1)}, bf16[1,16,2048]{2,1,0:T(8,128)(2,1)S(1)}, u32[]{:S(2)}, u32[]{:S(2)}) collective-permute-start(bf16[1,16,2048]{2,1,0:T(8,128)(2,1)S(1)} %get-tuple-element.41), channel_id=1, source_target_pairs={{0,16},{1,17},{2,18},{3,19},{4,20},{5,21},{6,22},{7,23},{8,24},{9,... | collective-permute-start | bytes 196616 | tf_op jit(solution)/shard_map/cls2_far/ppermute | solution.py:246
  39.7 6.6 %collective-permute-start.19 = (bf16[1,16,2048]{2,1,0:T(8,128)(2,1)S(1)}, bf16[1,16,2048]{2,1,0:T(8,128)(2,1)S(1)}, u32[]{:S(2)}, u32[]{:S(2)}) collective-permute-start(bf16[1,16,2048]{2,1,0:T(8,128)(2,1)S(1)} %get-tuple-element.40), channel_id=1, source_target_pairs={{0,24},{1,25},{2,26},{3,27},{4,28},{5,29},{6,30},{7,31},{8,16},{9,... | collective-permute-start | bytes 196616 | tf_op jit(solution)/shard_map/cls3_far/ppermute | solution.py:246
  42.8 7.3 %collective-permute-start.21 = (f32[1,16,2048]{2,1,0:T(8,128)S(1)}, f32[1,16,2048]{2,1,0:T(8,128)S(1)}, u32[]{:S(2)}, u32[]{:S(2)}) collective-permute-start(f32[1,16,2048]{2,1,0:T(8,128)S(1)} %get-tuple-element.35), channel_id=1, source_target_pairs={{0,4},{1,3},{2,6},{3,1},{4,0},{5,7},{6,2},{7,5},{8,12},{9,11},{10,... | collective-permute-start | bytes 393224 | tf_op jit(solution)/shard_map/plane_own2/ppermute | solution.py:246
  43.5 6.6 %collective-permute-start.22 = (f32[1,16,2048]{2,1,0:T(8,128)S(1)}, f32[1,16,2048]{2,1,0:T(8,128)S(1)}, u32[]{:S(2)}, u32[]{:S(2)}) collective-permute-start(f32[1,16,2048]{2,1,0:T(8,128)S(1)} %get-tuple-element.36), channel_id=1, source_target_pairs={{0,2},{1,5},{2,0},{3,7},{4,6},{5,1},{6,4},{7,3},{8,10},{9,13},{10,... | collective-permute-start | bytes 393224 | tf_op jit(solution)/shard_map/plane_own1/ppermute | solution.py:246
  44.8 5.4 %collective-permute-start.20 = (bf16[1,16,2048]{2,1,0:T(8,128)(2,1)S(1)}, bf16[1,16,2048]{2,1,0:T(8,128)(2,1)S(1)}, u32[]{:S(2)}, u32[]{:S(2)}) collective-permute-start(bf16[1,16,2048]{2,1,0:T(8,128)(2,1)S(1)} %get-tuple-element.34), channel_id=1, source_target_pairs={{0,6},{1,7},{2,4},{3,5},{4,2},{5,3},{6,0},{7,1},{8,14},{9,15},{10,... | collective-permute-start | bytes 196616 | tf_op jit(solution)/shard_map/plane_own3/ppermute | solution.py:246
  50.2 1.3 %collective-permute-start.23 = (f32[2,4,2048]{2,1,0:T(4,128)S(1)}, f32[2,4,2048]{2,1,0:T(4,128)S(1)}, u32[]{:S(2)}, u32[]{:S(2)}) collective-permute-start(f32[2,4,2048]{2,1,0:T(4,128)S(1)} %get-tuple-element.38), channel_id=1, source_target_pairs={{0,1},{1,0},{2,3},{3,2},{4,5},{5,4},{6,7},{7,6},{8,9},{9,8},{10,11... | collective-permute-start | bytes 196616 | tf_op jit(solution)/shard_map/core_sums/ppermute | solution.py:246

commit v5 on v4

--- a/solution.py
+++ b/solution.py
@@ -227,7 +227,7 @@
     totals = jnp.sum(exponent, axis=0, keepdims=True)
     weights = exponent / totals
     weights = jnp.concatenate([weights[lo:hi] for lo, hi in leave], axis=0).astype(SHORT)
-    evidence[...] = largest + jnp.log(totals)
+    evidence[...] = (largest + jnp.log(totals))[:, :local]
     weights_near[...] = weights[:cut]
     weigh_rows(weights[cut:], core, images, other, outs)
 
@@ -345,7 +345,7 @@
             functools.partial(
                 softmax_body, order, places, per_owner, own, leave, cut, len(partial)
             ),
-            [((cut, 2 * local), SHORT), ((1, 2 * local), FLOAT)] + specs_go,
+            [((cut, 2 * local), SHORT), ((1, local), FLOAT)] + specs_go,
             COSTS["softmax"],
             *partial,
             *others,
@@ -411,7 +411,7 @@
             got,
             smem=(0,),
         )[0]
-        return class_sums, evidence[0, :local]
+        return class_sums, evidence.reshape(local)
 
     return jax.shard_map(
         on_device,

time: 52.4 us -> 52.9 us (level)
  transfers between devices with their start and end apart: 24 -> 24, of which waited for: 10 -> 10; matrix products, arithmetic and copies ran while one was open for 1% -> 0% of each run, Pallas kernels for 3% -> 3%
where the time goes in v5:
time: 52.9 us; the launch traced here: 52.7 us
  starting transfers between devices  27.2 us (51%)
  waiting for transfers between devices  17.9 us (34%)
  Pallas kernels  4.2 us (8%)
  local copies, waits for them, and re-layouts  2.46 us (5%)
  between operations  0.83 us (2%)
    ppermute x24, starting transfers between devices, swap(): return lax.ppermute(value, AXES, pairs)  27.2 us
    ppermute x24, waiting for transfers between devices, swap(): return lax.ppermute(value, AXES, pairs)  17.9 us
    pallas_call x11, Pallas kernels, call(): pl.pallas_call(body, out_shape=out_shape, in_specs=spaces, out_specs=[pl....  4.2 us
    unnamed x11, local copies, waits for them, and re-layouts  2.45 us
  transfers between devices with their start and end apart: 24, of which 10 were waited for; matrix products, arithmetic and copies ran while one was open for 0% of the time, Pallas kernels for 3%

profile of v5, /device:TPU:0, one launch (start us, length us, event | category | flops | bytes accessed | tf_op | source)
XLA Modules:
  0.0 52.7 jit_solution(6893717595642547407)
XLA Ops:
  0.6 0.5 collective-permute-start
  1.1 0.8 %copy-done.2 = bf16[2,2,8192]{2,1,0:T(2,128)(2,1)S(1)} copy-done((bf16[2,2,8192]{2,1,0:T(2,128)(2,1)S(1)}, bf16[2,2,8192]{2,1,0:T(2,128)(2,1)}, u32[]{:S(2)}) %copy-start.2) | copy-done | bytes 65560
  2.3 3.0 %collective-permute-start.1 = (bf16[1,16,2048]{2,1,0:T(8,128)(2,1)S(1)}, bf16[1,16,2048]{2,1,0:T(8,128)(2,1)S(1)}, u32[]{:S(2)}, u32[]{:S(2)}) collective-permute-start(bf16[1,16,2048]{2,1,0:T(8,128)(2,1)S(1)} %shard_map.60), channel_id=1, source_target_pairs={{0,8},{1,9},{2,10},{3,11},{4,12},{5,13},{6,14},{7,15},{8,0},{9,1},... | collective-permute-start | bytes 196616 | tf_op jit(solution)/shard_map/cls1_rows/ppermute | solution.py:246
  5.3 2.6 %collective-permute-start.6 = (bf16[1,16,2048]{2,1,0:T(8,128)(2,1)S(1)}, bf16[1,16,2048]{2,1,0:T(8,128)(2,1)S(1)}, u32[]{:S(2)}, u32[]{:S(2)}) collective-permute-start(bf16[1,16,2048]{2,1,0:T(8,128)(2,1)S(1)} %shard_map.60), channel_id=1, source_target_pairs={{0,16},{1,17},{2,18},{3,19},{4,20},{5,21},{6,22},{7,23},{8,24},{9,... | collective-permute-start | bytes 196616 | tf_op jit(solution)/shard_map/cls2_rows/ppermute | solution.py:246
  7.9 1.6 %copy-done = bf16[128,8192]{1,0:T(8,128)(2,1)S(1)} copy-done((bf16[128,8192]{1,0:T(8,128)(2,1)S(1)}, bf16[128,8192]{1,0:T(8,128)(2,1)}, u32[]{:S(2)}) %copy-start) | copy-done | bytes 2097176
  9.7 1.8 %collective-permute-start.2 = (bf16[2,16,2048]{2,1,0:T(8,128)(2,1)S(1)}, bf16[2,16,2048]{2,1,0:T(8,128)(2,1)S(1)}, u32[]{:S(2)}, u32[]{:S(2)}) collective-permute-start(bf16[2,16,2048]{2,1,0:T(8,128)(2,1)S(1)} %pad_maximum_fusion.refs_0_), channel_id=1, source_target_pairs={{0,2},{1,5},{2,0},{3,7},{4,6},{5,1},{6,4},{7,3},{8,10},{9,13},{10,... | collective-permute-start | bytes 393224 | tf_op jit(solution)/shard_map/plane0_rows00/ppermute | solution.py:246
  11.5 1.5 %collective-permute-start.3 = (bf16[2,16,2048]{2,1,0:T(8,128)(2,1)S(1)}, bf16[2,16,2048]{2,1,0:T(8,128)(2,1)S(1)}, u32[]{:S(2)}, u32[]{:S(2)}) collective-permute-start(bf16[2,16,2048]{2,1,0:T(8,128)(2,1)S(1)} %pad_maximum_fusion.refs_0_), channel_id=1, source_target_pairs={{0,4},{1,3},{2,6},{3,1},{4,0},{5,7},{6,2},{7,5},{8,12},{9,11},{10,... | collective-permute-start | bytes 393224 | tf_op jit(solution)/shard_map/plane1_rows00/ppermute | solution.py:246
  13.0 1.1 %collective-permute-done.7 = bf16[1,16,2048]{2,1,0:T(8,128)(2,1)S(1)} collective-permute-done((bf16[1,16,2048]{2,1,0:T(8,128)(2,1)S(1)}, bf16[1,16,2048]{2,1,0:T(8,128)(2,1)S(1)}, u32[]{:S(2)}, u32[]{:S(2)}) %collective-permute-start.7) | collective-permute-done | bytes 65568 | tf_op jit(solution)/shard_map/cls3_rows/ppermute | solution.py:246
  14.1 1.5 %collective-permute-start.8 = (bf16[2,16,2048]{2,1,0:T(8,128)(2,1)S(1)}, bf16[2,16,2048]{2,1,0:T(8,128)(2,1)S(1)}, u32[]{:S(2)}, u32[]{:S(2)}) collective-permute-start(bf16[2,16,2048]{2,1,0:T(8,128)(2,1)S(1)} %constant_dynamic-update-slice_fusion.refs_0_), channel_id=1, source_target_pairs={{0,2},{1,5},{2,0},{3,7},{4,6},{5,1},{6,4},{7,3},{8,10},{9,13},{10,... | collective-permute-start | bytes 393224 | tf_op jit(solution)/shard_map/plane0_rows10/ppermute | solution.py:246
  15.6 1.9 %collective-permute-start.4 = (bf16[2,16,2048]{2,1,0:T(8,128)(2,1)S(1)}, bf16[2,16,2048]{2,1,0:T(8,128)(2,1)S(1)}, u32[]{:S(2)}, u32[]{:S(2)}) collective-permute-start(bf16[2,16,2048]{2,1,0:T(8,128)(2,1)S(1)} %collective-permute-done.2.refs_1_), channel_id=1, source_target_pairs={{0,4},{1,3},{2,6},{3,1},{4,0},{5,7},{6,2},{7,5},{8,12},{9,11},{10,... | collective-permute-start | bytes 393224 | tf_op jit(solution)/shard_map/plane1_rows01/ppermute | solution.py:246
  17.6 1.7 %collective-permute-start.9 = (bf16[2,16,2048]{2,1,0:T(8,128)(2,1)S(1)}, bf16[2,16,2048]{2,1,0:T(8,128)(2,1)S(1)}, u32[]{:S(2)}, u32[]{:S(2)}) collective-permute-start(bf16[2,16,2048]{2,1,0:T(8,128)(2,1)S(1)} %constant_dynamic-update-slice_fusion.refs_0_), channel_id=1, source_target_pairs={{0,4},{1,3},{2,6},{3,1},{4,0},{5,7},{6,2},{7,5},{8,12},{9,11},{10,... | collective-permute-start | bytes 393224 | tf_op jit(solution)/shard_map/plane1_rows10/ppermute | solution.py:246
  19.3 1.0 %collective-permute-done.8.refs_1_ = bf16[2,16,2048]{2,1,0:T(8,128)(2,1)S(1)} collective-permute-done((bf16[2,16,2048]{2,1,0:T(8,128)(2,1)S(1)}, bf16[2,16,2048]{2,1,0:T(8,128)(2,1)S(1)}, u32[]{:S(2)}, u32[]{:S(2)}) %collective-permute-start.8) | collective-permute-done | bytes 131104 | tf_op jit(solution)/shard_map/plane0_rows10/ppermute | solution.py:246
  20.4 1.6 %collective-permute-start.10 = (bf16[2,16,2048]{2,1,0:T(8,128)(2,1)S(1)}, bf16[2,16,2048]{2,1,0:T(8,128)(2,1)S(1)}, u32[]{:S(2)}, u32[]{:S(2)}) collective-permute-start(bf16[2,16,2048]{2,1,0:T(8,128)(2,1)S(1)} %collective-permute-done.8.refs_1_), channel_id=1, source_target_pairs={{0,4},{1,3},{2,6},{3,1},{4,0},{5,7},{6,2},{7,5},{8,12},{9,11},{10,... | collective-permute-start | bytes 393224 | tf_op jit(solution)/shard_map/plane1_rows11/ppermute | solution.py:246
  22.0 0.8 %shard_map.62.refs_0_ = f32[64,256]{1,0:T(8,128)S(1)} custom-call(bf16[2,16,2048]{2,1,0:T(8,128)(2,1)S(1)} %pad_maximum_fusion.refs_0_, bf16[2,16,2048]{2,1,0:T(8,128)(2,1)S(1)} %collective-permute-done.2.refs_1_, bf16[2,16,2048]{2,1,0:T(8,128)(2,1)S(1)} %collective-permute-done.3.refs_2_, bf16[2,16,2048]{2,1,0:T(8,128)(2,1)S(1)} %collective-permute-done.4.refs_3_, ...), custom_call_target="tpu_custom_call" | custom-call | flops 268435456 | bytes 2097152 | tf_op jit(solution)/shard_map/pallas_call | solution.py:42
  22.9 2.4 %collective-permute-done.10.refs_3_ = bf16[2,16,2048]{2,1,0:T(8,128)(2,1)S(1)} collective-permute-done((bf16[2,16,2048]{2,1,0:T(8,128)(2,1)S(1)}, bf16[2,16,2048]{2,1,0:T(8,128)(2,1)S(1)}, u32[]{:S(2)}, u32[]{:S(2)}) %collective-permute-start.10) | collective-permute-done | bytes 131104 | tf_op jit(solution)/shard_map/plane1_rows11/ppermute | solution.py:246
  25.3 0.8 %shard_map.63.refs_1_ = f32[64,256]{1,0:T(8,128)S(1)} custom-call(bf16[2,16,2048]{2,1,0:T(8,128)(2,1)S(1)} %constant_dynamic-update-slice_fusion.refs_0_, bf16[2,16,2048]{2,1,0:T(8,128)(2,1)S(1)} %collective-permute-done.8.refs_1_, bf16[2,16,2048]{2,1,0:T(8,128)(2,1)S(1)} %collective-permute-done.9.refs_2_, ...), custom_call_target="tpu_custom_call" | custom-call | flops 1048576 | bytes 1048576 | tf_op jit(solution)/shard_map/pallas_call | solution.py:42
  26.3 1.2 %collective-permute-done.12.refs_3_ = f32[64,256]{1,0:T(8,128)S(1)} collective-permute-done((f32[64,256]{1,0:T(8,128)S(1)}, f32[64,256]{1,0:T(8,128)S(1)}, u32[]{:S(2)}, u32[]{:S(2)}) %collective-permute-start.12) | collective-permute-done | bytes 65568 | tf_op jit(solution)/shard_map/core_scores1/ppermute | solution.py:246
  27.5 1.1 %shard_map.64 = (bf16[64,256]{1,0:T(8,128)(2,1)S(1)}, f32[1,128]{1,0:T(1,128)}, bf16[4,16,2048]{2,1,0:T(8,128)(2,1)S(1)}, bf16[2,16,2048]{2,1,0:T(8,128)(2,1)S(1)}, bf16[2,16,2048]{2,1,0:T(8,128)(2,1)S(1)}) custom-call(f32[64,256]{1,0:T(8,128)S(1)} %shard_map.62.refs_0_, f32[64,256]{1,0:T(8,128)S(1)} %shard_map.63.refs_1_, ...), custom_call_target="tpu_custom_call" | custom-call | flops 268435456 | bytes 4194304 | tf_op jit(solution)/shard_map/pallas_call | solution.py:42
  28.6 1.6 %collective-permute-start.16 = (bf16[2,16,2048]{2,1,0:T(8,128)(2,1)S(1)}, bf16[2,16,2048]{2,1,0:T(8,128)(2,1)S(1)}, u32[]{:S(2)}, u32[]{:S(2)}) collective-permute-start(bf16[2,16,2048]{2,1,0:T(8,128)(2,1)S(1)} %get-tuple-element.33), channel_id=1, source_target_pairs={{0,4},{1,3},{2,6},{3,1},{4,0},{5,7},{6,2},{7,5},{8,12},{9,11},{10,... | collective-permute-start | bytes 393224 | tf_op jit(solution)/shard_map/plane1_far1/ppermute | solution.py:246
  31.1 2.5 %collective-permute-done.16 = bf16[2,16,2048]{2,1,0:T(8,128)(2,1)S(1)} collective-permute-done((bf16[2,16,2048]{2,1,0:T(8,128)(2,1)S(1)}, bf16[2,16,2048]{2,1,0:T(8,128)(2,1)S(1)}, u32[]{:S(2)}, u32[]{:S(2)}) %collective-permute-start.16) | collective-permute-done | bytes 131104 | tf_op jit(solution)/shard_map/plane1_far1/ppermute | solution.py:246
  33.6 1.5 %collective-permute-start.17 = (bf16[2,16,2048]{2,1,0:T(8,128)(2,1)S(1)}, bf16[2,16,2048]{2,1,0:T(8,128)(2,1)S(1)}, u32[]{:S(2)}, u32[]{:S(2)}) collective-permute-start(bf16[2,16,2048]{2,1,0:T(8,128)(2,1)S(1)} %add_convert_fusion.1), channel_id=1, source_target_pairs={{0,2},{1,5},{2,0},{3,7},{4,6},{5,1},{6,4},{7,3},{8,10},{9,13},{10,... | collective-permute-start | bytes 393224 | tf_op jit(solution)/shard_map/plane0_far/ppermute | solution.py:246
  35.1 0.8 %collective-permute-start.14 = (bf16[4,16,2048]{2,1,0:T(8,128)(2,1)S(1)}, bf16[4,16,2048]{2,1,0:T(8,128)(2,1)S(1)}, u32[]{:S(2)}, u32[]{:S(2)}) collective-permute-start(bf16[4,16,2048]{2,1,0:T(8,128)(2,1)S(1)} %get-tuple-element.28), channel_id=1, source_target_pairs={{0,8},{1,9},{2,10},{3,11},{4,12},{5,13},{6,14},{7,15},{8,0},{9,1},... | collective-permute-start | bytes 786440 | tf_op jit(solution)/shard_map/cls1_near/ppermute | solution.py:246
  35.8 2.8 %collective-permute-done.17 = bf16[2,16,2048]{2,1,0:T(8,128)(2,1)S(1)} collective-permute-done((bf16[2,16,2048]{2,1,0:T(8,128)(2,1)S(1)}, bf16[2,16,2048]{2,1,0:T(8,128)(2,1)S(1)}, u32[]{:S(2)}, u32[]{:S(2)}) %collective-permute-start.17) | collective-permute-done | bytes 131104 | tf_op jit(solution)/shard_map/plane0_far/ppermute | solution.py:246
  38.7 1.5 %collective-permute-start.18 = (bf16[1,16,2048]{2,1,0:T(8,128)(2,1)S(1)}, bf16[1,16,2048]{2,1,0:T(8,128)(2,1)S(1)}, u32[]{:S(2)}, u32[]{:S(2)}) collective-permute-start(bf16[1,16,2048]{2,1,0:T(8,128)(2,1)S(1)} %get-tuple-element.41), channel_id=1, source_target_pairs={{0,16},{1,17},{2,18},{3,19},{4,20},{5,21},{6,22},{7,23},{8,24},{9,... | collective-permute-start | bytes 196616 | tf_op jit(solution)/shard_map/cls2_far/ppermute | solution.py:246
  40.2 1.4 %collective-permute-start.19 = (bf16[1,16,2048]{2,1,0:T(8,128)(2,1)S(1)}, bf16[1,16,2048]{2,1,0:T(8,128)(2,1)S(1)}, u32[]{:S(2)}, u32[]{:S(2)}) collective-permute-start(bf16[1,16,2048]{2,1,0:T(8,128)(2,1)S(1)} %get-tuple-element.40), channel_id=1, source_target_pairs={{0,24},{1,25},{2,26},{3,27},{4,28},{5,29},{6,30},{7,31},{8,16},{9,... | collective-permute-start | bytes 196616 | tf_op jit(solution)/shard_map/cls3_far/ppermute | solution.py:246
  41.5 1.7 %collective-permute-done.14.refs_1_ = bf16[4,16,2048]{2,1,0:T(8,128)(2,1)S(1)} collective-permute-done((bf16[4,16,2048]{2,1,0:T(8,128)(2,1)S(1)}, bf16[4,16,2048]{2,1,0:T(8,128)(2,1)S(1)}, u32[]{:S(2)}, u32[]{:S(2)}) %collective-permute-start.14) | collective-permute-done | bytes 262176 | tf_op jit(solution)/shard_map/cls1_near/ppermute | solution.py:246
  43.3 0.7 %collective-permute-start.21 = (f32[1,16,2048]{2,1,0:T(8,128)S(1)}, f32[1,16,2048]{2,1,0:T(8,128)S(1)}, u32[]{:S(2)}, u32[]{:S(2)}) collective-permute-start(f32[1,16,2048]{2,1,0:T(8,128)S(1)} %get-tuple-element.35), channel_id=1, source_target_pairs={{0,4},{1,3},{2,6},{3,1},{4,0},{5,7},{6,2},{7,5},{8,12},{9,11},{10,... | collective-permute-start | bytes 393224 | tf_op jit(solution)/shard_map/plane_own2/ppermute | solution.py:246
  43.9 1.2 %collective-permute-start.22 = (f32[1,16,2048]{2,1,0:T(8,128)S(1)}, f32[1,16,2048]{2,1,0:T(8,128)S(1)}, u32[]{:S(2)}, u32[]{:S(2)}) collective-permute-start(f32[1,16,2048]{2,1,0:T(8,128)S(1)} %get-tuple-element.36), channel_id=1, source_target_pairs={{0,2},{1,5},{2,0},{3,7},{4,6},{5,1},{6,4},{7,3},{8,10},{9,13},{10,... | collective-permute-start | bytes 393224 | tf_op jit(solution)/shard_map/plane_own1/ppermute | solution.py:246
  45.2 1.6 %collective-permute-start.20 = (bf16[1,16,2048]{2,1,0:T(8,128)(2,1)S(1)}, bf16[1,16,2048]{2,1,0:T(8,128)(2,1)S(1)}, u32[]{:S(2)}, u32[]{:S(2)}) collective-permute-start(bf16[1,16,2048]{2,1,0:T(8,128)(2,1)S(1)} %get-tuple-element.34), channel_id=1, source_target_pairs={{0,6},{1,7},{2,4},{3,5},{4,2},{5,3},{6,0},{7,1},{8,14},{9,15},{10,... | collective-permute-start | bytes 196616 | tf_op jit(solution)/shard_map/plane_own3/ppermute | solution.py:246
  46.8 3.7 %collective-permute-done.20.refs_2_ = bf16[1,16,2048]{2,1,0:T(8,128)(2,1)S(1)} collective-permute-done((bf16[1,16,2048]{2,1,0:T(8,128)(2,1)S(1)}, bf16[1,16,2048]{2,1,0:T(8,128)(2,1)S(1)}, u32[]{:S(2)}, u32[]{:S(2)}) %collective-permute-start.20) | collective-permute-done | bytes 65568 | tf_op jit(solution)/shard_map/plane_own3/ppermute | solution.py:246
  50.7 1.2 %collective-permute-done.23.got = f32[2,4,2048]{2,1,0:T(4,128)S(1)} collective-permute-done((f32[2,4,2048]{2,1,0:T(4,128)S(1)}, f32[2,4,2048]{2,1,0:T(4,128)S(1)}, u32[]{:S(2)}, u32[]{:S(2)}) %collective-permute-start.23) | collective-permute-done | bytes 65568 | tf_op jit(solution)/shard_map/core_sums/ppermute | solution.py:246
  52.0 0.7 %shard_map.69 = f32[2,2,8192]{2,1,0:T(2,128)} custom-call(s32[1]{0:T(128)} %bitcast.core.refs_4_.refs_7_, f32[2,4,2048]{2,1,0:T(4,128)S(1)} %get-tuple-element.37.kept, f32[2,4,2048]{2,1,0:T(4,128)S(1)} %collective-permute-done.23.got), custom_call_target="tpu_custom_call" | custom-call | bytes 262144 | tf_op jit(solution)/shard_map/pallas_call | solution.py:42
  (48 shorter events, 2.0 us)
Async XLA Ops:
  0.6 1.6 %collective-permute-start = (bf16[2,2,8192]{2,1,0:T(2,128)(2,1)}, bf16[2,2,8192]{2,1,0:T(2,128)(2,1)S(1)}, u32[]{:S(2)}, u32[]{:S(2)}) collective-permute-start(bf16[2,2,8192]{2,1,0:T(2,128)(2,1)} %source.1), channel_id=1, source_target_pairs={{0,1},{1,0},{2,3},{3,2},{4,5},{5,4},{6,7},{7,6},{8,9},{9,8},{10,11... | collective-permute-start | bytes 196616 | tf_op jit(solution)/shard_map/core_rows/ppermute | solution.py:246
  1.1 0.8 %copy-start.2 = (bf16[2,2,8192]{2,1,0:T(2,128)(2,1)S(1)}, bf16[2,2,8192]{2,1,0:T(2,128)(2,1)}, u32[]{:S(2)}) copy-start(bf16[2,2,8192]{2,1,0:T(2,128)(2,1)} %source.1) | copy-start | bytes 196612
  2.0 7.7 %copy-start.3 = (bf16[128]{0:T(256)(128)(2,1)S(1)}, bf16[128]{0:T(256)(128)(2,1)}, u32[]{:S(2)}) copy-start(bf16[128]{0:T(256)(128)(2,1)} %param.6) | copy-start | bytes 772
  2.3 15.2 %copy-start.4 = (s32[128,1]{0,1:T(1,128)S(1)}, s32[128,1]{0,1:T(1,128)}, u32[]{:S(2)}) copy-start(s32[128,1]{0,1:T(1,128)} %param.5) | copy-start | bytes 1540
  2.3 7.4 %collective-permute-start.1 = (bf16[1,16,2048]{2,1,0:T(8,128)(2,1)S(1)}, bf16[1,16,2048]{2,1,0:T(8,128)(2,1)S(1)}, u32[]{:S(2)}, u32[]{:S(2)}) collective-permute-start(bf16[1,16,2048]{2,1,0:T(8,128)(2,1)S(1)} %shard_map.60), channel_id=1, source_target_pairs={{0,8},{1,9},{2,10},{3,11},{4,12},{5,13},{6,14},{7,15},{8,0},{9,1},... | collective-permute-start | bytes 196616 | tf_op jit(solution)/shard_map/cls1_rows/ppermute | solution.py:246
  5.3 7.7 %collective-permute-start.6 = (bf16[1,16,2048]{2,1,0:T(8,128)(2,1)S(1)}, bf16[1,16,2048]{2,1,0:T(8,128)(2,1)S(1)}, u32[]{:S(2)}, u32[]{:S(2)}) collective-permute-start(bf16[1,16,2048]{2,1,0:T(8,128)(2,1)S(1)} %shard_map.60), channel_id=1, source_target_pairs={{0,16},{1,17},{2,18},{3,19},{4,20},{5,21},{6,22},{7,23},{8,24},{9,... | collective-permute-start | bytes 196616 | tf_op jit(solution)/shard_map/cls2_rows/ppermute | solution.py:246
  7.9 6.2 %collective-permute-start.7 = (bf16[1,16,2048]{2,1,0:T(8,128)(2,1)S(1)}, bf16[1,16,2048]{2,1,0:T(8,128)(2,1)S(1)}, u32[]{:S(2)}, u32[]{:S(2)}) collective-permute-start(bf16[1,16,2048]{2,1,0:T(8,128)(2,1)S(1)} %shard_map.60), channel_id=1, source_target_pairs={{0,24},{1,25},{2,26},{3,27},{4,28},{5,29},{6,30},{7,31},{8,16},{9,... | collective-permute-start | bytes 196616 | tf_op jit(solution)/shard_map/cls3_rows/ppermute | solution.py:246
  7.9 1.6 %copy-start = (bf16[128,8192]{1,0:T(8,128)(2,1)S(1)}, bf16[128,8192]{1,0:T(8,128)(2,1)}, u32[]{:S(2)}) copy-start(bf16[128,8192]{1,0:T(8,128)(2,1)} %images.2) | copy-start | bytes 6291460
  9.5 12.5 %copy-start.1 = (bf16[128,8192]{1,0:T(8,128)(2,1)S(1)}, bf16[128,8192]{1,0:T(8,128)(2,1)}, u32[]{:S(2)}) copy-start(bf16[128,8192]{1,0:T(8,128)(2,1)} %images.2) | copy-start | bytes 6291460
  9.6 12.4 %collective-permute-start.5 = (bf16[128,4096]{1,0:T(8,128)(2,1)S(1)}, bf16[128,4096]{1,0:T(8,128)(2,1)S(1)}, u32[]{:S(2)}, u32[]{:S(2)}) collective-permute-start(bf16[128,4096]{1,0:T(8,128)(2,1)S(1)} %shard_map.61), channel_id=1, source_target_pairs={{0,1},{1,0},{2,3},{3,2},{4,5},{5,4},{6,7},{7,6},{8,9},{9,8},{10,11... | collective-permute-start | bytes 3145736 | tf_op jit(solution)/shard_map/core_images/ppermute | solution.py:246
  9.7 5.9 %collective-permute-start.2 = (bf16[2,16,2048]{2,1,0:T(8,128)(2,1)S(1)}, bf16[2,16,2048]{2,1,0:T(8,128)(2,1)S(1)}, u32[]{:S(2)}, u32[]{:S(2)}) collective-permute-start(bf16[2,16,2048]{2,1,0:T(8,128)(2,1)S(1)} %pad_maximum_fusion.refs_0_), channel_id=1, source_target_pairs={{0,2},{1,5},{2,0},{3,7},{4,6},{5,1},{6,4},{7,3},{8,10},{9,13},{10,... | collective-permute-start | bytes 393224 | tf_op jit(solution)/shard_map/plane0_rows00/ppermute | solution.py:246
  11.5 6.1 %collective-permute-start.3 = (bf16[2,16,2048]{2,1,0:T(8,128)(2,1)S(1)}, bf16[2,16,2048]{2,1,0:T(8,128)(2,1)S(1)}, u32[]{:S(2)}, u32[]{:S(2)}) collective-permute-start(bf16[2,16,2048]{2,1,0:T(8,128)(2,1)S(1)} %pad_maximum_fusion.refs_0_), channel_id=1, source_target_pairs={{0,4},{1,3},{2,6},{3,1},{4,0},{5,7},{6,2},{7,5},{8,12},{9,11},{10,... | collective-permute-start | bytes 393224 | tf_op jit(solution)/shard_map/plane1_rows00/ppermute | solution.py:246
  14.1 6.3 %collective-permute-start.8 = (bf16[2,16,2048]{2,1,0:T(8,128)(2,1)S(1)}, bf16[2,16,2048]{2,1,0:T(8,128)(2,1)S(1)}, u32[]{:S(2)}, u32[]{:S(2)}) collective-permute-start(bf16[2,16,2048]{2,1,0:T(8,128)(2,1)S(1)} %constant_dynamic-update-slice_fusion.refs_0_), channel_id=1, source_target_pairs={{0,2},{1,5},{2,0},{3,7},{4,6},{5,1},{6,4},{7,3},{8,10},{9,13},{10,... | collective-permute-start | bytes 393224 | tf_op jit(solution)/shard_map/plane0_rows10/ppermute | solution.py:246
  15.6 6.4 %collective-permute-start.4 = (bf16[2,16,2048]{2,1,0:T(8,128)(2,1)S(1)}, bf16[2,16,2048]{2,1,0:T(8,128)(2,1)S(1)}, u32[]{:S(2)}, u32[]{:S(2)}) collective-permute-start(bf16[2,16,2048]{2,1,0:T(8,128)(2,1)S(1)} %collective-permute-done.2.refs_1_), channel_id=1, source_target_pairs={{0,4},{1,3},{2,6},{3,1},{4,0},{5,7},{6,2},{7,5},{8,12},{9,11},{10,... | collective-permute-start | bytes 393224 | tf_op jit(solution)/shard_map/plane1_rows01/ppermute | solution.py:246
  17.5 5.4 %collective-permute-start.13 = (f32[2,128]{1,0:T(2,128)S(1)}, f32[2,128]{1,0:T(2,128)S(1)}, u32[]{:S(2)}, u32[]{:S(2)}) collective-permute-start(f32[2,128]{1,0:T(2,128)S(1)} %pad_maximum_fusion.2), channel_id=1, source_target_pairs={{0,1},{1,0},{2,3},{3,2},{4,5},{5,4},{6,7},{7,6},{8,9},{9,8},{10,11... | collective-permute-start | bytes 3080 | tf_op jit(solution)/shard_map/core_side/ppermute | solution.py:246
  17.6 7.8 %collective-permute-start.9 = (bf16[2,16,2048]{2,1,0:T(8,128)(2,1)S(1)}, bf16[2,16,2048]{2,1,0:T(8,128)(2,1)S(1)}, u32[]{:S(2)}, u32[]{:S(2)}) collective-permute-start(bf16[2,16,2048]{2,1,0:T(8,128)(2,1)S(1)} %constant_dynamic-update-slice_fusion.refs_0_), channel_id=1, source_target_pairs={{0,4},{1,3},{2,6},{3,1},{4,0},{5,7},{6,2},{7,5},{8,12},{9,11},{10,... | collective-permute-start | bytes 393224 | tf_op jit(solution)/shard_map/plane1_rows10/ppermute | solution.py:246
  20.4 5.0 %collective-permute-start.10 = (bf16[2,16,2048]{2,1,0:T(8,128)(2,1)S(1)}, bf16[2,16,2048]{2,1,0:T(8,128)(2,1)S(1)}, u32[]{:S(2)}, u32[]{:S(2)}) collective-permute-start(bf16[2,16,2048]{2,1,0:T(8,128)(2,1)S(1)} %collective-permute-done.8.refs_1_), channel_id=1, source_target_pairs={{0,4},{1,3},{2,6},{3,1},{4,0},{5,7},{6,2},{7,5},{8,12},{9,11},{10,... | collective-permute-start | bytes 393224 | tf_op jit(solution)/shard_map/plane1_rows11/ppermute | solution.py:246
  22.8 2.5 %collective-permute-start.11 = (f32[64,256]{1,0:T(8,128)S(1)}, f32[64,256]{1,0:T(8,128)S(1)}, u32[]{:S(2)}, u32[]{:S(2)}) collective-permute-start(f32[64,256]{1,0:T(8,128)S(1)} %shard_map.62.refs_0_), channel_id=1, source_target_pairs={{0,1},{1,0},{2,3},{3,2},{4,5},{5,4},{6,7},{7,6},{8,9},{9,8},{10,11... | collective-permute-start | bytes 196616 | tf_op jit(solution)/shard_map/core_scores0/ppermute | solution.py:246
  26.2 1.3 %collective-permute-start.12 = (f32[64,256]{1,0:T(8,128)S(1)}, f32[64,256]{1,0:T(8,128)S(1)}, u32[]{:S(2)}, u32[]{:S(2)}) collective-permute-start(f32[64,256]{1,0:T(8,128)S(1)} %shard_map.63.refs_1_), channel_id=1, source_target_pairs={{0,1},{1,0},{2,3},{3,2},{4,5},{5,4},{6,7},{7,6},{8,9},{9,8},{10,11... | collective-permute-start | bytes 196616 | tf_op jit(solution)/shard_map/core_scores1/ppermute | solution.py:246
  28.6 5.0 %collective-permute-start.16 = (bf16[2,16,2048]{2,1,0:T(8,128)(2,1)S(1)}, bf16[2,16,2048]{2,1,0:T(8,128)(2,1)S(1)}, u32[]{:S(2)}, u32[]{:S(2)}) collective-permute-start(bf16[2,16,2048]{2,1,0:T(8,128)(2,1)S(1)} %get-tuple-element.33), channel_id=1, source_target_pairs={{0,4},{1,3},{2,6},{3,1},{4,0},{5,7},{6,2},{7,5},{8,12},{9,11},{10,... | collective-permute-start | bytes 393224 | tf_op jit(solution)/shard_map/plane1_far1/ppermute | solution.py:246
  30.2 5.6 %collective-permute-start.15 = (bf16[2,16,2048]{2,1,0:T(8,128)(2,1)S(1)}, bf16[2,16,2048]{2,1,0:T(8,128)(2,1)S(1)}, u32[]{:S(2)}, u32[]{:S(2)}) collective-permute-start(bf16[2,16,2048]{2,1,0:T(8,128)(2,1)S(1)} %get-tuple-element.31), channel_id=1, source_target_pairs={{0,4},{1,3},{2,6},{3,1},{4,0},{5,7},{6,2},{7,5},{8,12},{9,11},{10,... | collective-permute-start | bytes 393224 | tf_op jit(solution)/shard_map/plane1_far0/ppermute | solution.py:246
  33.6 5.0 %collective-permute-start.17 = (bf16[2,16,2048]{2,1,0:T(8,128)(2,1)S(1)}, bf16[2,16,2048]{2,1,0:T(8,128)(2,1)S(1)}, u32[]{:S(2)}, u32[]{:S(2)}) collective-permute-start(bf16[2,16,2048]{2,1,0:T(8,128)(2,1)S(1)} %add_convert_fusion.1), channel_id=1, source_target_pairs={{0,2},{1,5},{2,0},{3,7},{4,6},{5,1},{6,4},{7,3},{8,10},{9,13},{10,... | collective-permute-start | bytes 393224 | tf_op jit(solution)/shard_map/plane0_far/ppermute | solution.py:246
  35.1 8.1 %collective-permute-start.14 = (bf16[4,16,2048]{2,1,0:T(8,128)(2,1)S(1)}, bf16[4,16,2048]{2,1,0:T(8,128)(2,1)S(1)}, u32[]{:S(2)}, u32[]{:S(2)}) collective-permute-start(bf16[4,16,2048]{2,1,0:T(8,128)(2,1)S(1)} %get-tuple-element.28), channel_id=1, source_target_pairs={{0,8},{1,9},{2,10},{3,11},{4,12},{5,13},{6,14},{7,15},{8,0},{9,1},... | collective-permute-start | bytes 786440 | tf_op jit(solution)/shard_map/cls1_near/ppermute | solution.py:246
  38.7 8.1 %collective-permute-start.18 = (bf16[1,16,2048]{2,1,0:T(8,128)(2,1)S(1)}, bf16[1,16,2048]{2,1,0:T(8,128)(2,1)S(1)}, u32[]{:S(2)}, u32[]{:S(2)}) collective-permute-start(bf16[1,16,2048]{2,1,0:T(8,128)(2,1)S(1)} %get-tuple-element.41), channel_id=1, source_target_pairs={{0,16},{1,17},{2,18},{3,19},{4,20},{5,21},{6,22},{7,23},{8,24},{9,... | collective-permute-start | bytes 196616 | tf_op jit(solution)/shard_map/cls2_far/ppermute | solution.py:246
  40.2 6.6 %collective-permute-start.19 = (bf16[1,16,2048]{2,1,0:T(8,128)(2,1)S(1)}, bf16[1,16,2048]{2,1,0:T(8,128)(2,1)S(1)}, u32[]{:S(2)}, u32[]{:S(2)}) collective-permute-start(bf16[1,16,2048]{2,1,0:T(8,128)(2,1)S(1)} %get-tuple-element.40), channel_id=1, source_target_pairs={{0,24},{1,25},{2,26},{3,27},{4,28},{5,29},{6,30},{7,31},{8,16},{9,... | collective-permute-start | bytes 196616 | tf_op jit(solution)/shard_map/cls3_far/ppermute | solution.py:246
  43.3 7.3 %collective-permute-start.21 = (f32[1,16,2048]{2,1,0:T(8,128)S(1)}, f32[1,16,2048]{2,1,0:T(8,128)S(1)}, u32[]{:S(2)}, u32[]{:S(2)}) collective-permute-start(f32[1,16,2048]{2,1,0:T(8,128)S(1)} %get-tuple-element.35), channel_id=1, source_target_pairs={{0,4},{1,3},{2,6},{3,1},{4,0},{5,7},{6,2},{7,5},{8,12},{9,11},{10,... | collective-permute-start | bytes 393224 | tf_op jit(solution)/shard_map/plane_own2/ppermute | solution.py:246
  43.9 6.6 %collective-permute-start.22 = (f32[1,16,2048]{2,1,0:T(8,128)S(1)}, f32[1,16,2048]{2,1,0:T(8,128)S(1)}, u32[]{:S(2)}, u32[]{:S(2)}) collective-permute-start(f32[1,16,2048]{2,1,0:T(8,128)S(1)} %get-tuple-element.36), channel_id=1, source_target_pairs={{0,2},{1,5},{2,0},{3,7},{4,6},{5,1},{6,4},{7,3},{8,10},{9,13},{10,... | collective-permute-start | bytes 393224 | tf_op jit(solution)/shard_map/plane_own1/ppermute | solution.py:246
  45.2 5.4 %collective-permute-start.20 = (bf16[1,16,2048]{2,1,0:T(8,128)(2,1)S(1)}, bf16[1,16,2048]{2,1,0:T(8,128)(2,1)S(1)}, u32[]{:S(2)}, u32[]{:S(2)}) collective-permute-start(bf16[1,16,2048]{2,1,0:T(8,128)(2,1)S(1)} %get-tuple-element.34), channel_id=1, source_target_pairs={{0,6},{1,7},{2,4},{3,5},{4,2},{5,3},{6,0},{7,1},{8,14},{9,15},{10,... | collective-permute-start | bytes 196616 | tf_op jit(solution)/shard_map/plane_own3/ppermute | solution.py:246
  50.6 1.3 %collective-permute-start.23 = (f32[2,4,2048]{2,1,0:T(4,128)S(1)}, f32[2,4,2048]{2,1,0:T(4,128)S(1)}, u32[]{:S(2)}, u32[]{:S(2)}) collective-permute-start(f32[2,4,2048]{2,1,0:T(4,128)S(1)} %get-tuple-element.38), channel_id=1, source_target_pairs={{0,1},{1,0},{2,3},{3,2},{4,5},{5,4},{6,7},{7,6},{8,9},{9,8},{10,11... | collective-permute-start | bytes 196616 | tf_op jit(solution)/shard_map/core_sums/ppermute | solution.py:246

commit v6 on v4

--- a/solution.py
+++ b/solution.py
@@ -13,7 +13,7 @@
 FLOAT, SHORT = jnp.float32, jnp.bfloat16
 NT = (((1,), (1,)), ((), ()))
 COSTS = {
-    "part": (1 << 30, 1 << 20),
+    "part": (1 << 32, 1 << 20),
     "near_score": (1 << 28, 1 << 21),
     "far_score": (1 << 20, 1 << 20),
     "softmax": (1 << 28, 1 << 22),

time: 52.4 us -> 52.4 us (level)
  no operation moved by 1% of the time
where the time goes in v6:
time: 52.4 us; the launch traced here: 52.2 us
  starting transfers between devices  27.2 us (52%)
  waiting for transfers between devices  17.4 us (33%)
  Pallas kernels  3.68 us (7%)
  local copies, waits for them, and re-layouts  2.98 us (6%)
  between operations  0.84 us (2%)
    ppermute x24, starting transfers between devices, swap(): return lax.ppermute(value, AXES, pairs)  27.2 us
    ppermute x24, waiting for transfers between devices, swap(): return lax.ppermute(value, AXES, pairs)  17.4 us
    pallas_call x11, Pallas kernels, call(): pl.pallas_call(body, out_shape=out_shape, in_specs=spaces, out_specs=[pl....  3.68 us
    unnamed x11, local copies, waits for them, and re-layouts  2.45 us
  transfers between devices with their start and end apart: 24, of which 10 were waited for; matrix products, arithmetic and copies ran while one was open for 1% of the time, Pallas kernels for 3%

profile of v6, /device:TPU:0, one launch (start us, length us, event | category | flops | bytes accessed | tf_op | source)
XLA Modules:
  0.0 52.2 jit_solution(1102816167571765990)
XLA Ops:
  0.6 0.5 collective-permute-start
  1.1 0.8 %copy-done.2 = bf16[2,2,8192]{2,1,0:T(2,128)(2,1)S(1)} copy-done((bf16[2,2,8192]{2,1,0:T(2,128)(2,1)S(1)}, bf16[2,2,8192]{2,1,0:T(2,128)(2,1)}, u32[]{:S(2)}) %copy-start.2) | copy-done | bytes 65560
  2.3 3.0 %collective-permute-start.1 = (bf16[1,16,2048]{2,1,0:T(8,128)(2,1)S(1)}, bf16[1,16,2048]{2,1,0:T(8,128)(2,1)S(1)}, u32[]{:S(2)}, u32[]{:S(2)}) collective-permute-start(bf16[1,16,2048]{2,1,0:T(8,128)(2,1)S(1)} %shard_map.60), channel_id=1, source_target_pairs={{0,8},{1,9},{2,10},{3,11},{4,12},{5,13},{6,14},{7,15},{8,0},{9,1},... | collective-permute-start | bytes 196616 | tf_op jit(solution)/shard_map/cls1_rows/ppermute | solution.py:246
  5.3 2.6 %collective-permute-start.6 = (bf16[1,16,2048]{2,1,0:T(8,128)(2,1)S(1)}, bf16[1,16,2048]{2,1,0:T(8,128)(2,1)S(1)}, u32[]{:S(2)}, u32[]{:S(2)}) collective-permute-start(bf16[1,16,2048]{2,1,0:T(8,128)(2,1)S(1)} %shard_map.60), channel_id=1, source_target_pairs={{0,16},{1,17},{2,18},{3,19},{4,20},{5,21},{6,22},{7,23},{8,24},{9,... | collective-permute-start | bytes 196616 | tf_op jit(solution)/shard_map/cls2_rows/ppermute | solution.py:246
  7.9 1.6 %copy-done = bf16[128,8192]{1,0:T(8,128)(2,1)S(1)} copy-done((bf16[128,8192]{1,0:T(8,128)(2,1)S(1)}, bf16[128,8192]{1,0:T(8,128)(2,1)}, u32[]{:S(2)}) %copy-start) | copy-done | bytes 2097176
  9.7 1.8 %collective-permute-start.2 = (bf16[2,16,2048]{2,1,0:T(8,128)(2,1)S(1)}, bf16[2,16,2048]{2,1,0:T(8,128)(2,1)S(1)}, u32[]{:S(2)}, u32[]{:S(2)}) collective-permute-start(bf16[2,16,2048]{2,1,0:T(8,128)(2,1)S(1)} %pad_maximum_fusion.refs_0_), channel_id=1, source_target_pairs={{0,2},{1,5},{2,0},{3,7},{4,6},{5,1},{6,4},{7,3},{8,10},{9,13},{10,... | collective-permute-start | bytes 393224 | tf_op jit(solution)/shard_map/plane0_rows00/ppermute | solution.py:246
  11.5 1.5 %collective-permute-start.3 = (bf16[2,16,2048]{2,1,0:T(8,128)(2,1)S(1)}, bf16[2,16,2048]{2,1,0:T(8,128)(2,1)S(1)}, u32[]{:S(2)}, u32[]{:S(2)}) collective-permute-start(bf16[2,16,2048]{2,1,0:T(8,128)(2,1)S(1)} %pad_maximum_fusion.refs_0_), channel_id=1, source_target_pairs={{0,4},{1,3},{2,6},{3,1},{4,0},{5,7},{6,2},{7,5},{8,12},{9,11},{10,... | collective-permute-start | bytes 393224 | tf_op jit(solution)/shard_map/plane1_rows00/ppermute | solution.py:246
  13.0 1.1 %collective-permute-done.7 = bf16[1,16,2048]{2,1,0:T(8,128)(2,1)S(1)} collective-permute-done((bf16[1,16,2048]{2,1,0:T(8,128)(2,1)S(1)}, bf16[1,16,2048]{2,1,0:T(8,128)(2,1)S(1)}, u32[]{:S(2)}, u32[]{:S(2)}) %collective-permute-start.7) | collective-permute-done | bytes 65568 | tf_op jit(solution)/shard_map/cls3_rows/ppermute | solution.py:246
  14.1 1.5 %collective-permute-start.8 = (bf16[2,16,2048]{2,1,0:T(8,128)(2,1)S(1)}, bf16[2,16,2048]{2,1,0:T(8,128)(2,1)S(1)}, u32[]{:S(2)}, u32[]{:S(2)}) collective-permute-start(bf16[2,16,2048]{2,1,0:T(8,128)(2,1)S(1)} %constant_dynamic-update-slice_fusion.refs_0_), channel_id=1, source_target_pairs={{0,2},{1,5},{2,0},{3,7},{4,6},{5,1},{6,4},{7,3},{8,10},{9,13},{10,... | collective-permute-start | bytes 393224 | tf_op jit(solution)/shard_map/plane0_rows10/ppermute | solution.py:246
  15.6 1.9 %collective-permute-start.4 = (bf16[2,16,2048]{2,1,0:T(8,128)(2,1)S(1)}, bf16[2,16,2048]{2,1,0:T(8,128)(2,1)S(1)}, u32[]{:S(2)}, u32[]{:S(2)}) collective-permute-start(bf16[2,16,2048]{2,1,0:T(8,128)(2,1)S(1)} %collective-permute-done.2.refs_1_), channel_id=1, source_target_pairs={{0,4},{1,3},{2,6},{3,1},{4,0},{5,7},{6,2},{7,5},{8,12},{9,11},{10,... | collective-permute-start | bytes 393224 | tf_op jit(solution)/shard_map/plane1_rows01/ppermute | solution.py:246
  17.6 1.7 %collective-permute-start.9 = (bf16[2,16,2048]{2,1,0:T(8,128)(2,1)S(1)}, bf16[2,16,2048]{2,1,0:T(8,128)(2,1)S(1)}, u32[]{:S(2)}, u32[]{:S(2)}) collective-permute-start(bf16[2,16,2048]{2,1,0:T(8,128)(2,1)S(1)} %constant_dynamic-update-slice_fusion.refs_0_), channel_id=1, source_target_pairs={{0,4},{1,3},{2,6},{3,1},{4,0},{5,7},{6,2},{7,5},{8,12},{9,11},{10,... | collective-permute-start | bytes 393224 | tf_op jit(solution)/shard_map/plane1_rows10/ppermute | solution.py:246
  19.3 1.0 %collective-permute-done.8.refs_1_ = bf16[2,16,2048]{2,1,0:T(8,128)(2,1)S(1)} collective-permute-done((bf16[2,16,2048]{2,1,0:T(8,128)(2,1)S(1)}, bf16[2,16,2048]{2,1,0:T(8,128)(2,1)S(1)}, u32[]{:S(2)}, u32[]{:S(2)}) %collective-permute-start.8) | collective-permute-done | bytes 131104 | tf_op jit(solution)/shard_map/plane0_rows10/ppermute | solution.py:246
  20.4 1.6 %collective-permute-start.10 = (bf16[2,16,2048]{2,1,0:T(8,128)(2,1)S(1)}, bf16[2,16,2048]{2,1,0:T(8,128)(2,1)S(1)}, u32[]{:S(2)}, u32[]{:S(2)}) collective-permute-start(bf16[2,16,2048]{2,1,0:T(8,128)(2,1)S(1)} %collective-permute-done.8.refs_1_), channel_id=1, source_target_pairs={{0,4},{1,3},{2,6},{3,1},{4,0},{5,7},{6,2},{7,5},{8,12},{9,11},{10,... | collective-permute-start | bytes 393224 | tf_op jit(solution)/shard_map/plane1_rows11/ppermute | solution.py:246
  22.0 0.8 %shard_map.62.refs_0_ = f32[64,256]{1,0:T(8,128)S(1)} custom-call(bf16[2,16,2048]{2,1,0:T(8,128)(2,1)S(1)} %pad_maximum_fusion.refs_0_, bf16[2,16,2048]{2,1,0:T(8,128)(2,1)S(1)} %collective-permute-done.2.refs_1_, bf16[2,16,2048]{2,1,0:T(8,128)(2,1)S(1)} %collective-permute-done.3.refs_2_, bf16[2,16,2048]{2,1,0:T(8,128)(2,1)S(1)} %collective-permute-done.4.refs_3_, ...), custom_call_target="tpu_custom_call" | custom-call | flops 268435456 | bytes 2097152 | tf_op jit(solution)/shard_map/pallas_call | solution.py:42
  22.9 2.4 %collective-permute-done.10.refs_3_ = bf16[2,16,2048]{2,1,0:T(8,128)(2,1)S(1)} collective-permute-done((bf16[2,16,2048]{2,1,0:T(8,128)(2,1)S(1)}, bf16[2,16,2048]{2,1,0:T(8,128)(2,1)S(1)}, u32[]{:S(2)}, u32[]{:S(2)}) %collective-permute-start.10) | collective-permute-done | bytes 131104 | tf_op jit(solution)/shard_map/plane1_rows11/ppermute | solution.py:246
  25.3 0.8 %shard_map.63.refs_1_ = f32[64,256]{1,0:T(8,128)S(1)} custom-call(bf16[2,16,2048]{2,1,0:T(8,128)(2,1)S(1)} %constant_dynamic-update-slice_fusion.refs_0_, bf16[2,16,2048]{2,1,0:T(8,128)(2,1)S(1)} %collective-permute-done.8.refs_1_, bf16[2,16,2048]{2,1,0:T(8,128)(2,1)S(1)} %collective-permute-done.9.refs_2_, ...), custom_call_target="tpu_custom_call" | custom-call | flops 1048576 | bytes 1048576 | tf_op jit(solution)/shard_map/pallas_call | solution.py:42
  26.3 1.2 %collective-permute-done.12.refs_3_ = f32[64,256]{1,0:T(8,128)S(1)} collective-permute-done((f32[64,256]{1,0:T(8,128)S(1)}, f32[64,256]{1,0:T(8,128)S(1)}, u32[]{:S(2)}, u32[]{:S(2)}) %collective-permute-start.12) | collective-permute-done | bytes 65568 | tf_op jit(solution)/shard_map/core_scores1/ppermute | solution.py:246
  27.5 0.6 %shard_map.64 = (bf16[64,256]{1,0:T(8,128)(2,1)S(1)}, f32[1,256]{1,0:T(1,128)S(1)}, bf16[4,16,2048]{2,1,0:T(8,128)(2,1)S(1)}, bf16[2,16,2048]{2,1,0:T(8,128)(2,1)S(1)}, bf16[2,16,2048]{2,1,0:T(8,128)(2,1)S(1)}) custom-call(f32[64,256]{1,0:T(8,128)S(1)} %shard_map.62.refs_0_, f32[64,256]{1,0:T(8,128)S(1)} %shard_map.63.refs_1_, ...), custom_call_target="tpu_custom_call" | custom-call | flops 268435456 | bytes 4194304 | tf_op jit(solution)/shard_map/pallas_call | solution.py:42
  28.1 1.7 %collective-permute-start.16 = (bf16[2,16,2048]{2,1,0:T(8,128)(2,1)S(1)}, bf16[2,16,2048]{2,1,0:T(8,128)(2,1)S(1)}, u32[]{:S(2)}, u32[]{:S(2)}) collective-permute-start(bf16[2,16,2048]{2,1,0:T(8,128)(2,1)S(1)} %get-tuple-element.33), channel_id=1, source_target_pairs={{0,4},{1,3},{2,6},{3,1},{4,0},{5,7},{6,2},{7,5},{8,12},{9,11},{10,... | collective-permute-start | bytes 393224 | tf_op jit(solution)/shard_map/plane1_far1/ppermute | solution.py:246
  30.7 2.4 %collective-permute-done.16 = bf16[2,16,2048]{2,1,0:T(8,128)(2,1)S(1)} collective-permute-done((bf16[2,16,2048]{2,1,0:T(8,128)(2,1)S(1)}, bf16[2,16,2048]{2,1,0:T(8,128)(2,1)S(1)}, u32[]{:S(2)}, u32[]{:S(2)}) %collective-permute-start.16) | collective-permute-done | bytes 131104 | tf_op jit(solution)/shard_map/plane1_far1/ppermute | solution.py:246
  33.1 1.5 %collective-permute-start.17 = (bf16[2,16,2048]{2,1,0:T(8,128)(2,1)S(1)}, bf16[2,16,2048]{2,1,0:T(8,128)(2,1)S(1)}, u32[]{:S(2)}, u32[]{:S(2)}) collective-permute-start(bf16[2,16,2048]{2,1,0:T(8,128)(2,1)S(1)} %add_convert_fusion.1), channel_id=1, source_target_pairs={{0,2},{1,5},{2,0},{3,7},{4,6},{5,1},{6,4},{7,3},{8,10},{9,13},{10,... | collective-permute-start | bytes 393224 | tf_op jit(solution)/shard_map/plane0_far/ppermute | solution.py:246
  34.6 0.8 %collective-permute-start.14 = (bf16[4,16,2048]{2,1,0:T(8,128)(2,1)S(1)}, bf16[4,16,2048]{2,1,0:T(8,128)(2,1)S(1)}, u32[]{:S(2)}, u32[]{:S(2)}) collective-permute-start(bf16[4,16,2048]{2,1,0:T(8,128)(2,1)S(1)} %get-tuple-element.28), channel_id=1, source_target_pairs={{0,8},{1,9},{2,10},{3,11},{4,12},{5,13},{6,14},{7,15},{8,0},{9,1},... | collective-permute-start | bytes 786440 | tf_op jit(solution)/shard_map/cls1_near/ppermute | solution.py:246
  35.4 2.8 %collective-permute-done.17 = bf16[2,16,2048]{2,1,0:T(8,128)(2,1)S(1)} collective-permute-done((bf16[2,16,2048]{2,1,0:T(8,128)(2,1)S(1)}, bf16[2,16,2048]{2,1,0:T(8,128)(2,1)S(1)}, u32[]{:S(2)}, u32[]{:S(2)}) %collective-permute-start.17) | collective-permute-done | bytes 131104 | tf_op jit(solution)/shard_map/plane0_far/ppermute | solution.py:246
  38.2 1.5 %collective-permute-start.18 = (bf16[1,16,2048]{2,1,0:T(8,128)(2,1)S(1)}, bf16[1,16,2048]{2,1,0:T(8,128)(2,1)S(1)}, u32[]{:S(2)}, u32[]{:S(2)}) collective-permute-start(bf16[1,16,2048]{2,1,0:T(8,128)(2,1)S(1)} %get-tuple-element.41), channel_id=1, source_target_pairs={{0,16},{1,17},{2,18},{3,19},{4,20},{5,21},{6,22},{7,23},{8,24},{9,... | collective-permute-start | bytes 196616 | tf_op jit(solution)/shard_map/cls2_far/ppermute | solution.py:246
  39.7 1.3 %collective-permute-start.19 = (bf16[1,16,2048]{2,1,0:T(8,128)(2,1)S(1)}, bf16[1,16,2048]{2,1,0:T(8,128)(2,1)S(1)}, u32[]{:S(2)}, u32[]{:S(2)}) collective-permute-start(bf16[1,16,2048]{2,1,0:T(8,128)(2,1)S(1)} %get-tuple-element.40), channel_id=1, source_target_pairs={{0,24},{1,25},{2,26},{3,27},{4,28},{5,29},{6,30},{7,31},{8,16},{9,... | collective-permute-start | bytes 196616 | tf_op jit(solution)/shard_map/cls3_far/ppermute | solution.py:246
  41.1 1.7 %collective-permute-done.14.refs_1_ = bf16[4,16,2048]{2,1,0:T(8,128)(2,1)S(1)} collective-permute-done((bf16[4,16,2048]{2,1,0:T(8,128)(2,1)S(1)}, bf16[4,16,2048]{2,1,0:T(8,128)(2,1)S(1)}, u32[]{:S(2)}, u32[]{:S(2)}) %collective-permute-start.14) | collective-permute-done | bytes 262176 | tf_op jit(solution)/shard_map/cls1_near/ppermute | solution.py:246
  42.8 0.7 %collective-permute-start.21 = (f32[1,16,2048]{2,1,0:T(8,128)S(1)}, f32[1,16,2048]{2,1,0:T(8,128)S(1)}, u32[]{:S(2)}, u32[]{:S(2)}) collective-permute-start(f32[1,16,2048]{2,1,0:T(8,128)S(1)} %get-tuple-element.35), channel_id=1, source_target_pairs={{0,4},{1,3},{2,6},{3,1},{4,0},{5,7},{6,2},{7,5},{8,12},{9,11},{10,... | collective-permute-start | bytes 393224 | tf_op jit(solution)/shard_map/plane_own2/ppermute | solution.py:246
  43.5 1.2 %collective-permute-start.22 = (f32[1,16,2048]{2,1,0:T(8,128)S(1)}, f32[1,16,2048]{2,1,0:T(8,128)S(1)}, u32[]{:S(2)}, u32[]{:S(2)}) collective-permute-start(f32[1,16,2048]{2,1,0:T(8,128)S(1)} %get-tuple-element.36), channel_id=1, source_target_pairs={{0,2},{1,5},{2,0},{3,7},{4,6},{5,1},{6,4},{7,3},{8,10},{9,13},{10,... | collective-permute-start | bytes 393224 | tf_op jit(solution)/shard_map/plane_own1/ppermute | solution.py:246
  44.8 1.6 %collective-permute-start.20 = (bf16[1,16,2048]{2,1,0:T(8,128)(2,1)S(1)}, bf16[1,16,2048]{2,1,0:T(8,128)(2,1)S(1)}, u32[]{:S(2)}, u32[]{:S(2)}) collective-permute-start(bf16[1,16,2048]{2,1,0:T(8,128)(2,1)S(1)} %get-tuple-element.34), channel_id=1, source_target_pairs={{0,6},{1,7},{2,4},{3,5},{4,2},{5,3},{6,0},{7,1},{8,14},{9,15},{10,... | collective-permute-start | bytes 196616 | tf_op jit(solution)/shard_map/plane_own3/ppermute | solution.py:246
  46.4 3.7 %collective-permute-done.20.refs_2_ = bf16[1,16,2048]{2,1,0:T(8,128)(2,1)S(1)} collective-permute-done((bf16[1,16,2048]{2,1,0:T(8,128)(2,1)S(1)}, bf16[1,16,2048]{2,1,0:T(8,128)(2,1)S(1)}, u32[]{:S(2)}, u32[]{:S(2)}) %collective-permute-start.20) | collective-permute-done | bytes 65568 | tf_op jit(solution)/shard_map/plane_own3/ppermute | solution.py:246
  50.8 0.7 %collective-permute-done.23.got = f32[2,4,2048]{2,1,0:T(4,128)S(1)} collective-permute-done((f32[2,4,2048]{2,1,0:T(4,128)S(1)}, f32[2,4,2048]{2,1,0:T(4,128)S(1)}, u32[]{:S(2)}, u32[]{:S(2)}) %collective-permute-start.23) | collective-permute-done | bytes 65568 | tf_op jit(solution)/shard_map/core_sums/ppermute | solution.py:246
  51.5 0.7 %shard_map.69 = f32[2,2,8192]{2,1,0:T(2,128)} custom-call(s32[1]{0:T(128)} %bitcast.core.refs_4_.refs_7_, f32[2,4,2048]{2,1,0:T(4,128)S(1)} %get-tuple-element.37.kept, f32[2,4,2048]{2,1,0:T(4,128)S(1)} %collective-permute-done.23.got), custom_call_target="tpu_custom_call" | custom-call | bytes 262144 | tf_op jit(solution)/shard_map/pallas_call | solution.py:42
  (49 shorter events, 2.5 us)
Async XLA Ops:
  0.6 1.6 %collective-permute-start = (bf16[2,2,8192]{2,1,0:T(2,128)(2,1)}, bf16[2,2,8192]{2,1,0:T(2,128)(2,1)S(1)}, u32[]{:S(2)}, u32[]{:S(2)}) collective-permute-start(bf16[2,2,8192]{2,1,0:T(2,128)(2,1)} %source.1), channel_id=1, source_target_pairs={{0,1},{1,0},{2,3},{3,2},{4,5},{5,4},{6,7},{7,6},{8,9},{9,8},{10,11... | collective-permute-start | bytes 196616 | tf_op jit(solution)/shard_map/core_rows/ppermute | solution.py:246
  1.1 0.8 %copy-start.2 = (bf16[2,2,8192]{2,1,0:T(2,128)(2,1)S(1)}, bf16[2,2,8192]{2,1,0:T(2,128)(2,1)}, u32[]{:S(2)}) copy-start(bf16[2,2,8192]{2,1,0:T(2,128)(2,1)} %source.1) | copy-start | bytes 196612
  2.3 7.4 %copy-start.3 = (bf16[128]{0:T(256)(128)(2,1)S(1)}, bf16[128]{0:T(256)(128)(2,1)}, u32[]{:S(2)}) copy-start(bf16[128]{0:T(256)(128)(2,1)} %param.6) | copy-start | bytes 772
  2.3 15.2 %copy-start.4 = (s32[128,1]{0,1:T(1,128)S(1)}, s32[128,1]{0,1:T(1,128)}, u32[]{:S(2)}) copy-start(s32[128,1]{0,1:T(1,128)} %param.5) | copy-start | bytes 1540
  2.3 7.4 %collective-permute-start.1 = (bf16[1,16,2048]{2,1,0:T(8,128)(2,1)S(1)}, bf16[1,16,2048]{2,1,0:T(8,128)(2,1)S(1)}, u32[]{:S(2)}, u32[]{:S(2)}) collective-permute-start(bf16[1,16,2048]{2,1,0:T(8,128)(2,1)S(1)} %shard_map.60), channel_id=1, source_target_pairs={{0,8},{1,9},{2,10},{3,11},{4,12},{5,13},{6,14},{7,15},{8,0},{9,1},... | collective-permute-start | bytes 196616 | tf_op jit(solution)/shard_map/cls1_rows/ppermute | solution.py:246
  5.3 7.7 %collective-permute-start.6 = (bf16[1,16,2048]{2,1,0:T(8,128)(2,1)S(1)}, bf16[1,16,2048]{2,1,0:T(8,128)(2,1)S(1)}, u32[]{:S(2)}, u32[]{:S(2)}) collective-permute-start(bf16[1,16,2048]{2,1,0:T(8,128)(2,1)S(1)} %shard_map.60), channel_id=1, source_target_pairs={{0,16},{1,17},{2,18},{3,19},{4,20},{5,21},{6,22},{7,23},{8,24},{9,... | collective-permute-start | bytes 196616 | tf_op jit(solution)/shard_map/cls2_rows/ppermute | solution.py:246
  7.9 6.2 %collective-permute-start.7 = (bf16[1,16,2048]{2,1,0:T(8,128)(2,1)S(1)}, bf16[1,16,2048]{2,1,0:T(8,128)(2,1)S(1)}, u32[]{:S(2)}, u32[]{:S(2)}) collective-permute-start(bf16[1,16,2048]{2,1,0:T(8,128)(2,1)S(1)} %shard_map.60), channel_id=1, source_target_pairs={{0,24},{1,25},{2,26},{3,27},{4,28},{5,29},{6,30},{7,31},{8,16},{9,... | collective-permute-start | bytes 196616 | tf_op jit(solution)/shard_map/cls3_rows/ppermute | solution.py:246
  7.9 1.6 %copy-start = (bf16[128,8192]{1,0:T(8,128)(2,1)S(1)}, bf16[128,8192]{1,0:T(8,128)(2,1)}, u32[]{:S(2)}) copy-start(bf16[128,8192]{1,0:T(8,128)(2,1)} %images.2) | copy-start | bytes 6291460
  9.5 12.5 %copy-start.1 = (bf16[128,8192]{1,0:T(8,128)(2,1)S(1)}, bf16[128,8192]{1,0:T(8,128)(2,1)}, u32[]{:S(2)}) copy-start(bf16[128,8192]{1,0:T(8,128)(2,1)} %images.2) | copy-start | bytes 6291460
  9.6 12.4 %collective-permute-start.5 = (bf16[128,4096]{1,0:T(8,128)(2,1)S(1)}, bf16[128,4096]{1,0:T(8,128)(2,1)S(1)}, u32[]{:S(2)}, u32[]{:S(2)}) collective-permute-start(bf16[128,4096]{1,0:T(8,128)(2,1)S(1)} %shard_map.61), channel_id=1, source_target_pairs={{0,1},{1,0},{2,3},{3,2},{4,5},{5,4},{6,7},{7,6},{8,9},{9,8},{10,11... | collective-permute-start | bytes 3145736 | tf_op jit(solution)/shard_map/core_images/ppermute | solution.py:246
  9.7 5.9 %collective-permute-start.2 = (bf16[2,16,2048]{2,1,0:T(8,128)(2,1)S(1)}, bf16[2,16,2048]{2,1,0:T(8,128)(2,1)S(1)}, u32[]{:S(2)}, u32[]{:S(2)}) collective-permute-start(bf16[2,16,2048]{2,1,0:T(8,128)(2,1)S(1)} %pad_maximum_fusion.refs_0_), channel_id=1, source_target_pairs={{0,2},{1,5},{2,0},{3,7},{4,6},{5,1},{6,4},{7,3},{8,10},{9,13},{10,... | collective-permute-start | bytes 393224 | tf_op jit(solution)/shard_map/plane0_rows00/ppermute | solution.py:246
  11.5 6.1 %collective-permute-start.3 = (bf16[2,16,2048]{2,1,0:T(8,128)(2,1)S(1)}, bf16[2,16,2048]{2,1,0:T(8,128)(2,1)S(1)}, u32[]{:S(2)}, u32[]{:S(2)}) collective-permute-start(bf16[2,16,2048]{2,1,0:T(8,128)(2,1)S(1)} %pad_maximum_fusion.refs_0_), channel_id=1, source_target_pairs={{0,4},{1,3},{2,6},{3,1},{4,0},{5,7},{6,2},{7,5},{8,12},{9,11},{10,... | collective-permute-start | bytes 393224 | tf_op jit(solution)/shard_map/plane1_rows00/ppermute | solution.py:246
  14.1 6.3 %collective-permute-start.8 = (bf16[2,16,2048]{2,1,0:T(8,128)(2,1)S(1)}, bf16[2,16,2048]{2,1,0:T(8,128)(2,1)S(1)}, u32[]{:S(2)}, u32[]{:S(2)}) collective-permute-start(bf16[2,16,2048]{2,1,0:T(8,128)(2,1)S(1)} %constant_dynamic-update-slice_fusion.refs_0_), channel_id=1, source_target_pairs={{0,2},{1,5},{2,0},{3,7},{4,6},{5,1},{6,4},{7,3},{8,10},{9,13},{10,... | collective-permute-start | bytes 393224 | tf_op jit(solution)/shard_map/plane0_rows10/ppermute | solution.py:246
  15.6 6.4 %collective-permute-start.4 = (bf16[2,16,2048]{2,1,0:T(8,128)(2,1)S(1)}, bf16[2,16,2048]{2,1,0:T(8,128)(2,1)S(1)}, u32[]{:S(2)}, u32[]{:S(2)}) collective-permute-start(bf16[2,16,2048]{2,1,0:T(8,128)(2,1)S(1)} %collective-permute-done.2.refs_1_), channel_id=1, source_target_pairs={{0,4},{1,3},{2,6},{3,1},{4,0},{5,7},{6,2},{7,5},{8,12},{9,11},{10,... | collective-permute-start | bytes 393224 | tf_op jit(solution)/shard_map/plane1_rows01/ppermute | solution.py:246
  17.5 5.4 %collective-permute-start.13 = (f32[2,128]{1,0:T(2,128)S(1)}, f32[2,128]{1,0:T(2,128)S(1)}, u32[]{:S(2)}, u32[]{:S(2)}) collective-permute-start(f32[2,128]{1,0:T(2,128)S(1)} %pad_maximum_fusion.2), channel_id=1, source_target_pairs={{0,1},{1,0},{2,3},{3,2},{4,5},{5,4},{6,7},{7,6},{8,9},{9,8},{10,11... | collective-permute-start | bytes 3080 | tf_op jit(solution)/shard_map/core_side/ppermute | solution.py:246
  17.6 7.8 %collective-permute-start.9 = (bf16[2,16,2048]{2,1,0:T(8,128)(2,1)S(1)}, bf16[2,16,2048]{2,1,0:T(8,128)(2,1)S(1)}, u32[]{:S(2)}, u32[]{:S(2)}) collective-permute-start(bf16[2,16,2048]{2,1,0:T(8,128)(2,1)S(1)} %constant_dynamic-update-slice_fusion.refs_0_), channel_id=1, source_target_pairs={{0,4},{1,3},{2,6},{3,1},{4,0},{5,7},{6,2},{7,5},{8,12},{9,11},{10,... | collective-permute-start | bytes 393224 | tf_op jit(solution)/shard_map/plane1_rows10/ppermute | solution.py:246
  20.4 5.0 %collective-permute-start.10 = (bf16[2,16,2048]{2,1,0:T(8,128)(2,1)S(1)}, bf16[2,16,2048]{2,1,0:T(8,128)(2,1)S(1)}, u32[]{:S(2)}, u32[]{:S(2)}) collective-permute-start(bf16[2,16,2048]{2,1,0:T(8,128)(2,1)S(1)} %collective-permute-done.8.refs_1_), channel_id=1, source_target_pairs={{0,4},{1,3},{2,6},{3,1},{4,0},{5,7},{6,2},{7,5},{8,12},{9,11},{10,... | collective-permute-start | bytes 393224 | tf_op jit(solution)/shard_map/plane1_rows11/ppermute | solution.py:246
  22.8 2.5 %collective-permute-start.11 = (f32[64,256]{1,0:T(8,128)S(1)}, f32[64,256]{1,0:T(8,128)S(1)}, u32[]{:S(2)}, u32[]{:S(2)}) collective-permute-start(f32[64,256]{1,0:T(8,128)S(1)} %shard_map.62.refs_0_), channel_id=1, source_target_pairs={{0,1},{1,0},{2,3},{3,2},{4,5},{5,4},{6,7},{7,6},{8,9},{9,8},{10,11... | collective-permute-start | bytes 196616 | tf_op jit(solution)/shard_map/core_scores0/ppermute | solution.py:246
  26.2 1.3 %collective-permute-start.12 = (f32[64,256]{1,0:T(8,128)S(1)}, f32[64,256]{1,0:T(8,128)S(1)}, u32[]{:S(2)}, u32[]{:S(2)}) collective-permute-start(f32[64,256]{1,0:T(8,128)S(1)} %shard_map.63.refs_1_), channel_id=1, source_target_pairs={{0,1},{1,0},{2,3},{3,2},{4,5},{5,4},{6,7},{7,6},{8,9},{9,8},{10,11... | collective-permute-start | bytes 196616 | tf_op jit(solution)/shard_map/core_scores1/ppermute | solution.py:246
  28.1 5.0 %collective-permute-start.16 = (bf16[2,16,2048]{2,1,0:T(8,128)(2,1)S(1)}, bf16[2,16,2048]{2,1,0:T(8,128)(2,1)S(1)}, u32[]{:S(2)}, u32[]{:S(2)}) collective-permute-start(bf16[2,16,2048]{2,1,0:T(8,128)(2,1)S(1)} %get-tuple-element.33), channel_id=1, source_target_pairs={{0,4},{1,3},{2,6},{3,1},{4,0},{5,7},{6,2},{7,5},{8,12},{9,11},{10,... | collective-permute-start | bytes 393224 | tf_op jit(solution)/shard_map/plane1_far1/ppermute | solution.py:246
  29.7 5.6 %collective-permute-start.15 = (bf16[2,16,2048]{2,1,0:T(8,128)(2,1)S(1)}, bf16[2,16,2048]{2,1,0:T(8,128)(2,1)S(1)}, u32[]{:S(2)}, u32[]{:S(2)}) collective-permute-start(bf16[2,16,2048]{2,1,0:T(8,128)(2,1)S(1)} %get-tuple-element.31), channel_id=1, source_target_pairs={{0,4},{1,3},{2,6},{3,1},{4,0},{5,7},{6,2},{7,5},{8,12},{9,11},{10,... | collective-permute-start | bytes 393224 | tf_op jit(solution)/shard_map/plane1_far0/ppermute | solution.py:246
  33.1 5.0 %collective-permute-start.17 = (bf16[2,16,2048]{2,1,0:T(8,128)(2,1)S(1)}, bf16[2,16,2048]{2,1,0:T(8,128)(2,1)S(1)}, u32[]{:S(2)}, u32[]{:S(2)}) collective-permute-start(bf16[2,16,2048]{2,1,0:T(8,128)(2,1)S(1)} %add_convert_fusion.1), channel_id=1, source_target_pairs={{0,2},{1,5},{2,0},{3,7},{4,6},{5,1},{6,4},{7,3},{8,10},{9,13},{10,... | collective-permute-start | bytes 393224 | tf_op jit(solution)/shard_map/plane0_far/ppermute | solution.py:246
  34.6 8.1 %collective-permute-start.14 = (bf16[4,16,2048]{2,1,0:T(8,128)(2,1)S(1)}, bf16[4,16,2048]{2,1,0:T(8,128)(2,1)S(1)}, u32[]{:S(2)}, u32[]{:S(2)}) collective-permute-start(bf16[4,16,2048]{2,1,0:T(8,128)(2,1)S(1)} %get-tuple-element.28), channel_id=1, source_target_pairs={{0,8},{1,9},{2,10},{3,11},{4,12},{5,13},{6,14},{7,15},{8,0},{9,1},... | collective-permute-start | bytes 786440 | tf_op jit(solution)/shard_map/cls1_near/ppermute | solution.py:246
  38.2 8.1 %collective-permute-start.18 = (bf16[1,16,2048]{2,1,0:T(8,128)(2,1)S(1)}, bf16[1,16,2048]{2,1,0:T(8,128)(2,1)S(1)}, u32[]{:S(2)}, u32[]{:S(2)}) collective-permute-start(bf16[1,16,2048]{2,1,0:T(8,128)(2,1)S(1)} %get-tuple-element.41), channel_id=1, source_target_pairs={{0,16},{1,17},{2,18},{3,19},{4,20},{5,21},{6,22},{7,23},{8,24},{9,... | collective-permute-start | bytes 196616 | tf_op jit(solution)/shard_map/cls2_far/ppermute | solution.py:246
  39.7 6.6 %collective-permute-start.19 = (bf16[1,16,2048]{2,1,0:T(8,128)(2,1)S(1)}, bf16[1,16,2048]{2,1,0:T(8,128)(2,1)S(1)}, u32[]{:S(2)}, u32[]{:S(2)}) collective-permute-start(bf16[1,16,2048]{2,1,0:T(8,128)(2,1)S(1)} %get-tuple-element.40), channel_id=1, source_target_pairs={{0,24},{1,25},{2,26},{3,27},{4,28},{5,29},{6,30},{7,31},{8,16},{9,... | collective-permute-start | bytes 196616 | tf_op jit(solution)/shard_map/cls3_far/ppermute | solution.py:246
  42.8 7.3 %collective-permute-start.21 = (f32[1,16,2048]{2,1,0:T(8,128)S(1)}, f32[1,16,2048]{2,1,0:T(8,128)S(1)}, u32[]{:S(2)}, u32[]{:S(2)}) collective-permute-start(f32[1,16,2048]{2,1,0:T(8,128)S(1)} %get-tuple-element.35), channel_id=1, source_target_pairs={{0,4},{1,3},{2,6},{3,1},{4,0},{5,7},{6,2},{7,5},{8,12},{9,11},{10,... | collective-permute-start | bytes 393224 | tf_op jit(solution)/shard_map/plane_own2/ppermute | solution.py:246
  43.5 6.6 %collective-permute-start.22 = (f32[1,16,2048]{2,1,0:T(8,128)S(1)}, f32[1,16,2048]{2,1,0:T(8,128)S(1)}, u32[]{:S(2)}, u32[]{:S(2)}) collective-permute-start(f32[1,16,2048]{2,1,0:T(8,128)S(1)} %get-tuple-element.36), channel_id=1, source_target_pairs={{0,2},{1,5},{2,0},{3,7},{4,6},{5,1},{6,4},{7,3},{8,10},{9,13},{10,... | collective-permute-start | bytes 393224 | tf_op jit(solution)/shard_map/plane_own1/ppermute | solution.py:246
  44.8 5.4 %collective-permute-start.20 = (bf16[1,16,2048]{2,1,0:T(8,128)(2,1)S(1)}, bf16[1,16,2048]{2,1,0:T(8,128)(2,1)S(1)}, u32[]{:S(2)}, u32[]{:S(2)}) collective-permute-start(bf16[1,16,2048]{2,1,0:T(8,128)(2,1)S(1)} %get-tuple-element.34), channel_id=1, source_target_pairs={{0,6},{1,7},{2,4},{3,5},{4,2},{5,3},{6,0},{7,1},{8,14},{9,15},{10,... | collective-permute-start | bytes 196616 | tf_op jit(solution)/shard_map/plane_own3/ppermute | solution.py:246
  50.2 1.3 %collective-permute-start.23 = (f32[2,4,2048]{2,1,0:T(4,128)S(1)}, f32[2,4,2048]{2,1,0:T(4,128)S(1)}, u32[]{:S(2)}, u32[]{:S(2)}) collective-permute-start(f32[2,4,2048]{2,1,0:T(4,128)S(1)} %get-tuple-element.38), channel_id=1, source_target_pairs={{0,1},{1,0},{2,3},{3,2},{4,5},{5,4},{6,7},{7,6},{8,9},{9,8},{10,11... | collective-permute-start | bytes 196616 | tf_op jit(solution)/shard_map/core_sums/ppermute | solution.py:246
